TPU v7x, 32 devices: a whole 2x2x4 slice. The times are simulated.
32 devices in a mesh: queue: 4 (over z), seq: 8 (over y, x, core).
Axes of the slice: x: 2, y: 2, z: 4, core: 2. Of those that a mesh axis runs over, the one named last changes fastest.
Arguments:
- latents: bfloat16 [4, 8, 128, 3072], P('queue', None, 'seq'), may hold values from -6 to 6
- queries: bfloat16 [4, 8, 128, 3072], P('queue', None, 'seq'), may hold values from -5 to 5
- keys: bfloat16 [4, 8, 128, 3072], P('queue', None, 'seq'), may hold values from -5 to 5
- values: bfloat16 [4, 8, 128, 3072], P('queue', None, 'seq'), may hold values from -6 to 6
- fresh_frames: bfloat16 [2, 128, 3072], P(None, 'seq'), may hold values from -6 to 6
- timesteps: int32 [4], replicated, may hold values from 1 to 32, as said below
- offsets: int32 [4], P('queue'), may hold values from 1 to 2
Outputs:
- attended: bfloat16 [4, 8, 128, 3072], P('queue', None, 'seq')
- advanced: bfloat16 [4, 8, 128, 3072], P('queue', None, 'seq')
Inputs may be any that keep to these rules, and one draw needn't show every extreme that they name: `timesteps`: block b has an index from 8 b + 1 to 8 b + 8; the last block has 32.
All inputs are finite; a program needn't handle non-finite values.
Results may differ from a plain program's by a relative error of at most 0.0033.
Values may be sent and summed in bfloat16 or wider, within the bound.
No kernel may reach another device: no remote copies, remote signals or barrier semaphores. Data moves between devices by JAX's collectives and lax.ppermute only.
A program may use at most 64 MiB of HBM per device.

v0:
```python
import jax
import jax.numpy as jnp
from jax import lax
from jax.sharding import PartitionSpec as P

HEAD_SIZE = 128
GROUPS = 8
HEAD_GRP = 3
MAX_SHIFT = 2


def shifted(block, axis, distance):
    devices = range(lax.axis_size(axis))
    route = [(i - distance, i) for i in devices if i - distance in devices]
    return lax.ppermute(block, axis, route)


def level(step, count):
    ratio = step.astype(jnp.float32) / count
    return 7.0 * ratio / (1.0 + 6.0 * ratio)


def attend_items(query_part, key_part, value_part):
    length = query_part.shape[0]
    block = min(512, length)
    scale = HEAD_SIZE ** (-0.5)
    results = []
    for item in range(query_part.shape[1]):
        key_head = key_part[:, item]
        value_head = value_part[:, item]

        def one_block(query_block):
            scores = (
                jnp.einsum("qd,kd->qk", query_block, key_head, preferred_element_type=jnp.float32)
                * scale
            )
            top = jnp.max(scores, axis=-1, keepdims=True)
            weights = jnp.exp(scores - top)
            total = jnp.sum(weights, axis=-1, keepdims=True)
            mixed = (
                jnp.dot(
                    weights.astype(jnp.bfloat16), value_head, preferred_element_type=jnp.float32
                )
                / total
            )
            return mixed.astype(jnp.bfloat16)

        blocks = query_part[:, item].reshape(length // block, block, HEAD_SIZE)
        results.append(lax.map(one_block, blocks).reshape(length, HEAD_SIZE))
    return jnp.stack(results, axis=1)


def shards(latents, queries, keys, values, fresh_frames, timesteps, offsets):
    frame_count = latents.shape[1]
    frame_rows = latents.shape[2]
    seq_count = lax.axis_size("seq")
    quarters = seq_count // GROUPS
    row_count = frame_count * frame_rows
    quarter_rows = row_count // quarters
    quarter = lax.axis_index("seq") // GROUPS
    queue_count = lax.axis_size("queue")
    position = lax.axis_index("queue")
    split_keys = keys.reshape(row_count, 1, GROUPS, HEAD_GRP, 1, HEAD_SIZE)
    split_values = values.reshape(row_count, 1, GROUPS, HEAD_GRP, 1, HEAD_SIZE)
    split_queries = queries.reshape(row_count, 1, GROUPS, HEAD_GRP, 1, HEAD_SIZE)
    triple = jnp.concatenate([split_queries, split_keys, split_values], axis=4)
    triple = jnp.broadcast_to(triple, (row_count, quarters, GROUPS, HEAD_GRP, 3, HEAD_SIZE))
    triple = triple.reshape(row_count, seq_count, HEAD_GRP, 3, HEAD_SIZE)
    piece = lax.all_to_all(triple, "seq", split_axis=1, concat_axis=0, tiled=True)
    items = piece.shape[2]
    query_part = piece[:, 0, :, 0].reshape(seq_count, quarter_rows, quarters, items, HEAD_SIZE)
    query_part = lax.dynamic_index_in_dim(query_part, quarter, 2, keepdims=False)
    query_part = query_part.reshape(seq_count * quarter_rows, items, HEAD_SIZE)
    outcome = attend_items(query_part, piece[:, 0, :, 1], piece[:, 0, :, 2])
    outcome = outcome.reshape(seq_count, quarter_rows, HEAD_GRP * HEAD_SIZE)
    gathered = lax.all_to_all(outcome, "seq", split_axis=0, concat_axis=2, tiled=True)
    attended = gathered.reshape(latents.shape)
    level_count = 8 * queue_count
    own_step = lax.dynamic_index_in_dim(timesteps, position, 0, keepdims=False)
    delta = 8.0 * (level(own_step - 1, level_count) - level(own_step, level_count))
    updated = (latents.astype(jnp.float32) + delta * attended.astype(jnp.float32)).astype(
        jnp.bfloat16
    )
    incoming = shifted(updated[:, :MAX_SHIFT], "queue", -1)
    incoming = jnp.where(position == queue_count - 1, fresh_frames[None], incoming)
    joined = jnp.concatenate([updated, incoming], axis=1)
    advanced = lax.dynamic_slice_in_dim(joined, offsets[0], frame_count, 1)
    return (attended, advanced)


def solution(mesh):
    in_specs = (
        P("queue", None, "seq", None),
        P("queue", None, "seq", None),
        P("queue", None, "seq", None),
        P("queue", None, "seq", None),
        P(None, "seq", None),
        P(),
        P("queue"),
    )
    out_specs = (P("queue", None, "seq", None), P("queue", None, "seq", None))
    return jax.shard_map(shards, mesh=mesh, in_specs=in_specs, out_specs=out_specs, check_vma=False)
```

profile of v0, /device:TPU:0, one launch (start us, length us, event | category | flops | bytes accessed | tf_op | source)
XLA Modules:
  0.0 85.8 jit_solution(11485993758283965425)
XLA Ops:
  0.6 2.8 %reshape.67 = bf16[128,1,8,3,1,128]{5,3,2,0,4,1:T(4,128)(2,1)S(1)} reshape(bf16[1,8,16,3072]{3,2,1,0:T(8,128)(2,1)} %param.14) | data formatting | bytes 1572864 | tf_op jit(solution)/shard_map/reshape | solution.py:65
  3.5 1.2 %reshape.68 = bf16[128,1,8,3,1,128]{5,3,2,0,4,1:T(4,128)(2,1)S(1)} reshape(bf16[1,8,16,3072]{3,2,1,0:T(8,128)(2,1)S(1)} %copy-done.1) | data formatting | bytes 1572864 | tf_op jit(solution)/shard_map/reshape | solution.py:63
  4.6 2.7 %reshape.69 = bf16[128,1,8,3,1,128]{5,3,2,0,4,1:T(4,128)(2,1)S(1)} reshape(bf16[1,8,16,3072]{3,2,1,0:T(8,128)(2,1)} %param.16) | data formatting | bytes 1572864 | tf_op jit(solution)/shard_map/reshape | solution.py:64
  7.4 2.7 %maximum_bitcast_fusion = bf16[128,8,3,3,128]{4,2,1,0,3:T(4,128)(2,1)S(1)} fusion(bf16[128,1,8,3,1,128]{5,3,2,0,4,1:T(4,128)(2,1)S(1)} %reshape.69, bf16[128,1,8,3,1,128]{5,3,2,0,4,1:T(4,128)(2,1)S(1)} %reshape.68, bf16[128,1,8,3,1,128]{5,3,2,0,4,1:T(4,128)(2,1)S(1)} %reshape.67), kind=kLoop, calls=%fused_computation.45 | loop fusion | flops 2359296 | bytes 4718592 | tf_op jit(solution)/shard_map/reshape | solution.py:68
  10.1 2.5 %copy.20 = bf16[128,8,3,3,128]{4,0,3,2,1:T(8,128)(2,1)} copy(bf16[128,8,3,3,128]{4,2,1,0,3:T(4,128)(2,1)S(1)} %maximum_bitcast_fusion) | data formatting | bytes 4718592 | tf_op jit(solution)/shard_map/reshape | solution.py:68
  12.6 5.2 %all-to-all-start = ((bf16[128,8,3,3,128]{4,0,3,2,1:T(8,128)(2,1)}), bf16[128,8,3,3,128]{4,0,3,2,1:T(8,128)(2,1)S(1)}, u32[]{:S(2)}, u32[]{:S(2)}) async-start(bf16[128,8,3,3,128]{4,0,3,2,1:T(8,128)(2,1)} %copy.20), calls=%async_computation | async-start | bytes 4718592 | tf_op jit(solution)/shard_map/all_to_all | solution.py:69
  17.8 29.5 %all-to-all-done = bf16[128,8,3,3,128]{4,0,3,2,1:T(8,128)(2,1)S(1)} async-done(((bf16[128,8,3,3,128]{4,0,3,2,1:T(8,128)(2,1)}), bf16[128,8,3,3,128]{4,0,3,2,1:T(8,128)(2,1)S(1)}, u32[]{:S(2)}, u32[]{:S(2)}) %all-to-all-start) | async-done | bytes 2359328 | tf_op jit(solution)/shard_map/all_to_all | solution.py:69
  48.0 3.3 %while.30 = (s32[]{:T(128)}, bf16[2,512,128]{2,1,0:T(8,128)(2,1)S(1)}, bf16[2,512,128]{2,1,0:T(8,128)(2,1)S(1)}, bf16[1024,128]{1,0:T(8,128)(2,1)S(1)}, bf16[1024,128]{1,0:T(8,128)(2,1)S(1)}, /*index=5*/s32[]{:T(128)}) while((s32[]{:T(128)}, bf16[2,512,128]{2,1,0:T(8,128)(2,1)S(1)}, bf16[2,512,128]{2,1,0:T(8,128)(2,1)S(1)}, ...), condition=%wide.region_3.4_spmd, body=%wide.region_0.3_spmd.sunk | while | flops 272759808 | bytes 7088205 | solution.py:49
  48.0 0.5 multiply_reduce_fusion.6
  48.5 0.5 fusion.65
  49.0 0.6 fusion.66
  49.6 0.5 multiply_reduce_fusion.6
  50.1 0.5 fusion.65
  50.7 0.6 fusion.66
  51.5 3.3 %while.31 = (s32[]{:T(128)}, bf16[2,512,128]{2,1,0:T(8,128)(2,1)S(1)}, bf16[2,512,128]{2,1,0:T(8,128)(2,1)S(1)}, bf16[1024,128]{1,0:T(8,128)(2,1)S(1)}, bf16[1024,128]{1,0:T(8,128)(2,1)S(1)}, /*index=5*/s32[]{:T(128)}) while((s32[]{:T(128)}, bf16[2,512,128]{2,1,0:T(8,128)(2,1)S(1)}, bf16[2,512,128]{2,1,0:T(8,128)(2,1)S(1)}, ...), condition=%wide.region_7.8_spmd, body=%wide.region_4.7_spmd.sunk | while | flops 272759808 | bytes 7088205 | solution.py:49
  52.0 0.5 fusion.70
  52.5 0.6 fusion.71
  53.7 0.5 fusion.70
  54.2 0.6 fusion.71
  55.0 3.3 %while.32 = (s32[]{:T(128)}, bf16[2,512,128]{2,1,0:T(8,128)(2,1)S(1)}, bf16[2,512,128]{2,1,0:T(8,128)(2,1)S(1)}, bf16[1024,128]{1,0:T(8,128)(2,1)S(1)}, bf16[1024,128]{1,0:T(8,128)(2,1)S(1)}, /*index=5*/s32[]{:T(128)}) while((s32[]{:T(128)}, bf16[2,512,128]{2,1,0:T(8,128)(2,1)S(1)}, bf16[2,512,128]{2,1,0:T(8,128)(2,1)S(1)}, ...), condition=%wide.region_11.12_spmd, body=%wide.region_8.11_spmd.sunk | while | flops 272759808 | bytes 7088205 | solution.py:49
  55.5 0.5 fusion.75
  56.0 0.6 fusion.76
  57.2 0.5 fusion.75
  57.7 0.6 fusion.76
  58.7 1.0 %copy.25 = bf16[8,128,384]{1,2,0:T(8,128)(2,1)} copy(bf16[8,128,384]{1,0,2:T(8,128)(2,1)S(1)} %bitcast.117) | data formatting | bytes 1572864 | tf_op jit(solution)/shard_map/reshape | solution.py:75
  59.7 3.7 %all-to-all-start.1 = ((bf16[8,128,384]{1,2,0:T(8,128)(2,1)}), bf16[8,128,384]{1,2,0:T(8,128)(2,1)S(1)}, u32[]{:S(2)}, u32[]{:S(2)}) async-start(bf16[8,128,384]{1,2,0:T(8,128)(2,1)} %copy.25), calls=%async_computation.1 | async-start | bytes 1572864 | tf_op jit(solution)/shard_map/all_to_all | solution.py:76
  63.4 0.6 dynamic_slice.19
  65.4 10.5 %all-to-all-done.1 = bf16[8,128,384]{1,2,0:T(8,128)(2,1)S(1)} async-done(((bf16[8,128,384]{1,2,0:T(8,128)(2,1)}), bf16[8,128,384]{1,2,0:T(8,128)(2,1)S(1)}, u32[]{:S(2)}, u32[]{:S(2)}) %all-to-all-start.1) | async-done | bytes 786464 | tf_op jit(solution)/shard_map/all_to_all | solution.py:76
  76.0 0.5 copy.26
  77.2 1.3 %collective-permute-start = (bf16[1,2,16,3072]{3,2,1,0:T(8,128)(2,1)S(1)}, bf16[1,2,16,3072]{3,2,1,0:T(8,128)(2,1)S(1)}, u32[]{:S(2)}, u32[]{:S(2)}) collective-permute-start(bf16[1,2,16,3072]{3,2,1,0:T(8,128)(2,1)S(1)} %slice.64), channel_id=1, source_target_pairs={{8,0},{16,8},{24,16},{9,1},{17,9},{25,17},{10,2},{18,10},{26,18},{... | collective-permute-start | bytes 589832 | tf_op jit(solution)/shard_map/ppermute | solution.py:15
  79.1 5.6 %collective-permute-done = bf16[1,2,16,3072]{3,2,1,0:T(8,128)(2,1)S(1)} collective-permute-done((bf16[1,2,16,3072]{3,2,1,0:T(8,128)(2,1)S(1)}, bf16[1,2,16,3072]{3,2,1,0:T(8,128)(2,1)S(1)}, u32[]{:S(2)}, u32[]{:S(2)}) %collective-permute-start) | collective-permute-done | bytes 196640 | tf_op jit(solution)/shard_map/ppermute | solution.py:15
  84.8 1.1 %fusion.39 = bf16[1,8,16,3072]{3,2,1,0:T(8,128)(2,1)} fusion(s32[]{:T(128)S(6)} %select_n.23, bf16[1,8,16,3072]{3,2,1,0:T(8,128)(2,1)S(1)} %add_convert_fusion, bf16[1,2,16,3072]{3,2,1,0:T(8,128)(2,1)S(1)} %bitcast_select_fusion), kind=kLoop, calls=%fused_computation.49 | loop fusion | flops 393216 | bytes 1769476 | tf_op jit(solution)/shard_map/concatenate | solution.py:86
  (30 shorter events, 4.2 us)
Async XLA Ops:
  0.6 2.8 %copy-start.1 = (bf16[1,8,16,3072]{3,2,1,0:T(8,128)(2,1)S(1)}, bf16[1,8,16,3072]{3,2,1,0:T(8,128)(2,1)}, u32[]{:S(2)}) copy-start(bf16[1,8,16,3072]{3,2,1,0:T(8,128)(2,1)} %param.15) | copy-start | bytes 2359300
  12.6 34.6 %all-to-all-start = ((bf16[128,8,3,3,128]{4,0,3,2,1:T(8,128)(2,1)}), bf16[128,8,3,3,128]{4,0,3,2,1:T(8,128)(2,1)S(1)}, u32[]{:S(2)}, u32[]{:S(2)}) async-start(bf16[128,8,3,3,128]{4,0,3,2,1:T(8,128)(2,1)} %copy.20), calls=%async_computation | async-start | bytes 4718592 | tf_op jit(solution)/shard_map/all_to_all | solution.py:69
  58.5 4.9 %copy-start.4 = (s32[4]{0:T(128)S(1)}, s32[4]{0:T(128)}, u32[]{:S(2)}) copy-start(s32[4]{0:T(128)} %param.18) | copy-start | bytes 52
  59.7 17.1 %copy-start.2 = (bf16[1,8,16,3072]{3,2,1,0:T(8,128)(2,1)S(1)}, bf16[1,8,16,3072]{3,2,1,0:T(8,128)(2,1)}, u32[]{:S(2)}) copy-start(bf16[1,8,16,3072]{3,2,1,0:T(8,128)(2,1)} %param.13) | copy-start | bytes 2359300
  59.7 16.2 %all-to-all-start.1 = ((bf16[8,128,384]{1,2,0:T(8,128)(2,1)}), bf16[8,128,384]{1,2,0:T(8,128)(2,1)S(1)}, u32[]{:S(2)}, u32[]{:S(2)}) async-start(bf16[8,128,384]{1,2,0:T(8,128)(2,1)} %copy.25), calls=%async_computation.1 | async-start | bytes 1572864 | tf_op jit(solution)/shard_map/all_to_all | solution.py:76
  76.5 8.2 %copy-start.3 = (bf16[2,16,3072]{2,1,0:T(8,128)(2,1)S(1)}, bf16[2,16,3072]{2,1,0:T(8,128)(2,1)}, u32[]{:S(2)}) copy-start(bf16[2,16,3072]{2,1,0:T(8,128)(2,1)} %param.17) | copy-start | bytes 589828
  76.9 9.0 %copy-start = (bf16[1,8,16,3072]{3,2,1,0:T(8,128)(2,1)}, bf16[1,8,16,3072]{3,2,1,0:T(8,128)(2,1)S(1)}, u32[]{:S(2)}) copy-start(bf16[1,8,16,3072]{3,2,1,0:T(8,128)(2,1)S(1)} %reshape.73) | copy-start | bytes 2359300
  77.2 7.6 %collective-permute-start = (bf16[1,2,16,3072]{3,2,1,0:T(8,128)(2,1)S(1)}, bf16[1,2,16,3072]{3,2,1,0:T(8,128)(2,1)S(1)}, u32[]{:S(2)}, u32[]{:S(2)}) collective-permute-start(bf16[1,2,16,3072]{3,2,1,0:T(8,128)(2,1)S(1)} %slice.64), channel_id=1, source_target_pairs={{8,0},{16,8},{24,16},{9,1},{17,9},{25,17},{10,2},{18,10},{26,18},{... | collective-permute-start | bytes 589832 | tf_op jit(solution)/shard_map/ppermute | solution.py:15
where the time goes:
time: 86.2 us; the launch traced here: 85.8 us
  waiting for transfers between devices  45.6 us (53%)
  local copies, waits for them, and re-layouts  13.1 us (15%)
  starting transfers between devices  10.1 us (12%)
  other arithmetic  7.35 us (9%)
  matrix products  6.61 us (8%)
  between operations  2.93 us (3%)
    all_to_all x1, waiting for transfers between devices, shards(): lax.all_to_all(triple, 'seq', split_axis=1, concat_axis=0, tiled=True)  29.5 us
    all_to_all x1, waiting for transfers between devices, shards(): lax.all_to_all(outcome, 'seq', split_axis=0, concat_axis=2, tiled=True)  10.5 us
    ppermute x1, waiting for transfers between devices, shifted(): return lax.ppermute(block, axis, route)  5.61 us
    all_to_all x1, starting transfers between devices, shards(): lax.all_to_all(triple, 'seq', split_axis=1, concat_axis=0, tiled=True)  5.17 us
    all_to_all x1, starting transfers between devices, shards(): lax.all_to_all(outcome, 'seq', split_axis=0, concat_axis=2, tiled=True)  3.68 us
    dot_general x6, matrix products, one_block(): jnp.dot(weights.astype(jnp.bfloat16), value_head, preferred_element_type=...  3.51 us
    reduce_sum x6, other arithmetic, one_block(): total = jnp.sum(weights, axis=-1, keepdims=True)  3.2 us
    dot_general x6, matrix products, one_block(): jnp.einsum('qd,kd->qk', query_block, key_head, preferred_element_type=jnp...  3.1 us
  transfers between devices with their start and end apart: 3, of which 3 were waited for; matrix products, arithmetic and copies ran while one was open for 1% of the time, Pallas kernels for 0%

commit v1 on v0

--- a/solution.py
+++ b/solution.py
@@ -1,12 +1,17 @@
+import functools
 import jax
 import jax.numpy as jnp
 from jax import lax
+from jax.experimental import pallas as pl
+from jax.experimental.pallas import tpu as pltpu
 from jax.sharding import PartitionSpec as P
 
 HEAD_SIZE = 128
 GROUPS = 8
 HEAD_GRP = 3
 MAX_SHIFT = 2
+LOG2E = 1.4426950408889634
+CORE, ACROSS, DOWN = 1, 2, 4
 
 
 def shifted(block, axis, distance):
@@ -15,9 +20,29 @@
     return lax.ppermute(block, axis, route)
 
 
+def swapped(block, bit):
+    return lax.ppermute(block, "seq", [(i, i ^ bit) for i in range(lax.axis_size("seq"))])
+
+
 def level(step, count):
     ratio = step.astype(jnp.float32) / count
     return 7.0 * ratio / (1.0 + 6.0 * ratio)
+
+
+def advance(latents, attended, fresh_frames, timesteps, offsets):
+    queue_count = lax.axis_size("queue")
+    position = lax.axis_index("queue")
+    frame_count = latents.shape[1]
+    level_count = 8 * queue_count
+    own_step = lax.dynamic_index_in_dim(timesteps, position, 0, keepdims=False)
+    delta = 8.0 * (level(own_step - 1, level_count) - level(own_step, level_count))
+    updated = (latents.astype(jnp.float32) + delta * attended.astype(jnp.float32)).astype(
+        jnp.bfloat16
+    )
+    incoming = shifted(updated[:, :MAX_SHIFT], "queue", -1)
+    incoming = jnp.where(position == queue_count - 1, fresh_frames[None], incoming)
+    joined = jnp.concatenate([updated, incoming], axis=1)
+    return lax.dynamic_slice_in_dim(joined, offsets[0], frame_count, 1)
 
 
 def attend_items(query_part, key_part, value_part):
@@ -50,7 +75,7 @@
     return jnp.stack(results, axis=1)
 
 
-def shards(latents, queries, keys, values, fresh_frames, timesteps, offsets):
+def grouped_shards(latents, queries, keys, values, fresh_frames, timesteps, offsets):
     frame_count = latents.shape[1]
     frame_rows = latents.shape[2]
     seq_count = lax.axis_size("seq")
@@ -58,8 +83,6 @@
     row_count = frame_count * frame_rows
     quarter_rows = row_count // quarters
     quarter = lax.axis_index("seq") // GROUPS
-    queue_count = lax.axis_size("queue")
-    position = lax.axis_index("queue")
     split_keys = keys.reshape(row_count, 1, GROUPS, HEAD_GRP, 1, HEAD_SIZE)
     split_values = values.reshape(row_count, 1, GROUPS, HEAD_GRP, 1, HEAD_SIZE)
     split_queries = queries.reshape(row_count, 1, GROUPS, HEAD_GRP, 1, HEAD_SIZE)
@@ -75,17 +98,109 @@
     outcome = outcome.reshape(seq_count, quarter_rows, HEAD_GRP * HEAD_SIZE)
     gathered = lax.all_to_all(outcome, "seq", split_axis=0, concat_axis=2, tiled=True)
     attended = gathered.reshape(latents.shape)
-    level_count = 8 * queue_count
-    own_step = lax.dynamic_index_in_dim(timesteps, position, 0, keepdims=False)
-    delta = 8.0 * (level(own_step - 1, level_count) - level(own_step, level_count))
-    updated = (latents.astype(jnp.float32) + delta * attended.astype(jnp.float32)).astype(
-        jnp.bfloat16
-    )
-    incoming = shifted(updated[:, :MAX_SHIFT], "queue", -1)
-    incoming = jnp.where(position == queue_count - 1, fresh_frames[None], incoming)
-    joined = jnp.concatenate([updated, incoming], axis=1)
-    advanced = lax.dynamic_slice_in_dim(joined, offsets[0], frame_count, 1)
-    return (attended, advanced)
+    return (attended, advance(latents, attended, fresh_frames, timesteps, offsets))
+
+
+def attend_kernel(query_ref, near_ref, far_ref, core_ref, core_far_ref, own_ref, back_ref):
+    parts = (near_ref, far_ref, core_ref, core_far_ref)
+    rows = own_ref.shape[0]
+    factor = LOG2E * HEAD_SIZE ** (-0.5)
+    for head in range(query_ref.shape[1] // HEAD_SIZE):
+        cols = slice(head * HEAD_SIZE, (head + 1) * HEAD_SIZE)
+        for out_ref, start in ((own_ref, 0), (back_ref, rows)):
+            query = query_ref[start : start + rows, cols]
+            scores = [
+                lax.dot_general(
+                    query,
+                    part[0, :, cols],
+                    (((1,), (1,)), ((), ())),
+                    preferred_element_type=jnp.float32,
+                )
+                for part in parts
+            ]
+            top = jnp.maximum(
+                jnp.maximum(scores[0], scores[1]), jnp.maximum(scores[2], scores[3])
+            )
+            top = jnp.max(top, axis=-1, keepdims=True)
+            weights = [jnp.exp2((score - top) * factor) for score in scores]
+            total = (weights[0] + weights[1]) + (weights[2] + weights[3])
+            total = jnp.sum(total, axis=-1, keepdims=True)
+            mixed = sum(
+                jnp.dot(
+                    weight.astype(jnp.bfloat16),
+                    part[1, :, cols],
+                    preferred_element_type=jnp.float32,
+                )
+                for weight, part in zip(weights, parts)
+            )
+            out_ref[:, cols] = (mixed / total).astype(jnp.bfloat16)
+
+
+def attend(query, parts):
+    rows, width = query.shape
+    keys = sum(part.shape[1] for part in parts)
+    out = jax.ShapeDtypeStruct((rows // 2, width), jnp.bfloat16)
+    vmem = pl.BlockSpec(memory_space=pltpu.VMEM)
+    return pl.pallas_call(
+        attend_kernel,
+        out_shape=(out, out),
+        in_specs=[vmem] * 5,
+        out_specs=(vmem, vmem),
+        cost_estimate=pl.CostEstimate(
+            flops=4 * rows * keys * width,
+            bytes_accessed=4 * (rows + keys) * width,
+            transcendentals=rows * keys * width // HEAD_SIZE,
+        ),
+        compiler_params=pltpu.CompilerParams(vmem_limit_bytes=32 * 1024 * 1024),
+    )(query, *parts)
+
+
+CHUNKS = (4, 2)
+
+
+def paired_shards(latents, queries, keys, values, fresh_frames, timesteps, offsets):
+    rows = latents.shape[1] * latents.shape[2]
+    width = latents.shape[3]
+    queries, keys, values = (a.reshape(rows, width) for a in (queries, keys, values))
+    place = lax.axis_index("seq")
+    jobs = []
+    for bit, other, base in ((ACROSS, DOWN, 0), (DOWN, ACROSS, width // 2)):
+        side = (place // bit) % 2
+        start = 0
+        for heads in CHUNKS:
+            size = heads * HEAD_SIZE
+            mine = base + side * (width // 4) + start
+            theirs = base + (1 - side) * (width // 4) + start
+            jobs.append((bit, other, side, size, mine, theirs))
+            start += size
+    jobs = [jobs[0], jobs[2], jobs[1], jobs[3]]
+
+    def cut(array, at, size):
+        return lax.dynamic_slice(array, (0, at), (rows, size))
+
+    arrived = []
+    for bit, other, side, size, mine, theirs in jobs:
+        send = jnp.stack([cut(a, theirs, size) for a in (keys, values, queries)])
+        arrived.append(swapped(send, bit))
+    near = []
+    far = []
+    for (bit, other, side, size, mine, theirs), got in zip(jobs, arrived):
+        own = jnp.stack([cut(a, mine, size) for a in (keys, values)])
+        near.append(jnp.concatenate([own, got[:2]], axis=1))
+        far.append(swapped(near[-1], other))
+    halves = []
+    for (bit, other, side, size, mine, theirs), got, here, there in zip(jobs, arrived, near, far):
+        query = jnp.concatenate([cut(queries, mine, size), got[2]], axis=0)
+        own, back = attend(query, (here, there, swapped(here, CORE), swapped(there, CORE)))
+        back = swapped(back, bit)
+        first = jnp.where(side == 0, own, back)
+        second = jnp.where(side == 0, back, own)
+        halves.append((first, second))
+    order = []
+    for a, b in ((0, 2), (1, 3)):
+        order += [halves[a][0], halves[b][0], halves[a][1], halves[b][1]]
+    attended = jnp.concatenate(order, axis=1).reshape(latents.shape)
+    return (attended, advance(latents, attended, fresh_frames, timesteps, offsets))
 
 
 def solution(mesh):
@@ -99,4 +214,5 @@
         P("queue"),
     )
     out_specs = (P("queue", None, "seq", None), P("queue", None, "seq", None))
+    shards = paired_shards if mesh.shape["seq"] == 8 else grouped_shards
     return jax.shard_map(shards, mesh=mesh, in_specs=in_specs, out_specs=out_specs, check_vma=False)

time: 86.2 us -> 70.5 us (0.82)
  waiting for transfers between devices: 45.6 us -> 29.9 us
  starting transfers between devices: 10.1 us -> 19.1 us
  Pallas kernels: 0 us -> 8.99 us
  matrix products: 6.61 us -> 0 us
  local copies, waits for them, and re-layouts: 13.1 us -> 7.19 us
  other arithmetic: 7.35 us -> 1.87 us
    all_to_all x2 -> x0, waiting for transfers between devices: 40 us -> none  [the longest x1 29.5 us: shards(): lax.all_to_all(triple, 'seq', split_axis=1, concat_axis=0, tiled=True)]
    ppermute x0 -> x20, waiting for transfers between devices: none -> 24.3 us  [swapped(): lax.ppermute(block, 'seq', [(i, i ^ bit) for i in range(lax.axis_size('se...]
    ppermute x0 -> x20, starting transfers between devices: none -> 17.8 us  [swapped(): lax.ppermute(block, 'seq', [(i, i ^ bit) for i in range(lax.axis_size('se...]
    reshape x6 -> x0, local copies, waits for them, and re-layouts: 10.6 us -> none  [the longest x1 2.81 us: shards(): queries.reshape(row_count, 1, GROUPS, HEAD_GRP, 1, HEAD_SIZE)]
    pallas_call x0 -> x4, Pallas kernels: none -> 8.99 us  [attend(): pl.pallas_call(attend_kernel, out_shape=(out, out), in_specs=[vmem] * 5,...]
    all_to_all x2 -> x0, starting transfers between devices: 8.85 us -> none  [the longest x1 5.17 us: shards(): lax.all_to_all(triple, 'seq', split_axis=1, concat_axis=0, tiled=True)]
    dot_general x12 -> x0, matrix products: 6.61 us -> none  [the longest x6 3.51 us: one_block(): jnp.dot(weights.astype(jnp.bfloat16), value_head, preferred_element_type=...]
    reduce_sum x6 -> x0, other arithmetic: 3.2 us -> none  [one_block(): total = jnp.sum(weights, axis=-1, keepdims=True)]
  transfers between devices with their start and end apart: 3 -> 21, of which waited for: 3 -> 7; matrix products, arithmetic and copies ran while one was open for 1% -> 7% of each run, Pallas kernels for 0% -> 13%
where the time goes in v1:
time: 70.5 us; the launch traced here: 70.1 us
  waiting for transfers between devices  29.9 us (42%)
  starting transfers between devices  19.1 us (27%)
  Pallas kernels  8.99 us (13%)
  local copies, waits for them, and re-layouts  7.19 us (10%)
  between operations  3.11 us (4%)
  other arithmetic  1.87 us (3%)
    ppermute x20, waiting for transfers between devices, swapped(): lax.ppermute(block, 'seq', [(i, i ^ bit) for i in range(lax.axis_size('se...  24.3 us
    ppermute x20, starting transfers between devices, swapped(): lax.ppermute(block, 'seq', [(i, i ^ bit) for i in range(lax.axis_size('se...  17.8 us
    pallas_call x4, Pallas kernels, attend(): pl.pallas_call(attend_kernel, out_shape=(out, out), in_specs=[vmem] * 5,...  8.99 us
    ppermute x1, waiting for transfers between devices, shifted(): return lax.ppermute(block, axis, route)  5.61 us
    slice x4, local copies, waits for them, and re-layouts, paired_shards(): near.append(jnp.concatenate([own, got[:2]], axis=1))  1.86 us
    squeeze x4, local copies, waits for them, and re-layouts, paired_shards(): query = jnp.concatenate([cut(queries, mine, size), got[2]], axis=0)  1.71 us
  transfers between devices with their start and end apart: 21, of which 7 were waited for; matrix products, arithmetic and copies ran while one was open for 7% of the time, Pallas kernels for 13%

profile of v1, /device:TPU:0, one launch (start us, length us, event | category | flops | bytes accessed | tf_op | source)
XLA Modules:
  0.0 70.1 jit_solution(12847249028575165888)
XLA Ops:
  0.7 1.0 %constant_dynamic-slice_fusion = (bf16[128,256]{1,0:T(8,128)(2,1)S(1)}, bf16[1,128,256]{2,1,0:T(8,128)(2,1)S(1)}, bf16[1,128,256]{2,1,0:T(8,128)(2,1)S(1)}, bf16[128,256]{1,0:T(8,128)(2,1)S(1)}) fusion(bf16[128,3072]{1,0:T(8,128)(2,1)} %bitcast.65, s32[]{:T(128)S(6)} %select_n.136, s32[]{:T(128)S(6)} %select_n.137, s32[]{:T(128)S(6)} %select_n.125, ...), kind=kLoop, calls=%fused_computation.49 | loop fusion | bytes 524304 | tf_op jit(solution)/shard_map/dynamic_slice | solution.py:179
  1.7 1.2 %dynamic-slice_bitcast_fusion.10 = (bf16[1,128,256]{2,1,0:T(8,128)(2,1)S(1)}, bf16[1,128,256]{2,1,0:T(8,128)(2,1)S(1)}, bf16[1,128,256]{2,1,0:T(8,128)(2,1)S(1)}...) fusion(bf16[128,3072]{1,0:T(8,128)(2,1)} %bitcast.61, ...), kind=kLoop, calls=%fused_computation.37 | loop fusion | bytes 1048592 | tf_op jit(solution)/shard_map/stack | solution.py:188
  3.0 3.0 %collective-permute-start.15 = (bf16[3,128,256]{2,1,0:T(8,128)(2,1)S(1)}, bf16[3,128,256]{2,1,0:T(8,128)(2,1)}, u32[]{:S(2)}, u32[]{:S(2)}) collective-permute-start(bf16[3,128,256]{2,1,0:T(8,128)(2,1)S(1)} %pad_maximum_fusion.9), channel_id=1, source_target_pairs={{0,4},{1,5},{2,6},{3,7},{4,0},{5,1},{6,2},{7,3},{8,12},{9,13},{10,... | collective-permute-start | bytes 589832 | tf_op jit(solution)/shard_map/ppermute | solution.py:24
  6.3 1.5 %collective-permute-start = (bf16[3,128,512]{2,1,0:T(8,128)(2,1)S(1)}, bf16[3,128,512]{2,1,0:T(8,128)(2,1)S(1)}, u32[]{:S(2)}, u32[]{:S(2)}) collective-permute-start(bf16[3,128,512]{2,1,0:T(8,128)(2,1)S(1)} %pad_maximum_fusion.2), channel_id=1, source_target_pairs={{0,2},{1,3},{2,0},{3,1},{4,6},{5,7},{6,4},{7,5},{8,10},{9,11},{10,... | collective-permute-start | bytes 1179656 | tf_op jit(solution)/shard_map/ppermute | solution.py:24
  7.9 0.6 collective-permute-start.5
  8.5 1.1 %collective-permute-start.10 = (bf16[3,128,512]{2,1,0:T(8,128)(2,1)S(1)}, bf16[3,128,512]{2,1,0:T(8,128)(2,1)S(1)}, u32[]{:S(2)}, u32[]{:S(2)}) collective-permute-start(bf16[3,128,512]{2,1,0:T(8,128)(2,1)S(1)} %pad_maximum_fusion.3), channel_id=1, source_target_pairs={{0,4},{1,5},{2,6},{3,7},{4,0},{5,1},{6,2},{7,3},{8,12},{9,13},{10,... | collective-permute-start | bytes 1179656 | tf_op jit(solution)/shard_map/ppermute | solution.py:24
  9.6 0.6 dynamic_slice.103
  11.7 0.9 %slice.43 = bf16[2,128,256]{2,1,0:T(8,128)(2,1)S(1)} slice(bf16[3,128,256]{2,1,0:T(8,128)(2,1)} %collective-permute-done.15), slice={[0:2], [0:128], [0:256]} | slice | bytes 262144 | tf_op jit(solution)/shard_map/slice | solution.py:189
  12.7 2.0 %collective-permute-start.16 = (bf16[2,256,256]{2,1,0:T(8,128)(2,1)S(1)}, bf16[2,256,256]{2,1,0:T(8,128)(2,1)S(1)}, u32[]{:S(2)}, u32[]{:S(2)}) collective-permute-start(bf16[2,256,256]{2,1,0:T(8,128)(2,1)S(1)} %pad_maximum_fusion.7.near_ref), channel_id=1, source_target_pairs={{0,2},{1,3},{2,0},{3,1},{4,6},{5,7},{6,4},{7,5},{8,10},{9,11},{10,... | collective-permute-start | bytes 786440 | tf_op jit(solution)/shard_map/ppermute | solution.py:24
  14.7 8.0 %collective-permute-done.5 = bf16[3,128,256]{2,1,0:T(8,128)(2,1)} collective-permute-done((bf16[3,128,256]{2,1,0:T(8,128)(2,1)S(1)}, bf16[3,128,256]{2,1,0:T(8,128)(2,1)}, u32[]{:S(2)}, u32[]{:S(2)}) %collective-permute-start.5) | collective-permute-done | bytes 196640 | tf_op jit(solution)/shard_map/ppermute | solution.py:24
  22.7 0.9 %slice.39 = bf16[2,128,256]{2,1,0:T(8,128)(2,1)S(1)} slice(bf16[3,128,256]{2,1,0:T(8,128)(2,1)} %collective-permute-done.5), slice={[0:2], [0:128], [0:256]} | slice | bytes 262144 | tf_op jit(solution)/shard_map/slice | solution.py:189
  23.7 1.1 %collective-permute-start.6 = (bf16[2,256,256]{2,1,0:T(8,128)(2,1)S(1)}, bf16[2,256,256]{2,1,0:T(8,128)(2,1)S(1)}, u32[]{:S(2)}, u32[]{:S(2)}) collective-permute-start(bf16[2,256,256]{2,1,0:T(8,128)(2,1)S(1)} %pad_maximum_fusion.5.near_ref), channel_id=1, source_target_pairs={{0,4},{1,5},{2,6},{3,7},{4,0},{5,1},{6,2},{7,3},{8,12},{9,13},{10,... | collective-permute-start | bytes 786440 | tf_op jit(solution)/shard_map/ppermute | solution.py:24
  24.8 1.1 %collective-permute-start.1 = (bf16[2,256,512]{2,1,0:T(8,128)(2,1)S(1)}, bf16[2,256,512]{2,1,0:T(8,128)(2,1)S(1)}, u32[]{:S(2)}, u32[]{:S(2)}) collective-permute-start(bf16[2,256,512]{2,1,0:T(8,128)(2,1)S(1)} %pad_maximum_fusion.near_ref), channel_id=1, source_target_pairs={{0,4},{1,5},{2,6},{3,7},{4,0},{5,1},{6,2},{7,3},{8,12},{9,13},{10,... | collective-permute-start | bytes 1572872 | tf_op jit(solution)/shard_map/ppermute | solution.py:24
  25.9 0.8 %slice_bitcast_fusion.3 = bf16[128,256]{1,0:T(8,128)(2,1)S(1)} fusion(bf16[3,128,256]{2,1,0:T(8,128)(2,1)} %collective-permute-done.5), kind=kLoop, calls=%fused_computation.34 | loop fusion | bytes 131072 | tf_op jit(solution)/shard_map/squeeze | solution.py:193
  26.8 1.5 %collective-permute-start.11 = (bf16[2,256,512]{2,1,0:T(8,128)(2,1)S(1)}, bf16[2,256,512]{2,1,0:T(8,128)(2,1)S(1)}, u32[]{:S(2)}, u32[]{:S(2)}) collective-permute-start(bf16[2,256,512]{2,1,0:T(8,128)(2,1)S(1)} %pad_maximum_fusion.1.near_ref), channel_id=1, source_target_pairs={{0,2},{1,3},{2,0},{3,1},{4,6},{5,7},{6,4},{7,5},{8,10},{9,11},{10,... | collective-permute-start | bytes 1572872 | tf_op jit(solution)/shard_map/ppermute | solution.py:24
  28.4 0.8 %slice_bitcast_fusion.2 = bf16[128,256]{1,0:T(8,128)(2,1)S(1)} fusion(bf16[3,128,256]{2,1,0:T(8,128)(2,1)} %collective-permute-done.15), kind=kLoop, calls=%fused_computation.33 | loop fusion | bytes 131072 | tf_op jit(solution)/shard_map/squeeze | solution.py:193
  29.2 11.1 %collective-permute-done.1.far_ref = bf16[2,256,512]{2,1,0:T(8,128)(2,1)S(1)} collective-permute-done((bf16[2,256,512]{2,1,0:T(8,128)(2,1)S(1)}, bf16[2,256,512]{2,1,0:T(8,128)(2,1)S(1)}, u32[]{:S(2)}, u32[]{:S(2)}) %collective-permute-start.1) | collective-permute-done | bytes 524320 | tf_op jit(solution)/shard_map/ppermute | solution.py:24
  40.4 0.6 collective-permute-start.12
  41.7 0.6 collective-permute-done.3.core_far_ref
  42.4 3.0 %shard_map.86 = (bf16[128,512]{1,0:T(8,128)(2,1)S(1)}, bf16[128,512]{1,0:T(8,128)(2,1)S(1)}) custom-call(bf16[256,512]{1,0:T(8,128)(2,1)S(1)} %pad_maximum_fusion.4.query_ref, bf16[2,256,512]{2,1,0:T(8,128)(2,1)S(1)} %pad_maximum_fusion.near_ref, bf16[2,256,512]{2,1,0:T(8,128)(2,1)S(1)} %collective-permute-done.1.far_ref, ...), custom_call_target="tpu_custom_call" | custom-call | flops 536870912 | bytes 2621440 | tf_op jit(solution)/shard_map/pallas_call | solution.py:144
  45.4 1.6 %collective-permute-start.4 = (bf16[128,512]{1,0:T(8,128)(2,1)S(1)}, bf16[128,512]{1,0:T(8,128)(2,1)S(1)}, u32[]{:S(2)}, u32[]{:S(2)}) collective-permute-start(bf16[128,512]{1,0:T(8,128)(2,1)S(1)} %get-tuple-element.11), channel_id=1, source_target_pairs={{0,2},{1,3},{2,0},{3,1},{4,6},{5,7},{6,4},{7,5},{8,10},{9,11},{10,... | collective-permute-start | bytes 393224 | tf_op jit(solution)/shard_map/ppermute | solution.py:24
  47.0 1.5 %shard_map.89 = (bf16[128,256]{1,0:T(8,128)(2,1)S(1)}, bf16[128,256]{1,0:T(8,128)(2,1)S(1)}) custom-call(bf16[256,256]{1,0:T(8,128)(2,1)S(1)} %pad_maximum_fusion.11.query_ref, bf16[2,256,256]{2,1,0:T(8,128)(2,1)S(1)} %pad_maximum_fusion.7.near_ref, bf16[2,256,256]{2,1,0:T(8,128)(2,1)S(1)} %collective-permute-done.16.far_ref, ...), custom_call_target="tpu_custom_call" | custom-call | flops 268435456 | bytes 1310720 | tf_op jit(solution)/shard_map/pallas_call | solution.py:144
  48.5 1.7 %collective-permute-start.19 = (bf16[128,256]{1,0:T(8,128)(2,1)S(1)}, bf16[128,256]{1,0:T(8,128)(2,1)S(1)}, u32[]{:S(2)}, u32[]{:S(2)}) collective-permute-start(bf16[128,256]{1,0:T(8,128)(2,1)S(1)} %get-tuple-element.17), channel_id=1, source_target_pairs={{0,4},{1,5},{2,6},{3,7},{4,0},{5,1},{6,2},{7,3},{8,12},{9,13},{10,... | collective-permute-start | bytes 196616 | tf_op jit(solution)/shard_map/ppermute | solution.py:24
  50.2 1.5 %shard_map.87 = (bf16[128,256]{1,0:T(8,128)(2,1)S(1)}, bf16[128,256]{1,0:T(8,128)(2,1)S(1)}) custom-call(bf16[256,256]{1,0:T(8,128)(2,1)S(1)} %pad_maximum_fusion.10.query_ref, bf16[2,256,256]{2,1,0:T(8,128)(2,1)S(1)} %pad_maximum_fusion.5.near_ref, bf16[2,256,256]{2,1,0:T(8,128)(2,1)S(1)} %collective-permute-done.6.far_ref, ...), custom_call_target="tpu_custom_call" | custom-call | flops 268435456 | bytes 1310720 | tf_op jit(solution)/shard_map/pallas_call | solution.py:144
  51.8 0.6 collective-permute-start.9
  52.4 3.0 %shard_map.88 = (bf16[128,512]{1,0:T(8,128)(2,1)S(1)}, bf16[128,512]{1,0:T(8,128)(2,1)S(1)}) custom-call(bf16[256,512]{1,0:T(8,128)(2,1)S(1)} %pad_maximum_fusion.6.query_ref, bf16[2,256,512]{2,1,0:T(8,128)(2,1)S(1)} %pad_maximum_fusion.1.near_ref, bf16[2,256,512]{2,1,0:T(8,128)(2,1)S(1)} %collective-permute-done.11.far_ref, ...), custom_call_target="tpu_custom_call" | custom-call | flops 536870912 | bytes 2621440 | tf_op jit(solution)/shard_map/pallas_call | solution.py:144
  55.3 0.5 collective-permute-start.14
  56.2 4.2 %collective-permute-done.14 = bf16[128,512]{1,0:T(8,128)(2,1)S(1)} collective-permute-done((bf16[128,512]{1,0:T(8,128)(2,1)S(1)}, bf16[128,512]{1,0:T(8,128)(2,1)S(1)}, u32[]{:S(2)}, u32[]{:S(2)}) %collective-permute-start.14) | collective-permute-done | bytes 131104 | tf_op jit(solution)/shard_map/ppermute | solution.py:24
  60.8 0.6 copy-done
  61.4 1.3 %collective-permute-start.20 = (bf16[1,2,16,3072]{3,2,1,0:T(8,128)(2,1)S(1)}, bf16[1,2,16,3072]{3,2,1,0:T(8,128)(2,1)S(1)}, u32[]{:S(2)}, u32[]{:S(2)}) collective-permute-start(bf16[1,2,16,3072]{3,2,1,0:T(8,128)(2,1)S(1)} %slice.44), channel_id=1, source_target_pairs={{8,0},{16,8},{24,16},{9,1},{17,9},{25,17},{10,2},{18,10},{26,18},{... | collective-permute-start | bytes 589832 | tf_op jit(solution)/shard_map/ppermute | solution.py:20
  63.4 5.6 %collective-permute-done.20 = bf16[1,2,16,3072]{3,2,1,0:T(8,128)(2,1)S(1)} collective-permute-done((bf16[1,2,16,3072]{3,2,1,0:T(8,128)(2,1)S(1)}, bf16[1,2,16,3072]{3,2,1,0:T(8,128)(2,1)S(1)}, u32[]{:S(2)}, u32[]{:S(2)}) %collective-permute-start.20) | collective-permute-done | bytes 196640 | tf_op jit(solution)/shard_map/ppermute | solution.py:20
  69.0 1.1 %fusion = bf16[1,8,16,3072]{3,2,1,0:T(8,128)(2,1)} fusion(s32[]{:T(128)S(6)} %select_n.144, bf16[1,8,16,3072]{3,2,1,0:T(8,128)(2,1)S(1)} %add_convert_fusion, bf16[1,2,16,3072]{3,2,1,0:T(8,128)(2,1)S(1)} %bitcast_select_fusion), kind=kLoop, calls=%fused_computation.3 | loop fusion | flops 393216 | bytes 1769476 | tf_op jit(solution)/shard_map/concatenate | solution.py:44
  (65 shorter events, 2.4 us)
Async XLA Ops:
  1.7 4.3 %copy-start.4 = (bf16[1,8,16,3072]{3,2,1,0:T(8,128)(2,1)S(1)}, bf16[1,8,16,3072]{3,2,1,0:T(8,128)(2,1)}, u32[]{:S(2)}) copy-start(bf16[1,8,16,3072]{3,2,1,0:T(8,128)(2,1)} %param.8) | copy-start | bytes 2359300
  1.7 4.4 %copy-start.3 = (bf16[1,8,16,3072]{3,2,1,0:T(8,128)(2,1)S(1)}, bf16[1,8,16,3072]{3,2,1,0:T(8,128)(2,1)}, u32[]{:S(2)}) copy-start(bf16[1,8,16,3072]{3,2,1,0:T(8,128)(2,1)} %param.9) | copy-start | bytes 2359300
  2.9 3.1 %copy-start.2 = (bf16[1,8,16,3072]{3,2,1,0:T(8,128)(2,1)S(1)}, bf16[1,8,16,3072]{3,2,1,0:T(8,128)(2,1)}, u32[]{:S(2)}) copy-start(bf16[1,8,16,3072]{3,2,1,0:T(8,128)(2,1)} %param.10) | copy-start | bytes 2359300
  3.0 8.7 %collective-permute-start.15 = (bf16[3,128,256]{2,1,0:T(8,128)(2,1)S(1)}, bf16[3,128,256]{2,1,0:T(8,128)(2,1)}, u32[]{:S(2)}, u32[]{:S(2)}) collective-permute-start(bf16[3,128,256]{2,1,0:T(8,128)(2,1)S(1)} %pad_maximum_fusion.9), channel_id=1, source_target_pairs={{0,4},{1,5},{2,6},{3,7},{4,0},{5,1},{6,2},{7,3},{8,12},{9,13},{10,... | collective-permute-start | bytes 589832 | tf_op jit(solution)/shard_map/ppermute | solution.py:24
  6.3 3.3 %copy-start.6 = (s32[4]{0:T(128)S(1)}, s32[4]{0:T(128)}, u32[]{:S(2)}) copy-start(s32[4]{0:T(128)} %param.12) | copy-start | bytes 52
  6.3 18.4 %collective-permute-start = (bf16[3,128,512]{2,1,0:T(8,128)(2,1)S(1)}, bf16[3,128,512]{2,1,0:T(8,128)(2,1)S(1)}, u32[]{:S(2)}, u32[]{:S(2)}) collective-permute-start(bf16[3,128,512]{2,1,0:T(8,128)(2,1)S(1)} %pad_maximum_fusion.2), channel_id=1, source_target_pairs={{0,2},{1,3},{2,0},{3,1},{4,6},{5,7},{6,4},{7,5},{8,10},{9,11},{10,... | collective-permute-start | bytes 1179656 | tf_op jit(solution)/shard_map/ppermute | solution.py:24
  7.9 14.9 %collective-permute-start.5 = (bf16[3,128,256]{2,1,0:T(8,128)(2,1)S(1)}, bf16[3,128,256]{2,1,0:T(8,128)(2,1)}, u32[]{:S(2)}, u32[]{:S(2)}) collective-permute-start(bf16[3,128,256]{2,1,0:T(8,128)(2,1)S(1)} %pad_maximum_fusion.8), channel_id=1, source_target_pairs={{0,2},{1,3},{2,0},{3,1},{4,6},{5,7},{6,4},{7,5},{8,10},{9,11},{10,... | collective-permute-start | bytes 589832 | tf_op jit(solution)/shard_map/ppermute | solution.py:24
  8.5 18.2 %collective-permute-start.10 = (bf16[3,128,512]{2,1,0:T(8,128)(2,1)S(1)}, bf16[3,128,512]{2,1,0:T(8,128)(2,1)S(1)}, u32[]{:S(2)}, u32[]{:S(2)}) collective-permute-start(bf16[3,128,512]{2,1,0:T(8,128)(2,1)S(1)} %pad_maximum_fusion.3), channel_id=1, source_target_pairs={{0,4},{1,5},{2,6},{3,7},{4,0},{5,1},{6,2},{7,3},{8,12},{9,13},{10,... | collective-permute-start | bytes 1179656 | tf_op jit(solution)/shard_map/ppermute | solution.py:24
  12.6 16.6 %collective-permute-start.17 = (bf16[2,256,256]{2,1,0:T(8,128)(2,1)S(1)}, bf16[2,256,256]{2,1,0:T(8,128)(2,1)S(1)}, u32[]{:S(2)}, u32[]{:S(2)}) collective-permute-start(bf16[2,256,256]{2,1,0:T(8,128)(2,1)S(1)} %pad_maximum_fusion.7.near_ref), channel_id=1, source_target_pairs={{0,1},{1,0},{2,3},{3,2},{4,5},{5,4},{6,7},{7,6},{8,9},{9,8},{10,11... | collective-permute-start | bytes 786440 | tf_op jit(solution)/shard_map/ppermute | solution.py:24
  12.7 27.7 %collective-permute-start.16 = (bf16[2,256,256]{2,1,0:T(8,128)(2,1)S(1)}, bf16[2,256,256]{2,1,0:T(8,128)(2,1)S(1)}, u32[]{:S(2)}, u32[]{:S(2)}) collective-permute-start(bf16[2,256,256]{2,1,0:T(8,128)(2,1)S(1)} %pad_maximum_fusion.7.near_ref), channel_id=1, source_target_pairs={{0,2},{1,3},{2,0},{3,1},{4,6},{5,7},{6,4},{7,5},{8,10},{9,11},{10,... | collective-permute-start | bytes 786440 | tf_op jit(solution)/shard_map/ppermute | solution.py:24
  23.7 17.3 %collective-permute-start.6 = (bf16[2,256,256]{2,1,0:T(8,128)(2,1)S(1)}, bf16[2,256,256]{2,1,0:T(8,128)(2,1)S(1)}, u32[]{:S(2)}, u32[]{:S(2)}) collective-permute-start(bf16[2,256,256]{2,1,0:T(8,128)(2,1)S(1)} %pad_maximum_fusion.5.near_ref), channel_id=1, source_target_pairs={{0,4},{1,5},{2,6},{3,7},{4,0},{5,1},{6,2},{7,3},{8,12},{9,13},{10,... | collective-permute-start | bytes 786440 | tf_op jit(solution)/shard_map/ppermute | solution.py:24
  24.8 15.6 %collective-permute-start.1 = (bf16[2,256,512]{2,1,0:T(8,128)(2,1)S(1)}, bf16[2,256,512]{2,1,0:T(8,128)(2,1)S(1)}, u32[]{:S(2)}, u32[]{:S(2)}) collective-permute-start(bf16[2,256,512]{2,1,0:T(8,128)(2,1)S(1)} %pad_maximum_fusion.near_ref), channel_id=1, source_target_pairs={{0,4},{1,5},{2,6},{3,7},{4,0},{5,1},{6,2},{7,3},{8,12},{9,13},{10,... | collective-permute-start | bytes 1572872 | tf_op jit(solution)/shard_map/ppermute | solution.py:24
  26.8 14.2 %collective-permute-start.11 = (bf16[2,256,512]{2,1,0:T(8,128)(2,1)S(1)}, bf16[2,256,512]{2,1,0:T(8,128)(2,1)S(1)}, u32[]{:S(2)}, u32[]{:S(2)}) collective-permute-start(bf16[2,256,512]{2,1,0:T(8,128)(2,1)S(1)} %pad_maximum_fusion.1.near_ref), channel_id=1, source_target_pairs={{0,2},{1,3},{2,0},{3,1},{4,6},{5,7},{6,4},{7,5},{8,10},{9,11},{10,... | collective-permute-start | bytes 1572872 | tf_op jit(solution)/shard_map/ppermute | solution.py:24
  29.2 12.3 %collective-permute-start.2 = (bf16[2,256,512]{2,1,0:T(8,128)(2,1)S(1)}, bf16[2,256,512]{2,1,0:T(8,128)(2,1)S(1)}, u32[]{:S(2)}, u32[]{:S(2)}) collective-permute-start(bf16[2,256,512]{2,1,0:T(8,128)(2,1)S(1)} %pad_maximum_fusion.near_ref), channel_id=1, source_target_pairs={{0,1},{1,0},{2,3},{3,2},{4,5},{5,4},{6,7},{7,6},{8,9},{9,8},{10,11... | collective-permute-start | bytes 1572872 | tf_op jit(solution)/shard_map/ppermute | solution.py:24
  40.3 1.9 %collective-permute-start.3 = (bf16[2,256,512]{2,1,0:T(8,128)(2,1)S(1)}, bf16[2,256,512]{2,1,0:T(8,128)(2,1)S(1)}, u32[]{:S(2)}, u32[]{:S(2)}) collective-permute-start(bf16[2,256,512]{2,1,0:T(8,128)(2,1)S(1)} %collective-permute-done.1.far_ref), channel_id=1, source_target_pairs={{0,1},{1,0},{2,3},{3,2},{4,5},{5,4},{6,7},{7,6},{8,9},{9,8},{10,11... | collective-permute-start | bytes 1572872 | tf_op jit(solution)/shard_map/ppermute | solution.py:24
  40.4 12.0 %collective-permute-start.12 = (bf16[2,256,512]{2,1,0:T(8,128)(2,1)S(1)}, bf16[2,256,512]{2,1,0:T(8,128)(2,1)S(1)}, u32[]{:S(2)}, u32[]{:S(2)}) collective-permute-start(bf16[2,256,512]{2,1,0:T(8,128)(2,1)S(1)} %pad_maximum_fusion.1.near_ref), channel_id=1, source_target_pairs={{0,1},{1,0},{2,3},{3,2},{4,5},{5,4},{6,7},{7,6},{8,9},{9,8},{10,11... | collective-permute-start | bytes 1572872 | tf_op jit(solution)/shard_map/ppermute | solution.py:24
  41.0 4.4 %collective-permute-start.18 = (bf16[2,256,256]{2,1,0:T(8,128)(2,1)S(1)}, bf16[2,256,256]{2,1,0:T(8,128)(2,1)S(1)}, u32[]{:S(2)}, u32[]{:S(2)}) collective-permute-start(bf16[2,256,256]{2,1,0:T(8,128)(2,1)S(1)} %collective-permute-done.16.far_ref), channel_id=1, source_target_pairs={{0,1},{1,0},{2,3},{3,2},{4,5},{5,4},{6,7},{7,6},{8,9},{9,8},{10,11... | collective-permute-start | bytes 786440 | tf_op jit(solution)/shard_map/ppermute | solution.py:24
  41.1 11.3 %collective-permute-start.13 = (bf16[2,256,512]{2,1,0:T(8,128)(2,1)S(1)}, bf16[2,256,512]{2,1,0:T(8,128)(2,1)S(1)}, u32[]{:S(2)}, u32[]{:S(2)}) collective-permute-start(bf16[2,256,512]{2,1,0:T(8,128)(2,1)S(1)} %collective-permute-done.11.far_ref), channel_id=1, source_target_pairs={{0,1},{1,0},{2,3},{3,2},{4,5},{5,4},{6,7},{7,6},{8,9},{9,8},{10,11... | collective-permute-start | bytes 1572872 | tf_op jit(solution)/shard_map/ppermute | solution.py:24
  41.5 7.0 %collective-permute-start.7 = (bf16[2,256,256]{2,1,0:T(8,128)(2,1)S(1)}, bf16[2,256,256]{2,1,0:T(8,128)(2,1)S(1)}, u32[]{:S(2)}, u32[]{:S(2)}) collective-permute-start(bf16[2,256,256]{2,1,0:T(8,128)(2,1)S(1)} %pad_maximum_fusion.5.near_ref), channel_id=1, source_target_pairs={{0,1},{1,0},{2,3},{3,2},{4,5},{5,4},{6,7},{7,6},{8,9},{9,8},{10,11... | collective-permute-start | bytes 786440 | tf_op jit(solution)/shard_map/ppermute | solution.py:24
  42.3 8.0 %collective-permute-start.8 = (bf16[2,256,256]{2,1,0:T(8,128)(2,1)S(1)}, bf16[2,256,256]{2,1,0:T(8,128)(2,1)S(1)}, u32[]{:S(2)}, u32[]{:S(2)}) collective-permute-start(bf16[2,256,256]{2,1,0:T(8,128)(2,1)S(1)} %collective-permute-done.6.far_ref), channel_id=1, source_target_pairs={{0,1},{1,0},{2,3},{3,2},{4,5},{5,4},{6,7},{7,6},{8,9},{9,8},{10,11... | collective-permute-start | bytes 786440 | tf_op jit(solution)/shard_map/ppermute | solution.py:24
  45.4 10.4 %collective-permute-start.4 = (bf16[128,512]{1,0:T(8,128)(2,1)S(1)}, bf16[128,512]{1,0:T(8,128)(2,1)S(1)}, u32[]{:S(2)}, u32[]{:S(2)}) collective-permute-start(bf16[128,512]{1,0:T(8,128)(2,1)S(1)} %get-tuple-element.11), channel_id=1, source_target_pairs={{0,2},{1,3},{2,0},{3,1},{4,6},{5,7},{6,4},{7,5},{8,10},{9,11},{10,... | collective-permute-start | bytes 393224 | tf_op jit(solution)/shard_map/ppermute | solution.py:24
  48.5 11.9 %collective-permute-start.19 = (bf16[128,256]{1,0:T(8,128)(2,1)S(1)}, bf16[128,256]{1,0:T(8,128)(2,1)S(1)}, u32[]{:S(2)}, u32[]{:S(2)}) collective-permute-start(bf16[128,256]{1,0:T(8,128)(2,1)S(1)} %get-tuple-element.17), channel_id=1, source_target_pairs={{0,4},{1,5},{2,6},{3,7},{4,0},{5,1},{6,2},{7,3},{8,12},{9,13},{10,... | collective-permute-start | bytes 196616 | tf_op jit(solution)/shard_map/ppermute | solution.py:24
  51.8 4.3 %collective-permute-start.9 = (bf16[128,256]{1,0:T(8,128)(2,1)S(1)}, bf16[128,256]{1,0:T(8,128)(2,1)S(1)}, u32[]{:S(2)}, u32[]{:S(2)}) collective-permute-start(bf16[128,256]{1,0:T(8,128)(2,1)S(1)} %get-tuple-element.13), channel_id=1, source_target_pairs={{0,2},{1,3},{2,0},{3,1},{4,6},{5,7},{6,4},{7,5},{8,10},{9,11},{10,... | collective-permute-start | bytes 196616 | tf_op jit(solution)/shard_map/ppermute | solution.py:24
  55.3 5.0 %collective-permute-start.14 = (bf16[128,512]{1,0:T(8,128)(2,1)S(1)}, bf16[128,512]{1,0:T(8,128)(2,1)S(1)}, u32[]{:S(2)}, u32[]{:S(2)}) collective-permute-start(bf16[128,512]{1,0:T(8,128)(2,1)S(1)} %get-tuple-element.15), channel_id=1, source_target_pairs={{0,4},{1,5},{2,6},{3,7},{4,0},{5,1},{6,2},{7,3},{8,12},{9,13},{10,... | collective-permute-start | bytes 393224 | tf_op jit(solution)/shard_map/ppermute | solution.py:24
  56.2 4.4 %copy-start.1 = (bf16[1,8,16,3072]{3,2,1,0:T(8,128)(2,1)S(1)}, bf16[1,8,16,3072]{3,2,1,0:T(8,128)(2,1)}, u32[]{:S(2)}) copy-start(bf16[1,8,16,3072]{3,2,1,0:T(8,128)(2,1)} %param.7) | copy-start | bytes 2359300
  60.5 0.9 %copy-start = (bf16[128,3072]{1,0:T(8,128)(2,1)}, bf16[128,3072]{1,0:T(8,128)(2,1)S(1)}, u32[]{:S(2)}) copy-start(bf16[128,3072]{1,0:T(8,128)(2,1)S(1)} %select_dynamic-update-slice_fusion.4) | copy-start | bytes 2359300
  60.5 8.4 %copy-start.5 = (bf16[2,16,3072]{2,1,0:T(8,128)(2,1)S(1)}, bf16[2,16,3072]{2,1,0:T(8,128)(2,1)}, u32[]{:S(2)}) copy-start(bf16[2,16,3072]{2,1,0:T(8,128)(2,1)} %param.11) | copy-start | bytes 589828
  61.4 7.6 %collective-permute-start.20 = (bf16[1,2,16,3072]{3,2,1,0:T(8,128)(2,1)S(1)}, bf16[1,2,16,3072]{3,2,1,0:T(8,128)(2,1)S(1)}, u32[]{:S(2)}, u32[]{:S(2)}) collective-permute-start(bf16[1,2,16,3072]{3,2,1,0:T(8,128)(2,1)S(1)} %slice.44), channel_id=1, source_target_pairs={{8,0},{16,8},{24,16},{9,1},{17,9},{25,17},{10,2},{18,10},{26,18},{... | collective-permute-start | bytes 589832 | tf_op jit(solution)/shard_map/ppermute | solution.py:20

commit v2 on v0

--- a/solution.py
+++ b/solution.py
@@ -1,12 +1,17 @@
+import functools
 import jax
 import jax.numpy as jnp
 from jax import lax
+from jax.experimental import pallas as pl
+from jax.experimental.pallas import tpu as pltpu
 from jax.sharding import PartitionSpec as P
 
 HEAD_SIZE = 128
 GROUPS = 8
 HEAD_GRP = 3
 MAX_SHIFT = 2
+LOG2E = 1.4426950408889634
+CORE, ACROSS, DOWN = 1, 2, 4
 
 
 def shifted(block, axis, distance):
@@ -15,9 +20,33 @@
     return lax.ppermute(block, axis, route)
 
 
+def swapped(block, bit):
+    return lax.ppermute(block, "seq", [(i, i ^ bit) for i in range(lax.axis_size("seq"))])
+
+
+def after(block, *others):
+    return lax.optimization_barrier((block, *others))[0]
+
+
 def level(step, count):
     ratio = step.astype(jnp.float32) / count
     return 7.0 * ratio / (1.0 + 6.0 * ratio)
+
+
+def advance(latents, attended, fresh_frames, timesteps, offsets):
+    queue_count = lax.axis_size("queue")
+    position = lax.axis_index("queue")
+    frame_count = latents.shape[1]
+    level_count = 8 * queue_count
+    own_step = lax.dynamic_index_in_dim(timesteps, position, 0, keepdims=False)
+    delta = 8.0 * (level(own_step - 1, level_count) - level(own_step, level_count))
+    updated = (latents.astype(jnp.float32) + delta * attended.astype(jnp.float32)).astype(
+        jnp.bfloat16
+    )
+    incoming = shifted(updated[:, :MAX_SHIFT], "queue", -1)
+    incoming = jnp.where(position == queue_count - 1, fresh_frames[None], incoming)
+    joined = jnp.concatenate([updated, incoming], axis=1)
+    return lax.dynamic_slice_in_dim(joined, offsets[0], frame_count, 1)
 
 
 def attend_items(query_part, key_part, value_part):
@@ -50,7 +79,7 @@
     return jnp.stack(results, axis=1)
 
 
-def shards(latents, queries, keys, values, fresh_frames, timesteps, offsets):
+def grouped_shards(latents, queries, keys, values, fresh_frames, timesteps, offsets):
     frame_count = latents.shape[1]
     frame_rows = latents.shape[2]
     seq_count = lax.axis_size("seq")
@@ -58,8 +87,6 @@
     row_count = frame_count * frame_rows
     quarter_rows = row_count // quarters
     quarter = lax.axis_index("seq") // GROUPS
-    queue_count = lax.axis_size("queue")
-    position = lax.axis_index("queue")
     split_keys = keys.reshape(row_count, 1, GROUPS, HEAD_GRP, 1, HEAD_SIZE)
     split_values = values.reshape(row_count, 1, GROUPS, HEAD_GRP, 1, HEAD_SIZE)
     split_queries = queries.reshape(row_count, 1, GROUPS, HEAD_GRP, 1, HEAD_SIZE)
@@ -75,17 +102,344 @@
     outcome = outcome.reshape(seq_count, quarter_rows, HEAD_GRP * HEAD_SIZE)
     gathered = lax.all_to_all(outcome, "seq", split_axis=0, concat_axis=2, tiled=True)
     attended = gathered.reshape(latents.shape)
-    level_count = 8 * queue_count
-    own_step = lax.dynamic_index_in_dim(timesteps, position, 0, keepdims=False)
-    delta = 8.0 * (level(own_step - 1, level_count) - level(own_step, level_count))
-    updated = (latents.astype(jnp.float32) + delta * attended.astype(jnp.float32)).astype(
-        jnp.bfloat16
+    return (attended, advance(latents, attended, fresh_frames, timesteps, offsets))
+
+
+CHUNKS = (4, 2)
+VMEM_LIMIT = 16 * 1024 * 1024
+PACK_LIMIT = 249 * 256 * 1024
+VMEM = pl.BlockSpec(memory_space=pltpu.VMEM)
+SMEM = pl.BlockSpec(memory_space=pltpu.SMEM)
+HBM = pl.BlockSpec(memory_space=pltpu.HBM)
+
+
+def call(kernel, out_shape, in_specs, out_specs, scratch_shapes=(), cost=(0, 0, 0), **options):
+    limit = options.pop("limit", VMEM_LIMIT)
+    return pl.pallas_call(
+        kernel,
+        out_shape=out_shape,
+        in_specs=in_specs,
+        out_specs=out_specs,
+        scratch_shapes=scratch_shapes,
+        cost_estimate=pl.CostEstimate(
+            flops=cost[0], bytes_accessed=cost[1], transcendentals=cost[2]
+        ),
+        compiler_params=pltpu.CompilerParams(vmem_limit_bytes=limit),
+        **options,
     )
-    incoming = shifted(updated[:, :MAX_SHIFT], "queue", -1)
-    incoming = jnp.where(position == queue_count - 1, fresh_frames[None], incoming)
-    joined = jnp.concatenate([updated, incoming], axis=1)
-    advanced = lax.dynamic_slice_in_dim(joined, offsets[0], frame_count, 1)
-    return (attended, advanced)
+
+
+def half_start(side, mine, width):
+    bit, _, base = side
+    index = (lax.axis_index("seq") // bit) % 2
+    index = index if mine else 1 - index
+    return base + index * (width // 4)
+
+
+def columns(start, size):
+    return pl.ds(pl.multiple_of(start, HEAD_SIZE), size)
+
+
+def step_size(timesteps_ref):
+    position, queue_count = lax.axis_index("queue"), lax.axis_size("queue")
+    step = jnp.full((1, HEAD_SIZE), timesteps_ref[position], jnp.int32)
+    delta = 8.0 * (level(step - 1, 8 * queue_count) - level(step, 8 * queue_count))
+    return delta[:, :1]
+
+
+def pack_kernel(sides, *refs):
+    arrays, outs, sems = refs[:3], refs[3:-1], refs[-1]
+    width = arrays[0].shape[1]
+    copies = []
+    for index, (side, out) in enumerate(zip(sides, outs)):
+        cols = columns(half_start(side, False, width), out.shape[2])
+        for which, array in enumerate(arrays):
+            copies.append(
+                pltpu.make_async_copy(array.at[:, cols], out.at[which], sems.at[index, which])
+            )
+    for copy in copies:
+        copy.start()
+    for copy in copies:
+        copy.wait()
+
+
+def pack(sides, arrays):
+    rows, width = arrays[0].shape
+    out = jax.ShapeDtypeStruct((3, rows, width // 4), jnp.bfloat16)
+    return call(
+        functools.partial(pack_kernel, sides),
+        (out,) * len(sides),
+        [HBM] * 3,
+        (VMEM,) * len(sides),
+        [pltpu.SemaphoreType.DMA((len(sides), 3))],
+        (0, 3 * rows * width * len(sides), 0),
+        limit=PACK_LIMIT,
+    )(*arrays)
+
+
+def join_kernel(side, keys_ref, values_ref, got_ref, whole_ref, *part_refs):
+    rows, width = keys_ref.shape
+    cols = columns(half_start(side, True, width), width // 4)
+    for which, source in enumerate((keys_ref, values_ref)):
+        for first, block in ((0, source[:, cols]), (rows, got_ref[which])):
+            whole_ref[which, first : first + rows] = block
+            start = 0
+            for part in part_refs:
+                size = part.shape[2]
+                part[which, first : first + rows] = block[:, start : start + size]
+                start += size
+
+
+def join(side, keys, values, got, sizes):
+    rows, width = got.shape[1:]
+    outs = tuple(
+        jax.ShapeDtypeStruct((2, 2 * rows, size), jnp.bfloat16) for size in (width, *sizes)
+    )
+    return call(
+        functools.partial(join_kernel, side),
+        outs,
+        [VMEM] * 3,
+        (VMEM,) * len(outs),
+        cost=(0, 24 * rows * width, 0),
+    )(keys, values, got)
+
+
+def attend_kernel(side, start, queries_ref, near_ref, got_ref, core_ref, far_ref, core_far_ref, own_ref, back_ref):
+    rows, width = queries_ref.shape
+    factor = LOG2E * HEAD_SIZE ** (-0.5)
+    heads = own_ref.shape[1] // HEAD_SIZE
+    first = half_start(side, True, width) + start
+
+    def narrow(head):
+        return slice(head * HEAD_SIZE, (head + 1) * HEAD_SIZE)
+
+    def wide(head):
+        return slice(start + head * HEAD_SIZE, start + (head + 1) * HEAD_SIZE)
+
+    def tokens(which, head):
+        return (
+            near_ref[which, :, wide(head)],
+            core_ref[which, :, wide(head)],
+            far_ref[which, :, narrow(head)],
+            core_far_ref[which, :, narrow(head)],
+        )
+
+    def score(head):
+        query = jnp.concatenate(
+            [queries_ref[:, columns(first + head * HEAD_SIZE, HEAD_SIZE)], got_ref[2, :, wide(head)]]
+        )
+        return [
+            lax.dot_general(
+                query, key, (((1,), (1,)), ((), ())), preferred_element_type=jnp.float32
+            )
+            for key in tokens(0, head)
+        ]
+
+    scores = score(0)
+    for head in range(heads):
+        following = score(head + 1) if head + 1 < heads else None
+        top = jnp.maximum(jnp.maximum(scores[0], scores[1]), jnp.maximum(scores[2], scores[3]))
+        top = jnp.max(top, axis=-1, keepdims=True)
+        weights = [jnp.exp2((part - top) * factor) for part in scores]
+        total = (weights[0] + weights[1]) + (weights[2] + weights[3])
+        total = jnp.sum(total, axis=-1, keepdims=True)
+        mixed = sum(
+            jnp.dot(weight.astype(jnp.bfloat16), value, preferred_element_type=jnp.float32)
+            for weight, value in zip(weights, tokens(1, head))
+        )
+        mixed = (mixed / total).astype(jnp.bfloat16)
+        own_ref[:, narrow(head)] = mixed[:rows]
+        back_ref[:, narrow(head)] = mixed[rows:]
+        scores = following
+
+
+def attend(side, start, queries, near, got, core, far, core_far):
+    rows = queries.shape[0]
+    keys, width = 4 * far.shape[1], far.shape[2]
+    out = jax.ShapeDtypeStruct((rows, width), jnp.bfloat16)
+    return call(
+        functools.partial(attend_kernel, side, start),
+        (out, out),
+        [VMEM] * 6,
+        (VMEM, VMEM),
+        cost=(8 * rows * keys * width, 8 * keys * width, 2 * rows * keys * width // HEAD_SIZE),
+    )(queries, near, got, core, far, core_far)
+
+
+def moved(latents, attended, delta):
+    change = delta * attended.astype(jnp.float32)
+    return (latents.astype(jnp.float32) + change).astype(jnp.bfloat16)
+
+
+def lead_kernel(places, timesteps_ref, latents_ref, *refs):
+    pieces, out_ref = refs[:-1], refs[-1]
+    rows, width = out_ref.shape[0], latents_ref.shape[1]
+    delta = step_size(timesteps_ref)
+    at = 0
+    for (side, mine, start), piece in zip(places, pieces):
+        size = piece.shape[1]
+        cols = columns(half_start(side, mine, width) + start, size)
+        out_ref[:, at : at + size] = moved(latents_ref[:rows, cols], piece[:rows], delta)
+        at += size
+
+
+def lead(places, rows, timesteps, latents, pieces):
+    size = sum(piece.shape[1] for piece in pieces)
+    return call(
+        functools.partial(lead_kernel, places),
+        jax.ShapeDtypeStruct((rows, size), jnp.bfloat16),
+        [SMEM] + [VMEM] * (1 + len(pieces)),
+        VMEM,
+        cost=(2 * rows * size, 6 * rows * size, 0),
+    )(timesteps, latents, *pieces)
+
+
+def finish_kernel(places, timesteps_ref, offset_ref, latents_ref, *refs):
+    pieces = refs[: len(places)]
+    attended_ref, advanced_ref, whole_ref, updated_ref, out_sem, move_sem = refs[len(places) :]
+    offset, delta = offset_ref[0], step_size(timesteps_ref)
+    frames, rows, width = attended_ref.shape
+    out_copies, move_copies = [], []
+    for frame in range(frames):
+        span = slice(frame * rows, (frame + 1) * rows)
+        for (side, mine, start), piece in zip(places, pieces):
+            cols = columns(half_start(side, mine, width) + start, piece.shape[1])
+            whole_ref[frame, :, cols] = piece[span]
+        out_copies.append(
+            pltpu.make_async_copy(whole_ref.at[frame], attended_ref.at[frame], out_sem.at[frame])
+        )
+        out_copies[-1].start()
+        if frame == 0:
+            continue
+        updated_ref[frame] = moved(latents_ref[span], whole_ref[frame], delta)
+        copy = pltpu.make_async_copy(
+            updated_ref.at[frame],
+            advanced_ref.at[jnp.maximum(frame - offset, 0)],
+            move_sem.at[frame],
+        )
+        if frame < MAX_SHIFT:
+            pl.when(frame >= offset)(copy.start)
+        else:
+            copy.start()
+        move_copies.append((frame, copy))
+    for copy in out_copies:
+        copy.wait()
+    for frame, copy in move_copies:
+        if frame < MAX_SHIFT:
+            pl.when(frame >= offset)(copy.wait)
+        else:
+            copy.wait()
+
+
+def finish(shape, places, timesteps, offsets, latents, pieces):
+    out = jax.ShapeDtypeStruct(shape, jnp.bfloat16)
+    return call(
+        functools.partial(finish_kernel, places),
+        (out, out),
+        [SMEM] * 2 + [VMEM] * (1 + len(pieces)),
+        (HBM, HBM),
+        [
+            pltpu.VMEM(shape, jnp.bfloat16),
+            pltpu.VMEM(shape, jnp.bfloat16),
+            pltpu.SemaphoreType.DMA((shape[0],)),
+            pltpu.SemaphoreType.DMA((shape[0],)),
+        ],
+        (2 * latents.size, 8 * latents.size, 0),
+    )(timesteps, offsets, latents, *pieces)
+
+
+def fill_kernel(groups, offset_ref, fresh_ref, *refs):
+    leads = refs[: len(groups)]
+    _, advanced_ref, coming_ref, sem = refs[len(groups) :]
+    offset = offset_ref[0]
+    frames, rows, width = advanced_ref.shape
+    newest = lax.axis_index("queue") == lax.axis_size("queue") - 1
+
+    @pl.when(newest)
+    def _():
+        coming_ref[...] = fresh_ref[...]
+
+    @pl.when(jnp.logical_not(newest))
+    def _():
+        for places, part in zip(groups, leads):
+            at = 0
+            for side, mine, start, size in places:
+                cols = columns(half_start(side, mine, width) + start, size)
+                for frame in range(MAX_SHIFT):
+                    span = slice(frame * rows, (frame + 1) * rows)
+                    coming_ref[frame, :, cols] = part[span, at : at + size]
+                at += size
+
+    copies = [
+        pltpu.make_async_copy(
+            coming_ref.at[frame],
+            advanced_ref.at[jnp.minimum(frames - offset + frame, frames - 1)],
+            sem.at[frame],
+        )
+        for frame in range(MAX_SHIFT)
+    ]
+    for frame, copy in enumerate(copies):
+        pl.when(frame < offset)(copy.start)
+    for frame, copy in enumerate(copies):
+        pl.when(frame < offset)(copy.wait)
+
+
+def fill(groups, offsets, fresh, leads, advanced):
+    return call(
+        functools.partial(fill_kernel, groups),
+        jax.ShapeDtypeStruct(advanced.shape, advanced.dtype),
+        [SMEM] + [VMEM] * (1 + len(leads)) + [HBM],
+        HBM,
+        [pltpu.VMEM(fresh.shape, jnp.bfloat16), pltpu.SemaphoreType.DMA((MAX_SHIFT,))],
+        (0, 6 * fresh.size, 0),
+        input_output_aliases={2 + len(leads): 0},
+    )(offsets, fresh, *leads, advanced)
+
+
+def paired_shards(latents, queries, keys, values, fresh_frames, timesteps, offsets):
+    shape = latents.shape[1:]
+    rows = shape[0] * shape[1]
+    first_rows = MAX_SHIFT * shape[1]
+    width = shape[2]
+    latents, queries, keys, values = (
+        a.reshape(rows, width) for a in (latents, queries, keys, values)
+    )
+    sides = ((ACROSS, DOWN, 0), (DOWN, ACROSS, width // 2))
+    sizes = [heads * HEAD_SIZE for heads in CHUNKS]
+    sends = pack(sides, (keys, values, queries))
+    arrived = [swapped(send, side[0]) for send, side in zip(sends, sides)]
+    joined = [join(side, keys, values, got, sizes) for side, got in zip(sides, arrived)]
+    across = [swapped(parts[0], CORE) for parts in joined]
+    pieces, places, groups, leads, outcome = [], [], [], [], []
+    start = 0
+    for chunk, size in enumerate(sizes):
+        part_pieces, part_places = [], []
+        for which, side in enumerate(sides):
+            far = swapped(joined[which][1 + chunk], side[1])
+            if chunk:
+                far = after(far, outcome[-len(sides)])
+            own, back = attend(
+                side,
+                start,
+                queries,
+                joined[which][0],
+                arrived[which],
+                across[which],
+                far,
+                swapped(far, CORE),
+            )
+            outcome.append(own)
+            part_pieces += [own, swapped(back, side[0])]
+            part_places += [(side, True, start), (side, False, start)]
+        head = lead(part_places, first_rows, timesteps, latents, part_pieces)
+        leads.append(shifted(head, "queue", -1))
+        groups.append([(*place, size) for place in part_places])
+        pieces += part_pieces
+        places += part_places
+        start += size
+    attended, advanced = finish(shape, places, timesteps, offsets, latents, pieces)
+    advanced = fill(groups, offsets, fresh_frames, leads, advanced)
+    return (attended[None], advanced[None])
 
 
 def solution(mesh):
@@ -99,4 +453,5 @@
         P("queue"),
     )
     out_specs = (P("queue", None, "seq", None), P("queue", None, "seq", None))
+    shards = paired_shards if mesh.shape["seq"] == 8 else grouped_shards
     return jax.shard_map(shards, mesh=mesh, in_specs=in_specs, out_specs=out_specs, check_vma=False)

time: 86.2 us -> 62.1 us (0.72)
  waiting for transfers between devices: 45.6 us -> 31.3 us
  local copies, waits for them, and re-layouts: 13.1 us -> 0.03 us
  Pallas kernels: 0 us -> 11.3 us
  starting transfers between devices: 10.1 us -> 17.9 us
  other arithmetic: 7.35 us -> 0 us
  matrix products: 6.61 us -> 0 us
  between operations: 2.93 us -> 1.43 us
    all_to_all x2 -> x0, waiting for transfers between devices: 40 us -> none  [the longest x1 29.5 us: shards(): lax.all_to_all(triple, 'seq', split_axis=1, concat_axis=0, tiled=True)]
    ppermute x0 -> x16, waiting for transfers between devices: none -> 28.9 us  [swapped(): lax.ppermute(block, 'seq', [(i, i ^ bit) for i in range(lax.axis_size('se...]
    ppermute x0 -> x16, starting transfers between devices: none -> 15.3 us  [swapped(): lax.ppermute(block, 'seq', [(i, i ^ bit) for i in range(lax.axis_size('se...]
    pallas_call x0 -> x11, Pallas kernels: none -> 11.3 us  [the longest x4 4.91 us: attend(): call(functools.partial(attend_kernel, side, start), (out, out), [VMEM] *...]
    reshape x6 -> x0, local copies, waits for them, and re-layouts: 10.6 us -> none  [the longest x1 2.81 us: shards(): queries.reshape(row_count, 1, GROUPS, HEAD_GRP, 1, HEAD_SIZE)]
    all_to_all x2 -> x0, starting transfers between devices: 8.85 us -> none  [the longest x1 5.17 us: shards(): lax.all_to_all(triple, 'seq', split_axis=1, concat_axis=0, tiled=True)]
    dot_general x12 -> x0, matrix products: 6.61 us -> none  [the longest x6 3.51 us: one_block(): jnp.dot(weights.astype(jnp.bfloat16), value_head, preferred_element_type=...]
    ppermute x1 -> x2, waiting for transfers between devices: 5.61 us -> 2.38 us  [shifted(): return lax.ppermute(block, axis, route)]
  transfers between devices with their start and end apart: 3 -> 18, of which waited for: 3 -> 8; matrix products, arithmetic and copies ran while one was open for 1% -> 0% of each run, Pallas kernels for 0% -> 13%
where the time goes in v2:
time: 62.1 us; the launch traced here: 61.9 us
  waiting for transfers between devices  31.3 us (50%)
  starting transfers between devices  17.9 us (29%)
  Pallas kernels  11.3 us (18%)
  between operations  1.43 us (2%)
    ppermute x16, waiting for transfers between devices, swapped(): lax.ppermute(block, 'seq', [(i, i ^ bit) for i in range(lax.axis_size('se...  28.9 us
    ppermute x16, starting transfers between devices, swapped(): lax.ppermute(block, 'seq', [(i, i ^ bit) for i in range(lax.axis_size('se...  15.3 us
    pallas_call x4, Pallas kernels, attend(): call(functools.partial(attend_kernel, side, start), (out, out), [VMEM] *...  4.91 us
    ppermute x2, starting transfers between devices, shifted(): return lax.ppermute(block, axis, route)  2.58 us
    pallas_call x1, Pallas kernels, pack(): call(functools.partial(pack_kernel, sides), (out,) * len(sides), [HBM] *...  2.52 us
    ppermute x2, waiting for transfers between devices, shifted(): return lax.ppermute(block, axis, route)  2.38 us
    pallas_call x1, Pallas kernels, finish(): call(functools.partial(finish_kernel, places), (out, out), [SMEM] * 2 + [...  1.81 us
  transfers between devices with their start and end apart: 18, of which 8 were waited for; matrix products, arithmetic and copies ran while one was open for 0% of the time, Pallas kernels for 13%

profile of v2, /device:TPU:0, one launch (start us, length us, event | category | flops | bytes accessed | tf_op | source)
XLA Modules:
  0.0 61.9 jit_solution(13460147322620062881)
XLA Ops:
  0.6 2.5 %shard_map.86 = (bf16[3,128,768]{2,1,0:T(8,128)(2,1)}, bf16[3,128,768]{2,1,0:T(8,128)(2,1)}) custom-call(bf16[128,3072]{1,0:T(8,128)(2,1)} %bitcast.11, bf16[128,3072]{1,0:T(8,128)(2,1)} %bitcast.14, bf16[128,3072]{1,0:T(8,128)(2,1)} %bitcast.6), custom_call_target="tpu_custom_call" | custom-call | bytes 2359296 | tf_op jit(solution)/shard_map/pallas_call | solution.py:169
  3.2 3.0 %collective-permute-start.5 = (bf16[3,128,768]{2,1,0:T(8,128)(2,1)}, bf16[3,128,768]{2,1,0:T(8,128)(2,1)S(1)}, u32[]{:S(2)}, u32[]{:S(2)}) collective-permute-start(bf16[3,128,768]{2,1,0:T(8,128)(2,1)} %get-tuple-element.27), channel_id=1, source_target_pairs={{0,4},{1,5},{2,6},{3,7},{4,0},{5,1},{6,2},{7,3},{8,12},{9,13},{10,... | collective-permute-start | bytes 1769480 | tf_op jit(solution)/shard_map/ppermute | solution.py:24
  6.2 1.5 %collective-permute-start = (bf16[3,128,768]{2,1,0:T(8,128)(2,1)}, bf16[3,128,768]{2,1,0:T(8,128)(2,1)S(1)}, u32[]{:S(2)}, u32[]{:S(2)}) collective-permute-start(bf16[3,128,768]{2,1,0:T(8,128)(2,1)} %get-tuple-element.22), channel_id=1, source_target_pairs={{0,2},{1,3},{2,0},{3,1},{4,6},{5,7},{6,4},{7,5},{8,10},{9,11},{10,... | collective-permute-start | bytes 1769480 | tf_op jit(solution)/shard_map/ppermute | solution.py:24
  7.7 12.0 %collective-permute-done.5.got_ref = bf16[3,128,768]{2,1,0:T(8,128)(2,1)S(1)} collective-permute-done((bf16[3,128,768]{2,1,0:T(8,128)(2,1)}, bf16[3,128,768]{2,1,0:T(8,128)(2,1)S(1)}, u32[]{:S(2)}, u32[]{:S(2)}) %collective-permute-start.5) | collective-permute-done | bytes 589856 | tf_op jit(solution)/shard_map/ppermute | solution.py:24
  19.8 0.1 shard_map.89
  19.9 1.8 %collective-permute-start.7 = (bf16[2,256,512]{2,1,0:T(8,128)(2,1)S(1)}, bf16[2,256,512]{2,1,0:T(8,128)(2,1)S(1)}, u32[]{:S(2)}, u32[]{:S(2)}) collective-permute-start(bf16[2,256,512]{2,1,0:T(8,128)(2,1)S(1)} %get-tuple-element.29), channel_id=1, source_target_pairs={{0,2},{1,3},{2,0},{3,1},{4,6},{5,7},{6,4},{7,5},{8,10},{9,11},{10,... | collective-permute-start | bytes 1572872 | tf_op jit(solution)/shard_map/ppermute | solution.py:24
  21.8 1.6 %collective-permute-start.2 = (bf16[2,256,512]{2,1,0:T(8,128)(2,1)S(1)}, bf16[2,256,512]{2,1,0:T(8,128)(2,1)S(1)}, u32[]{:S(2)}, u32[]{:S(2)}) collective-permute-start(bf16[2,256,512]{2,1,0:T(8,128)(2,1)S(1)} %get-tuple-element.24), channel_id=1, source_target_pairs={{0,4},{1,5},{2,6},{3,7},{4,0},{5,1},{6,2},{7,3},{8,12},{9,13},{10,... | collective-permute-start | bytes 1572872 | tf_op jit(solution)/shard_map/ppermute | solution.py:24
  23.4 0.5 collective-permute-start.1
  23.9 9.2 %collective-permute-done.7.far_ref = bf16[2,256,512]{2,1,0:T(8,128)(2,1)S(1)} collective-permute-done((bf16[2,256,512]{2,1,0:T(8,128)(2,1)S(1)}, bf16[2,256,512]{2,1,0:T(8,128)(2,1)S(1)}, u32[]{:S(2)}, u32[]{:S(2)}) %collective-permute-start.7) | collective-permute-done | bytes 524320 | tf_op jit(solution)/shard_map/ppermute | solution.py:24
  33.1 1.3 %collective-permute-done.2.far_ref = bf16[2,256,512]{2,1,0:T(8,128)(2,1)S(1)} collective-permute-done((bf16[2,256,512]{2,1,0:T(8,128)(2,1)S(1)}, bf16[2,256,512]{2,1,0:T(8,128)(2,1)S(1)}, u32[]{:S(2)}, u32[]{:S(2)}) %collective-permute-start.2) | collective-permute-done | bytes 524320 | tf_op jit(solution)/shard_map/ppermute | solution.py:24
  34.3 1.0 %collective-permute-start.13 = (bf16[2,256,256]{2,1,0:T(8,128)(2,1)S(1)}, bf16[2,256,256]{2,1,0:T(8,128)(2,1)S(1)}, u32[]{:S(2)}, u32[]{:S(2)}) collective-permute-start(bf16[2,256,256]{2,1,0:T(8,128)(2,1)S(1)} %get-tuple-element.36), channel_id=1, source_target_pairs={{0,2},{1,3},{2,0},{3,1},{4,6},{5,7},{6,4},{7,5},{8,10},{9,11},{10,... | collective-permute-start | bytes 786440 | tf_op jit(solution)/shard_map/ppermute | solution.py:24
  35.4 1.1 %collective-permute-start.10 = (bf16[2,256,256]{2,1,0:T(8,128)(2,1)S(1)}, bf16[2,256,256]{2,1,0:T(8,128)(2,1)S(1)}, u32[]{:S(2)}, u32[]{:S(2)}) collective-permute-start(bf16[2,256,256]{2,1,0:T(8,128)(2,1)S(1)} %get-tuple-element.32), channel_id=1, source_target_pairs={{0,4},{1,5},{2,6},{3,7},{4,0},{5,1},{6,2},{7,3},{8,12},{9,13},{10,... | collective-permute-start | bytes 786440 | tf_op jit(solution)/shard_map/ppermute | solution.py:24
  36.5 1.5 %shard_map.90 = (bf16[128,512]{1,0:T(8,128)(2,1)S(1)}, bf16[128,512]{1,0:T(8,128)(2,1)S(1)}) custom-call(bf16[128,3072]{1,0:T(8,128)(2,1)S(1)} %bitcast.7, bf16[2,256,768]{2,1,0:T(8,128)(2,1)S(1)} %get-tuple-element.28.near_ref, bf16[3,128,768]{2,1,0:T(8,128)(2,1)S(1)} %collective-permute-done.5.got_ref, ...), custom_call_target="tpu_custom_call" | custom-call | flops 536870912 | bytes 4194304 | tf_op jit(solution)/shard_map/pallas_call | solution.py:260
  38.0 5.0 %collective-permute-done.13.far_ref = bf16[2,256,256]{2,1,0:T(8,128)(2,1)S(1)} collective-permute-done((bf16[2,256,256]{2,1,0:T(8,128)(2,1)S(1)}, bf16[2,256,256]{2,1,0:T(8,128)(2,1)S(1)}, u32[]{:S(2)}, u32[]{:S(2)}) %collective-permute-start.13) | collective-permute-done | bytes 262176 | tf_op jit(solution)/shard_map/ppermute | solution.py:24
  43.1 1.5 %shard_map.88 = (bf16[128,512]{1,0:T(8,128)(2,1)S(1)}, bf16[128,512]{1,0:T(8,128)(2,1)S(1)}) custom-call(bf16[128,3072]{1,0:T(8,128)(2,1)S(1)} %bitcast.8, bf16[2,256,768]{2,1,0:T(8,128)(2,1)S(1)} %get-tuple-element.23.near_ref, bf16[3,128,768]{2,1,0:T(8,128)(2,1)S(1)} %collective-permute-done.got_ref, ...), custom_call_target="tpu_custom_call" | custom-call | flops 536870912 | bytes 4194304 | tf_op jit(solution)/shard_map/pallas_call | solution.py:260
  44.6 0.6 collective-permute-start.11
  45.2 1.5 %collective-permute-start.9 = (bf16[128,512]{1,0:T(8,128)(2,1)S(1)}, bf16[128,512]{1,0:T(8,128)(2,1)S(1)}, u32[]{:S(2)}, u32[]{:S(2)}) collective-permute-start(bf16[128,512]{1,0:T(8,128)(2,1)S(1)} %get-tuple-element.31), channel_id=1, source_target_pairs={{0,4},{1,5},{2,6},{3,7},{4,0},{5,1},{6,2},{7,3},{8,12},{9,13},{10,... | collective-permute-start | bytes 393224 | tf_op jit(solution)/shard_map/ppermute | solution.py:24
  46.7 0.5 collective-permute-start.4
  47.2 0.9 %shard_map.92 = (bf16[128,256]{1,0:T(8,128)(2,1)S(1)}, bf16[128,256]{1,0:T(8,128)(2,1)S(1)}) custom-call(bf16[128,3072]{1,0:T(8,128)(2,1)S(1)} %bitcast.9, bf16[2,256,768]{2,1,0:T(8,128)(2,1)S(1)} %get-tuple-element.28.near_ref, bf16[3,128,768]{2,1,0:T(8,128)(2,1)S(1)} %collective-permute-done.5.got_ref, ...), custom_call_target="tpu_custom_call" | custom-call | flops 268435456 | bytes 2097152 | tf_op jit(solution)/shard_map/pallas_call | solution.py:260
  48.2 1.0 %collective-permute-start.15 = (bf16[128,256]{1,0:T(8,128)(2,1)S(1)}, bf16[128,256]{1,0:T(8,128)(2,1)S(1)}, u32[]{:S(2)}, u32[]{:S(2)}) collective-permute-start(bf16[128,256]{1,0:T(8,128)(2,1)S(1)} %get-tuple-element.39), channel_id=1, source_target_pairs={{0,4},{1,5},{2,6},{3,7},{4,0},{5,1},{6,2},{7,3},{8,12},{9,13},{10,... | collective-permute-start | bytes 196616 | tf_op jit(solution)/shard_map/ppermute | solution.py:24
  49.2 0.9 %shard_map.91 = (bf16[128,256]{1,0:T(8,128)(2,1)S(1)}, bf16[128,256]{1,0:T(8,128)(2,1)S(1)}) custom-call(bf16[128,3072]{1,0:T(8,128)(2,1)S(1)} %bitcast.10, bf16[2,256,768]{2,1,0:T(8,128)(2,1)S(1)} %get-tuple-element.23.near_ref, bf16[3,128,768]{2,1,0:T(8,128)(2,1)S(1)} %collective-permute-done.got_ref, ...), custom_call_target="tpu_custom_call" | custom-call | flops 268435456 | bytes 2097152 | tf_op jit(solution)/shard_map/pallas_call | solution.py:260
  50.2 1.1 %collective-permute-start.12 = (bf16[128,256]{1,0:T(8,128)(2,1)S(1)}, bf16[128,256]{1,0:T(8,128)(2,1)S(1)}, u32[]{:S(2)}, u32[]{:S(2)}) collective-permute-start(bf16[128,256]{1,0:T(8,128)(2,1)S(1)} %get-tuple-element.35), channel_id=1, source_target_pairs={{0,2},{1,3},{2,0},{3,1},{4,6},{5,7},{6,4},{7,5},{8,10},{9,11},{10,... | collective-permute-start | bytes 196616 | tf_op jit(solution)/shard_map/ppermute | solution.py:24
  51.3 0.6 %collective-permute-done.4.refs_1_ = bf16[128,512]{1,0:T(8,128)(2,1)S(1)} collective-permute-done((bf16[128,512]{1,0:T(8,128)(2,1)S(1)}, bf16[128,512]{1,0:T(8,128)(2,1)S(1)}, u32[]{:S(2)}, u32[]{:S(2)}) %collective-permute-start.4) | collective-permute-done | bytes 131104 | tf_op jit(solution)/shard_map/ppermute | solution.py:24
  51.9 0.6 shard_map.94
  52.5 1.3 %collective-permute-start.16 = (bf16[32,2048]{1,0:T(8,128)(2,1)S(1)}, bf16[32,2048]{1,0:T(8,128)(2,1)S(1)}, u32[]{:S(2)}, u32[]{:S(2)}) collective-permute-start(bf16[32,2048]{1,0:T(8,128)(2,1)S(1)} %shard_map.94), channel_id=1, source_target_pairs={{8,0},{16,8},{24,16},{9,1},{17,9},{25,17},{10,2},{18,10},{26,18},{... | collective-permute-start | bytes 393224 | tf_op jit(solution)/shard_map/ppermute | solution.py:20
  53.8 0.7 %collective-permute-done.12.refs_5_.refs_1_ = bf16[128,256]{1,0:T(8,128)(2,1)S(1)} collective-permute-done((bf16[128,256]{1,0:T(8,128)(2,1)S(1)}, bf16[128,256]{1,0:T(8,128)(2,1)S(1)}, u32[]{:S(2)}, u32[]{:S(2)}) %collective-permute-start.12) | collective-permute-done | bytes 65568 | tf_op jit(solution)/shard_map/ppermute | solution.py:24
  54.5 0.6 shard_map.95
  55.1 1.3 %collective-permute-start.17 = (bf16[32,1024]{1,0:T(8,128)(2,1)S(1)}, bf16[32,1024]{1,0:T(8,128)(2,1)S(1)}, u32[]{:S(2)}, u32[]{:S(2)}) collective-permute-start(bf16[32,1024]{1,0:T(8,128)(2,1)S(1)} %shard_map.95), channel_id=1, source_target_pairs={{8,0},{16,8},{24,16},{9,1},{17,9},{25,17},{10,2},{18,10},{26,18},{... | collective-permute-start | bytes 196616 | tf_op jit(solution)/shard_map/ppermute | solution.py:20
  57.0 1.8 %shard_map.93 = (bf16[8,16,3072]{2,1,0:T(8,128)(2,1)}, bf16[8,16,3072]{2,1,0:T(8,128)(2,1)}) custom-call(s32[4]{0:T(128)S(1)} %copy-done.5, s32[1]{0:T(128)S(6)} %copy.11.offset_ref, bf16[128,3072]{1,0:T(8,128)(2,1)S(1)} %bitcast.19, bf16[128,512]{1,0:T(8,128)(2,1)S(1)} %get-tuple-element.25.refs_0_, bf16[128,512]{1,0:T(8,128)(2,1)S(1)} %collective-permute-done.4.refs_1_, ...), custom_call_target="tpu_custom_call" | custom-call | flops 786432 | bytes 3145728 | tf_op jit(solution)/shard_map/pallas_call | solution.py:336
  58.9 1.2 %collective-permute-done.16.refs_0_ = bf16[32,2048]{1,0:T(8,128)(2,1)S(1)} collective-permute-done((bf16[32,2048]{1,0:T(8,128)(2,1)S(1)}, bf16[32,2048]{1,0:T(8,128)(2,1)S(1)}, u32[]{:S(2)}, u32[]{:S(2)}) %collective-permute-start.16) | collective-permute-done | bytes 131104 | tf_op jit(solution)/shard_map/ppermute | solution.py:20
  60.1 1.2 %collective-permute-done.17.refs_1_ = bf16[32,1024]{1,0:T(8,128)(2,1)S(1)} collective-permute-done((bf16[32,1024]{1,0:T(8,128)(2,1)S(1)}, bf16[32,1024]{1,0:T(8,128)(2,1)S(1)}, u32[]{:S(2)}, u32[]{:S(2)}) %collective-permute-start.17) | collective-permute-done | bytes 65568 | tf_op jit(solution)/shard_map/ppermute | solution.py:20
  61.3 0.7 %shard_map.96 = bf16[8,16,3072]{2,1,0:T(8,128)(2,1)} custom-call(s32[1]{0:T(128)S(6)} %copy.11.offset_ref, bf16[2,16,3072]{2,1,0:T(8,128)(2,1)S(1)} %copy-done.4, bf16[32,2048]{1,0:T(8,128)(2,1)S(1)} %collective-permute-done.16.refs_0_, bf16[32,1024]{1,0:T(8,128)(2,1)S(1)} %collective-permute-done.17.refs_1_, ...), custom_call_target="tpu_custom_call", output_to_operand_aliasing={{}: (4, {})} | custom-call | bytes 589824 | tf_op jit(solution)/shard_map/pallas_call | solution.py:388
  (27 shorter events, 0.2 us)
Async XLA Ops:
  0.6 19.1 %copy-start.1 = (bf16[1,8,16,3072]{3,2,1,0:T(8,128)(2,1)S(1)}, bf16[1,8,16,3072]{3,2,1,0:T(8,128)(2,1)}, u32[]{:S(2)}) copy-start(bf16[1,8,16,3072]{3,2,1,0:T(8,128)(2,1)} %param.9) | copy-start | bytes 2359300
  0.6 19.1 %copy-start.2 = (bf16[1,8,16,3072]{3,2,1,0:T(8,128)(2,1)S(1)}, bf16[1,8,16,3072]{3,2,1,0:T(8,128)(2,1)}, u32[]{:S(2)}) copy-start(bf16[1,8,16,3072]{3,2,1,0:T(8,128)(2,1)} %param.10) | copy-start | bytes 2359300
  3.2 16.6 %collective-permute-start.5 = (bf16[3,128,768]{2,1,0:T(8,128)(2,1)}, bf16[3,128,768]{2,1,0:T(8,128)(2,1)S(1)}, u32[]{:S(2)}, u32[]{:S(2)}) collective-permute-start(bf16[3,128,768]{2,1,0:T(8,128)(2,1)} %get-tuple-element.27), channel_id=1, source_target_pairs={{0,4},{1,5},{2,6},{3,7},{4,0},{5,1},{6,2},{7,3},{8,12},{9,13},{10,... | collective-permute-start | bytes 1769480 | tf_op jit(solution)/shard_map/ppermute | solution.py:24
  6.2 15.4 %collective-permute-start = (bf16[3,128,768]{2,1,0:T(8,128)(2,1)}, bf16[3,128,768]{2,1,0:T(8,128)(2,1)S(1)}, u32[]{:S(2)}, u32[]{:S(2)}) collective-permute-start(bf16[3,128,768]{2,1,0:T(8,128)(2,1)} %get-tuple-element.22), channel_id=1, source_target_pairs={{0,2},{1,3},{2,0},{3,1},{4,6},{5,7},{6,4},{7,5},{8,10},{9,11},{10,... | collective-permute-start | bytes 1769480 | tf_op jit(solution)/shard_map/ppermute | solution.py:24
  19.9 16.6 %copy-start = (bf16[1,8,16,3072]{3,2,1,0:T(8,128)(2,1)S(1)}, bf16[1,8,16,3072]{3,2,1,0:T(8,128)(2,1)}, u32[]{:S(2)}) copy-start(bf16[1,8,16,3072]{3,2,1,0:T(8,128)(2,1)} %param.8) | copy-start | bytes 2359300
  19.9 13.2 %collective-permute-start.7 = (bf16[2,256,512]{2,1,0:T(8,128)(2,1)S(1)}, bf16[2,256,512]{2,1,0:T(8,128)(2,1)S(1)}, u32[]{:S(2)}, u32[]{:S(2)}) collective-permute-start(bf16[2,256,512]{2,1,0:T(8,128)(2,1)S(1)} %get-tuple-element.29), channel_id=1, source_target_pairs={{0,2},{1,3},{2,0},{3,1},{4,6},{5,7},{6,4},{7,5},{8,10},{9,11},{10,... | collective-permute-start | bytes 1572872 | tf_op jit(solution)/shard_map/ppermute | solution.py:24
  21.8 12.6 %collective-permute-start.2 = (bf16[2,256,512]{2,1,0:T(8,128)(2,1)S(1)}, bf16[2,256,512]{2,1,0:T(8,128)(2,1)S(1)}, u32[]{:S(2)}, u32[]{:S(2)}) collective-permute-start(bf16[2,256,512]{2,1,0:T(8,128)(2,1)S(1)} %get-tuple-element.24), channel_id=1, source_target_pairs={{0,4},{1,5},{2,6},{3,7},{4,0},{5,1},{6,2},{7,3},{8,12},{9,13},{10,... | collective-permute-start | bytes 1572872 | tf_op jit(solution)/shard_map/ppermute | solution.py:24
  23.3 12.0 %collective-permute-start.6 = (bf16[2,256,768]{2,1,0:T(8,128)(2,1)S(1)}, bf16[2,256,768]{2,1,0:T(8,128)(2,1)S(1)}, u32[]{:S(2)}, u32[]{:S(2)}) collective-permute-start(bf16[2,256,768]{2,1,0:T(8,128)(2,1)S(1)} %get-tuple-element.28.near_ref), channel_id=1, source_target_pairs={{0,1},{1,0},{2,3},{3,2},{4,5},{5,4},{6,7},{7,6},{8,9},{9,8},{10,11... | collective-permute-start | bytes 2359304 | tf_op jit(solution)/shard_map/ppermute | solution.py:24
  23.4 19.7 %collective-permute-start.1 = (bf16[2,256,768]{2,1,0:T(8,128)(2,1)S(1)}, bf16[2,256,768]{2,1,0:T(8,128)(2,1)S(1)}, u32[]{:S(2)}, u32[]{:S(2)}) collective-permute-start(bf16[2,256,768]{2,1,0:T(8,128)(2,1)S(1)} %get-tuple-element.23.near_ref), channel_id=1, source_target_pairs={{0,1},{1,0},{2,3},{3,2},{4,5},{5,4},{6,7},{7,6},{8,9},{9,8},{10,11... | collective-permute-start | bytes 2359304 | tf_op jit(solution)/shard_map/ppermute | solution.py:24
  33.1 3.4 %collective-permute-start.8 = (bf16[2,256,512]{2,1,0:T(8,128)(2,1)S(1)}, bf16[2,256,512]{2,1,0:T(8,128)(2,1)S(1)}, u32[]{:S(2)}, u32[]{:S(2)}) collective-permute-start(bf16[2,256,512]{2,1,0:T(8,128)(2,1)S(1)} %collective-permute-done.7.far_ref), channel_id=1, source_target_pairs={{0,1},{1,0},{2,3},{3,2},{4,5},{5,4},{6,7},{7,6},{8,9},{9,8},{10,11... | collective-permute-start | bytes 1572872 | tf_op jit(solution)/shard_map/ppermute | solution.py:24
  34.3 8.7 %collective-permute-start.3 = (bf16[2,256,512]{2,1,0:T(8,128)(2,1)S(1)}, bf16[2,256,512]{2,1,0:T(8,128)(2,1)S(1)}, u32[]{:S(2)}, u32[]{:S(2)}) collective-permute-start(bf16[2,256,512]{2,1,0:T(8,128)(2,1)S(1)} %collective-permute-done.2.far_ref), channel_id=1, source_target_pairs={{0,1},{1,0},{2,3},{3,2},{4,5},{5,4},{6,7},{7,6},{8,9},{9,8},{10,11... | collective-permute-start | bytes 1572872 | tf_op jit(solution)/shard_map/ppermute | solution.py:24
  34.3 8.7 %collective-permute-start.13 = (bf16[2,256,256]{2,1,0:T(8,128)(2,1)S(1)}, bf16[2,256,256]{2,1,0:T(8,128)(2,1)S(1)}, u32[]{:S(2)}, u32[]{:S(2)}) collective-permute-start(bf16[2,256,256]{2,1,0:T(8,128)(2,1)S(1)} %get-tuple-element.36), channel_id=1, source_target_pairs={{0,2},{1,3},{2,0},{3,1},{4,6},{5,7},{6,4},{7,5},{8,10},{9,11},{10,... | collective-permute-start | bytes 786440 | tf_op jit(solution)/shard_map/ppermute | solution.py:24
  35.4 9.3 %collective-permute-start.10 = (bf16[2,256,256]{2,1,0:T(8,128)(2,1)S(1)}, bf16[2,256,256]{2,1,0:T(8,128)(2,1)S(1)}, u32[]{:S(2)}, u32[]{:S(2)}) collective-permute-start(bf16[2,256,256]{2,1,0:T(8,128)(2,1)S(1)} %get-tuple-element.32), channel_id=1, source_target_pairs={{0,4},{1,5},{2,6},{3,7},{4,0},{5,1},{6,2},{7,3},{8,12},{9,13},{10,... | collective-permute-start | bytes 786440 | tf_op jit(solution)/shard_map/ppermute | solution.py:24
  43.1 4.2 %collective-permute-start.14 = (bf16[2,256,256]{2,1,0:T(8,128)(2,1)S(1)}, bf16[2,256,256]{2,1,0:T(8,128)(2,1)S(1)}, u32[]{:S(2)}, u32[]{:S(2)}) collective-permute-start(bf16[2,256,256]{2,1,0:T(8,128)(2,1)S(1)} %collective-permute-done.13.far_ref), channel_id=1, source_target_pairs={{0,1},{1,0},{2,3},{3,2},{4,5},{5,4},{6,7},{7,6},{8,9},{9,8},{10,11... | collective-permute-start | bytes 786440 | tf_op jit(solution)/shard_map/ppermute | solution.py:24
  44.6 4.6 %collective-permute-start.11 = (bf16[2,256,256]{2,1,0:T(8,128)(2,1)S(1)}, bf16[2,256,256]{2,1,0:T(8,128)(2,1)S(1)}, u32[]{:S(2)}, u32[]{:S(2)}) collective-permute-start(bf16[2,256,256]{2,1,0:T(8,128)(2,1)S(1)} %collective-permute-done.10.far_ref), channel_id=1, source_target_pairs={{0,1},{1,0},{2,3},{3,2},{4,5},{5,4},{6,7},{7,6},{8,9},{9,8},{10,11... | collective-permute-start | bytes 786440 | tf_op jit(solution)/shard_map/ppermute | solution.py:24
  45.2 6.1 %collective-permute-start.9 = (bf16[128,512]{1,0:T(8,128)(2,1)S(1)}, bf16[128,512]{1,0:T(8,128)(2,1)S(1)}, u32[]{:S(2)}, u32[]{:S(2)}) collective-permute-start(bf16[128,512]{1,0:T(8,128)(2,1)S(1)} %get-tuple-element.31), channel_id=1, source_target_pairs={{0,4},{1,5},{2,6},{3,7},{4,0},{5,1},{6,2},{7,3},{8,12},{9,13},{10,... | collective-permute-start | bytes 393224 | tf_op jit(solution)/shard_map/ppermute | solution.py:24
  46.7 5.2 %collective-permute-start.4 = (bf16[128,512]{1,0:T(8,128)(2,1)S(1)}, bf16[128,512]{1,0:T(8,128)(2,1)S(1)}, u32[]{:S(2)}, u32[]{:S(2)}) collective-permute-start(bf16[128,512]{1,0:T(8,128)(2,1)S(1)} %get-tuple-element.26), channel_id=1, source_target_pairs={{0,2},{1,3},{2,0},{3,1},{4,6},{5,7},{6,4},{7,5},{8,10},{9,11},{10,... | collective-permute-start | bytes 393224 | tf_op jit(solution)/shard_map/ppermute | solution.py:24
  48.2 3.7 %copy-start.3 = (bf16[1,8,16,3072]{3,2,1,0:T(8,128)(2,1)S(1)}, bf16[1,8,16,3072]{3,2,1,0:T(8,128)(2,1)}, u32[]{:S(2)}) copy-start(bf16[1,8,16,3072]{3,2,1,0:T(8,128)(2,1)} %param.7) | copy-start | bytes 2359300
  48.2 5.6 %collective-permute-start.15 = (bf16[128,256]{1,0:T(8,128)(2,1)S(1)}, bf16[128,256]{1,0:T(8,128)(2,1)S(1)}, u32[]{:S(2)}, u32[]{:S(2)}) collective-permute-start(bf16[128,256]{1,0:T(8,128)(2,1)S(1)} %get-tuple-element.39), channel_id=1, source_target_pairs={{0,4},{1,5},{2,6},{3,7},{4,0},{5,1},{6,2},{7,3},{8,12},{9,13},{10,... | collective-permute-start | bytes 196616 | tf_op jit(solution)/shard_map/ppermute | solution.py:24
  50.2 1.8 %copy-start.5 = (s32[4]{0:T(128)S(1)}, s32[4]{0:T(128)}, u32[]{:S(2)}) copy-start(s32[4]{0:T(128)} %timesteps_ref.5) | copy-start | bytes 52
  50.2 4.3 %collective-permute-start.12 = (bf16[128,256]{1,0:T(8,128)(2,1)S(1)}, bf16[128,256]{1,0:T(8,128)(2,1)S(1)}, u32[]{:S(2)}, u32[]{:S(2)}) collective-permute-start(bf16[128,256]{1,0:T(8,128)(2,1)S(1)} %get-tuple-element.35), channel_id=1, source_target_pairs={{0,2},{1,3},{2,0},{3,1},{4,6},{5,7},{6,4},{7,5},{8,10},{9,11},{10,... | collective-permute-start | bytes 196616 | tf_op jit(solution)/shard_map/ppermute | solution.py:24
  52.5 7.6 %collective-permute-start.16 = (bf16[32,2048]{1,0:T(8,128)(2,1)S(1)}, bf16[32,2048]{1,0:T(8,128)(2,1)S(1)}, u32[]{:S(2)}, u32[]{:S(2)}) collective-permute-start(bf16[32,2048]{1,0:T(8,128)(2,1)S(1)} %shard_map.94), channel_id=1, source_target_pairs={{8,0},{16,8},{24,16},{9,1},{17,9},{25,17},{10,2},{18,10},{26,18},{... | collective-permute-start | bytes 393224 | tf_op jit(solution)/shard_map/ppermute | solution.py:20
  55.1 6.2 %collective-permute-start.17 = (bf16[32,1024]{1,0:T(8,128)(2,1)S(1)}, bf16[32,1024]{1,0:T(8,128)(2,1)S(1)}, u32[]{:S(2)}, u32[]{:S(2)}) collective-permute-start(bf16[32,1024]{1,0:T(8,128)(2,1)S(1)} %shard_map.95), channel_id=1, source_target_pairs={{8,0},{16,8},{24,16},{9,1},{17,9},{25,17},{10,2},{18,10},{26,18},{... | collective-permute-start | bytes 196616 | tf_op jit(solution)/shard_map/ppermute | solution.py:20
  57.0 4.2 %copy-start.4 = (bf16[2,16,3072]{2,1,0:T(8,128)(2,1)S(1)}, bf16[2,16,3072]{2,1,0:T(8,128)(2,1)}, u32[]{:S(2)}) copy-start(bf16[2,16,3072]{2,1,0:T(8,128)(2,1)} %fresh_ref.1) | copy-start | bytes 589828

commit v3 on v2

--- a/solution.py
+++ b/solution.py
@@ -105,7 +105,6 @@
     return (attended, advance(latents, attended, fresh_frames, timesteps, offsets))
 
 
-CHUNKS = (4, 2)
 VMEM_LIMIT = 16 * 1024 * 1024
 PACK_LIMIT = 249 * 256 * 1024
 VMEM = pl.BlockSpec(memory_space=pltpu.VMEM)
@@ -129,15 +128,27 @@
     )
 
 
-def half_start(side, mine, width):
+def columns(side, mask, width):
     bit, _, base = side
-    index = (lax.axis_index("seq") // bit) % 2
-    index = index if mine else 1 - index
-    return base + index * (width // 4)
-
-
-def columns(start, size):
-    return pl.ds(pl.multiple_of(start, HEAD_SIZE), size)
+    index = lax.bitwise_xor(lax.axis_index("seq"), mask)
+    start = base + (index // bit) % 2 * (width // 4) + index % 2 * (width // 8)
+    return pl.ds(pl.multiple_of(start, HEAD_SIZE), width // 8)
+
+
+def half_columns(side, mask, width):
+    bit, _, base = side
+    index = lax.bitwise_xor(lax.axis_index("seq"), mask)
+    start = base + (index // bit) % 2 * (width // 4)
+    return pl.ds(pl.multiple_of(start, HEAD_SIZE), width // 4)
+
+
+def share(other, width, skip=0, size=None):
+    index = (lax.axis_index("seq") + other) % 2
+    return pl.ds(pl.multiple_of(index * (width // 2) + skip, HEAD_SIZE), size or width // 2)
+
+
+def peers(side):
+    return (CORE, side[0], side[0] | CORE)
 
 
 def step_size(timesteps_ref):
@@ -147,123 +158,196 @@
     return delta[:, :1]
 
 
-def pack_kernel(sides, *refs):
+def pack_kernel(cuts, *refs):
     arrays, outs, sems = refs[:3], refs[3:-1], refs[-1]
     width = arrays[0].shape[1]
     copies = []
-    for index, (side, out) in enumerate(zip(sides, outs)):
-        cols = columns(half_start(side, False, width), out.shape[2])
-        for which, array in enumerate(arrays):
-            copies.append(
-                pltpu.make_async_copy(array.at[:, cols], out.at[which], sems.at[index, which])
-            )
+    for index, ((cut, side, mask, _), out) in enumerate(zip(cuts, outs)):
+        for which in range(out.shape[0]):
+            source = arrays[which].at[:, cut(side, mask, width)]
+            copies.append(pltpu.make_async_copy(source, out.at[which], sems.at[index, which]))
     for copy in copies:
         copy.start()
     for copy in copies:
         copy.wait()
 
 
-def pack(sides, arrays):
+def pack(cuts, arrays, limit):
     rows, width = arrays[0].shape
-    out = jax.ShapeDtypeStruct((3, rows, width // 4), jnp.bfloat16)
-    return call(
-        functools.partial(pack_kernel, sides),
-        (out,) * len(sides),
+    outs = tuple(
+        jax.ShapeDtypeStruct(
+            (count, rows, width // (4 if cut is half_columns else 8)), jnp.bfloat16
+        )
+        for cut, _, _, count in cuts
+    )
+    return call(
+        functools.partial(pack_kernel, cuts),
+        outs,
         [HBM] * 3,
-        (VMEM,) * len(sides),
-        [pltpu.SemaphoreType.DMA((len(sides), 3))],
-        (0, 3 * rows * width * len(sides), 0),
-        limit=PACK_LIMIT,
+        (VMEM,) * len(outs),
+        [pltpu.SemaphoreType.DMA((len(outs), 3))],
+        (0, sum(4 * out.size for out in outs), 0),
+        limit=limit,
     )(*arrays)
 
 
-def join_kernel(side, keys_ref, values_ref, got_ref, whole_ref, *part_refs):
-    rows, width = keys_ref.shape
-    cols = columns(half_start(side, True, width), width // 4)
-    for which, source in enumerate((keys_ref, values_ref)):
-        for first, block in ((0, source[:, cols]), (rows, got_ref[which])):
-            whole_ref[which, first : first + rows] = block
-            start = 0
-            for part in part_refs:
-                size = part.shape[2]
-                part[which, first : first + rows] = block[:, start : start + size]
-                start += size
-
-
-def join(side, keys, values, got, sizes):
-    rows, width = got.shape[1:]
-    outs = tuple(
-        jax.ShapeDtypeStruct((2, 2 * rows, size), jnp.bfloat16) for size in (width, *sizes)
+def split_kernel(got_ref, out_ref):
+    out_ref[...] = got_ref[:, :, share(1, got_ref.shape[2])]
+
+
+def split(got):
+    count, rows, width = got.shape
+    return call(
+        split_kernel,
+        jax.ShapeDtypeStruct((count, rows, width // 2), jnp.bfloat16),
+        [VMEM],
+        VMEM,
+        cost=(0, 2 * got.size, 0),
+    )(got)
+
+
+def join_kernel(got_ref, core_ref, out_ref):
+    rows = got_ref.shape[1]
+    for which in range(2):
+        out_ref[which, :rows] = got_ref[which, :, share(0, got_ref.shape[2])]
+        out_ref[which, rows:] = core_ref[which]
+
+
+def join(got, core):
+    rows, size = core.shape[1:]
+    return call(
+        join_kernel,
+        jax.ShapeDtypeStruct((2, 2 * rows, size), jnp.bfloat16),
+        [VMEM] * 2,
+        VMEM,
+        cost=(0, 16 * rows * size, 0),
+    )(got, core)
+
+
+def weigh(scores, values, before=None):
+    factor = LOG2E * HEAD_SIZE ** (-0.5)
+    shape = (scores[0].shape[0], HEAD_SIZE)
+    top = jnp.max(functools.reduce(jnp.maximum, scores), axis=-1, keepdims=True)
+    top = jnp.broadcast_to(top, shape)
+    if before is not None:
+        top = jnp.maximum(top, before[1])
+    tops = jnp.concatenate([top] * (scores[0].shape[1] // HEAD_SIZE), axis=1)
+    weights = [jnp.exp2((part - tops) * factor) for part in scores]
+    total = jnp.sum(functools.reduce(jnp.add, weights), axis=-1, keepdims=True)
+    total = jnp.broadcast_to(total, shape)
+    mixed = sum(
+        jnp.dot(weight.astype(jnp.bfloat16), value, preferred_element_type=jnp.float32)
+        for weight, value in zip(weights, values)
     )
-    return call(
-        functools.partial(join_kernel, side),
-        outs,
-        [VMEM] * 3,
-        (VMEM,) * len(outs),
-        cost=(0, 24 * rows * width, 0),
-    )(keys, values, got)
-
-
-def attend_kernel(side, start, queries_ref, near_ref, got_ref, core_ref, far_ref, core_far_ref, own_ref, back_ref):
+    if before is not None:
+        keep = jnp.exp2((before[1] - top) * factor)
+        mixed = mixed + keep * before[0]
+        total = total + keep * before[2]
+    return mixed, top, total
+
+
+def dots(query, keys):
+    return [
+        lax.dot_general(query, key, (((1,), (1,)), ((), ())), preferred_element_type=jnp.float32)
+        for key in keys
+    ]
+
+
+def attend_kernel(
+    side,
+    keys_ref,
+    values_ref,
+    queries_ref,
+    core_ref,
+    got_ref,
+    got_core_ref,
+    far_ref,
+    far_core_ref,
+    *outs,
+):
     rows, width = queries_ref.shape
-    factor = LOG2E * HEAD_SIZE ** (-0.5)
-    heads = own_ref.shape[1] // HEAD_SIZE
-    first = half_start(side, True, width) + start
-
-    def narrow(head):
-        return slice(head * HEAD_SIZE, (head + 1) * HEAD_SIZE)
-
-    def wide(head):
-        return slice(start + head * HEAD_SIZE, start + (head + 1) * HEAD_SIZE)
+    wholes = (keys_ref, values_ref, queries_ref)
+    first = columns(side, 0, width).start
+    tasks = [(head, pair) for head in range(core_ref.shape[2] // HEAD_SIZE) for pair in range(2)]
 
     def tokens(which, head):
-        return (
-            near_ref[which, :, wide(head)],
-            core_ref[which, :, wide(head)],
-            far_ref[which, :, narrow(head)],
-            core_far_ref[which, :, narrow(head)],
-        )
-
-    def score(head):
-        query = jnp.concatenate(
-            [queries_ref[:, columns(first + head * HEAD_SIZE, HEAD_SIZE)], got_ref[2, :, wide(head)]]
-        )
-        return [
-            lax.dot_general(
-                query, key, (((1,), (1,)), ((), ())), preferred_element_type=jnp.float32
-            )
-            for key in tokens(0, head)
+        start = head * HEAD_SIZE
+        cols = slice(start, start + HEAD_SIZE)
+        mine = pl.ds(pl.multiple_of(first + start, HEAD_SIZE), HEAD_SIZE)
+        ours = share(0, got_ref.shape[2], start, HEAD_SIZE)
+        parts = [
+            (wholes[which][:, mine], core_ref[which, :, cols]),
+            (got_ref[which, :, ours], got_core_ref[which, :, cols]),
         ]
-
-    scores = score(0)
-    for head in range(heads):
-        following = score(head + 1) if head + 1 < heads else None
-        top = jnp.maximum(jnp.maximum(scores[0], scores[1]), jnp.maximum(scores[2], scores[3]))
-        top = jnp.max(top, axis=-1, keepdims=True)
-        weights = [jnp.exp2((part - top) * factor) for part in scores]
-        total = (weights[0] + weights[1]) + (weights[2] + weights[3])
-        total = jnp.sum(total, axis=-1, keepdims=True)
-        mixed = sum(
-            jnp.dot(weight.astype(jnp.bfloat16), value, preferred_element_type=jnp.float32)
-            for weight, value in zip(weights, tokens(1, head))
-        )
+        if which < 2:
+            parts.append((far_ref[which, :, ours], far_core_ref[which, :, cols]))
+        return [jnp.concatenate(part) for part in parts]
+
+    def score(head, pair):
+        return dots(tokens(2, head)[pair], tokens(0, head))
+
+    scores = score(*tasks[0])
+    for index, (head, pair) in enumerate(tasks):
+        following = score(*tasks[index + 1]) if index + 1 < len(tasks) else None
+        cols = slice(head * HEAD_SIZE, (head + 1) * HEAD_SIZE)
+        for out, value in zip(outs, weigh(scores, tokens(1, head))):
+            out[2 * rows * pair : 2 * rows * (pair + 1), cols] = value
+        scores = following
+
+
+def attend(side, *arrays):
+    rows, width = arrays[0].shape
+    size = width // 8
+    out = jax.ShapeDtypeStruct((4 * rows, size), jnp.float32)
+    return call(
+        functools.partial(attend_kernel, side),
+        (out,) * 3,
+        [VMEM] * 8,
+        (VMEM,) * 3,
+        cost=(96 * rows * rows * size, 64 * rows * size, 24 * rows * rows * size // HEAD_SIZE),
+    )(*arrays)
+
+
+def complete_kernel(side, queries_ref, core_ref, got_ref, got_core_ref, far_got_ref, *refs):
+    old, outs = refs[:3], refs[3:]
+    rows, width = queries_ref.shape
+    first = columns(side, 0, width).start
+    tasks = [(head, pair) for head in range(core_ref.shape[2] // HEAD_SIZE) for pair in range(2)]
+
+    def score(head, pair):
+        start = head * HEAD_SIZE
+        cols = slice(start, start + HEAD_SIZE)
+        if pair == 0:
+            mine = pl.ds(pl.multiple_of(first + start, HEAD_SIZE), HEAD_SIZE)
+            query = (queries_ref[:, mine], core_ref[2, :, cols])
+        else:
+            ours = share(0, got_ref.shape[2], start, HEAD_SIZE)
+            query = (got_ref[2, :, ours], got_core_ref[2, :, cols])
+        return dots(jnp.concatenate(query), [far_got_ref[0, :, cols]])
+
+    scores = score(*tasks[0])
+    for index, (head, pair) in enumerate(tasks):
+        following = score(*tasks[index + 1]) if index + 1 < len(tasks) else None
+        cols = slice(head * HEAD_SIZE, (head + 1) * HEAD_SIZE)
+        before = [ref[2 * rows * pair : 2 * rows * (pair + 1), cols] for ref in old]
+        mixed, _, total = weigh(scores, [far_got_ref[1, :, cols]], before)
         mixed = (mixed / total).astype(jnp.bfloat16)
-        own_ref[:, narrow(head)] = mixed[:rows]
-        back_ref[:, narrow(head)] = mixed[rows:]
+        outs[2 * pair][:, cols] = mixed[:rows]
+        outs[2 * pair + 1][:, cols] = mixed[rows:]
         scores = following
 
 
-def attend(side, start, queries, near, got, core, far, core_far):
-    rows = queries.shape[0]
-    keys, width = 4 * far.shape[1], far.shape[2]
-    out = jax.ShapeDtypeStruct((rows, width), jnp.bfloat16)
-    return call(
-        functools.partial(attend_kernel, side, start),
-        (out, out),
-        [VMEM] * 6,
-        (VMEM, VMEM),
-        cost=(8 * rows * keys * width, 8 * keys * width, 2 * rows * keys * width // HEAD_SIZE),
-    )(queries, near, got, core, far, core_far)
+def complete(side, queries, core, got, far_core, far_got, old):
+    rows, width = queries.shape
+    size = width // 8
+    out = jax.ShapeDtypeStruct((rows, size), jnp.bfloat16)
+    return call(
+        functools.partial(complete_kernel, side),
+        (out,) * 4,
+        [VMEM] * 8,
+        (VMEM,) * 4,
+        cost=(32 * rows * rows * size, 64 * rows * size, 8 * rows * rows * size // HEAD_SIZE),
+    )(queries, core, got, far_core, far_got, *old)
 
 
 def moved(latents, attended, delta):
@@ -276,9 +360,9 @@
     rows, width = out_ref.shape[0], latents_ref.shape[1]
     delta = step_size(timesteps_ref)
     at = 0
-    for (side, mine, start), piece in zip(places, pieces):
+    for place, piece in zip(places, pieces):
         size = piece.shape[1]
-        cols = columns(half_start(side, mine, width) + start, size)
+        cols = columns(*place, width)
         out_ref[:, at : at + size] = moved(latents_ref[:rows, cols], piece[:rows], delta)
         at += size
 
@@ -302,8 +386,8 @@
     out_copies, move_copies = [], []
     for frame in range(frames):
         span = slice(frame * rows, (frame + 1) * rows)
-        for (side, mine, start), piece in zip(places, pieces):
-            cols = columns(half_start(side, mine, width) + start, piece.shape[1])
+        for place, piece in zip(places, pieces):
+            cols = columns(*place, width)
             whole_ref[frame, :, cols] = piece[span]
         out_copies.append(
             pltpu.make_async_copy(whole_ref.at[frame], attended_ref.at[frame], out_sem.at[frame])
@@ -363,8 +447,9 @@
     def _():
         for places, part in zip(groups, leads):
             at = 0
-            for side, mine, start, size in places:
-                cols = columns(half_start(side, mine, width) + start, size)
+            size = part.shape[1] // len(places)
+            for place in places:
+                cols = columns(*place, width)
                 for frame in range(MAX_SHIFT):
                     span = slice(frame * rows, (frame + 1) * rows)
                     coming_ref[frame, :, cols] = part[span, at : at + size]
@@ -405,38 +490,38 @@
         a.reshape(rows, width) for a in (latents, queries, keys, values)
     )
     sides = ((ACROSS, DOWN, 0), (DOWN, ACROSS, width // 2))
-    sizes = [heads * HEAD_SIZE for heads in CHUNKS]
-    sends = pack(sides, (keys, values, queries))
-    arrived = [swapped(send, side[0]) for send, side in zip(sends, sides)]
-    joined = [join(side, keys, values, got, sizes) for side, got in zip(sides, arrived)]
-    across = [swapped(parts[0], CORE) for parts in joined]
-    pieces, places, groups, leads, outcome = [], [], [], [], []
-    start = 0
-    for chunk, size in enumerate(sizes):
-        part_pieces, part_places = [], []
-        for which, side in enumerate(sides):
-            far = swapped(joined[which][1 + chunk], side[1])
-            if chunk:
-                far = after(far, outcome[-len(sides)])
-            own, back = attend(
-                side,
-                start,
-                queries,
-                joined[which][0],
-                arrived[which],
-                across[which],
-                far,
-                swapped(far, CORE),
-            )
-            outcome.append(own)
-            part_pieces += [own, swapped(back, side[0])]
-            part_places += [(side, True, start), (side, False, start)]
-        head = lead(part_places, first_rows, timesteps, latents, part_pieces)
+    arrays = (keys, values, queries)
+    sends = pack([(half_columns, side, side[0], 3) for side in sides], arrays, PACK_LIMIT)
+    owns = pack([(half_columns, side, 0, 2) for side in sides], arrays, VMEM_LIMIT)
+    cores = pack([(columns, side, CORE, 3) for side in sides], arrays, VMEM_LIMIT)
+    gots = [swapped(send, side[0]) for side, send in zip(sides, sends)]
+    fars = [swapped(own, side[1]) for side, own in zip(sides, owns)]
+    cores = [swapped(core, CORE) for core in cores]
+    far_cores = [swapped(split(far), CORE) for far in fars]
+    got_cores = [swapped(split(got), CORE) for got in gots]
+    far_gots = [
+        swapped(join(got, core), side[1]) for side, got, core in zip(sides, gots, got_cores)
+    ]
+    received = list(zip(cores, gots, got_cores, fars, far_cores))
+    states = [attend(side, *arrays, *parts) for side, parts in zip(sides, received)]
+    far_gots = [after(far, states[1 - index][0]) for index, far in enumerate(far_gots)]
+    pieces, places, groups, leads = [], [], [], []
+    for index, side in enumerate(sides):
+        own, *backs = complete(
+            side,
+            queries,
+            cores[index],
+            gots[index],
+            got_cores[index],
+            far_gots[index],
+            states[index],
+        )
+        groups.append([(side, mask) for mask in (0, *peers(side))])
+        parts = [own] + [swapped(back, mask) for back, mask in zip(backs, peers(side))]
+        head = lead(groups[-1], first_rows, timesteps, latents, parts)
         leads.append(shifted(head, "queue", -1))
-        groups.append([(*place, size) for place in part_places])
-        pieces += part_pieces
-        places += part_places
-        start += size
+        pieces += parts
+        places += groups[-1]
     attended, advanced = finish(shape, places, timesteps, offsets, latents, pieces)
     advanced = fill(groups, offsets, fresh_frames, leads, advanced)
     return (attended[None], advanced[None])

time: 62.1 us -> 57.9 us (0.932)
  waiting for transfers between devices: 31.3 us -> 27.6 us
  starting transfers between devices: 17.9 us -> 14.6 us
  local copies, waits for them, and re-layouts: 0.03 us -> 1.81 us
  Pallas kernels: 11.3 us -> 12.2 us
    ppermute x16 -> x18, waiting for transfers between devices: 28.9 us -> 23.9 us  [swapped(): lax.ppermute(block, 'seq', [(i, i ^ bit) for i in range(lax.axis_size('se...]
    ppermute x16 -> x18, starting transfers between devices: 15.3 us -> 12 us  [swapped(): lax.ppermute(block, 'seq', [(i, i ^ bit) for i in range(lax.axis_size('se...]
    unnamed x12 -> x14, local copies, waits for them, and re-layouts: 0.03 us -> 1.81 us
    ppermute x2, waiting for transfers between devices: 2.38 us -> 3.69 us  [shifted(): return lax.ppermute(block, axis, route)]
    pallas_call x7 -> x13, Pallas kernels: 7.64 us -> 8.41 us  [the longest x2 3.59 us: attend(): call(functools.partial(attend_kernel, side), (out,) * 3, [VMEM] * 8, (VME...]
  transfers between devices with their start and end apart: 18 -> 20, of which waited for: 8 -> 10; matrix products, arithmetic and copies ran while one was open for 0% -> 0% of each run, Pallas kernels for 13% -> 15%
where the time goes in v3:
time: 57.9 us; the launch traced here: 57.7 us
  waiting for transfers between devices  27.6 us (48%)
  starting transfers between devices  14.6 us (25%)
  Pallas kernels  12.2 us (21%)
  local copies, waits for them, and re-layouts  1.81 us (3%)
  between operations  1.52 us (3%)
    ppermute x18, waiting for transfers between devices, swapped(): lax.ppermute(block, 'seq', [(i, i ^ bit) for i in range(lax.axis_size('se...  23.9 us
    ppermute x18, starting transfers between devices, swapped(): lax.ppermute(block, 'seq', [(i, i ^ bit) for i in range(lax.axis_size('se...  12 us
    ppermute x2, waiting for transfers between devices, shifted(): return lax.ppermute(block, axis, route)  3.69 us
    pallas_call x2, Pallas kernels, attend(): call(functools.partial(attend_kernel, side), (out,) * 3, [VMEM] * 8, (VME...  3.59 us
    pallas_call x3, Pallas kernels, pack(): call(functools.partial(pack_kernel, cuts), outs, [HBM] * 3, (VMEM,) * len...  2.87 us
    ppermute x2, starting transfers between devices, shifted(): return lax.ppermute(block, axis, route)  2.58 us
    pallas_call x1, Pallas kernels, finish(): call(functools.partial(finish_kernel, places), (out, out), [SMEM] * 2 + [...  1.84 us
    unnamed x14, local copies, waits for them, and re-layouts  1.81 us
  transfers between devices with their start and end apart: 20, of which 10 were waited for; matrix products, arithmetic and copies ran while one was open for 0% of the time, Pallas kernels for 15%

profile of v3, /device:TPU:0, one launch (start us, length us, event | category | flops | bytes accessed | tf_op | source)
XLA Modules:
  0.0 57.7 jit_solution(10165678743425969288)
XLA Ops:
  0.6 2.5 %shard_map.87 = (bf16[3,128,768]{2,1,0:T(8,128)(2,1)}, bf16[3,128,768]{2,1,0:T(8,128)(2,1)}) custom-call(bf16[128,3072]{1,0:T(8,128)(2,1)} %bitcast.13, bf16[128,3072]{1,0:T(8,128)(2,1)} %bitcast.18, bf16[128,3072]{1,0:T(8,128)(2,1)} %bitcast.6), custom_call_target="tpu_custom_call" | custom-call | bytes 2359296 | tf_op jit(solution)/shard_map/pallas_call | solution.py:183
  3.2 3.0 %collective-permute-start.5 = (bf16[3,128,768]{2,1,0:T(8,128)(2,1)}, bf16[3,128,768]{2,1,0:T(8,128)(2,1)S(1)}, u32[]{:S(2)}, u32[]{:S(2)}) collective-permute-start(bf16[3,128,768]{2,1,0:T(8,128)(2,1)} %get-tuple-element.29), channel_id=1, source_target_pairs={{0,4},{1,5},{2,6},{3,7},{4,0},{5,1},{6,2},{7,3},{8,12},{9,13},{10,... | collective-permute-start | bytes 1769480 | tf_op jit(solution)/shard_map/ppermute | solution.py:24
  6.2 1.5 %collective-permute-start.1 = (bf16[3,128,768]{2,1,0:T(8,128)(2,1)}, bf16[3,128,768]{2,1,0:T(8,128)(2,1)S(1)}, u32[]{:S(2)}, u32[]{:S(2)}) collective-permute-start(bf16[3,128,768]{2,1,0:T(8,128)(2,1)} %get-tuple-element.27), channel_id=1, source_target_pairs={{0,2},{1,3},{2,0},{3,1},{4,6},{5,7},{6,4},{7,5},{8,10},{9,11},{10,... | collective-permute-start | bytes 1769480 | tf_op jit(solution)/shard_map/ppermute | solution.py:24
  7.7 1.1 %copy-done.2 = bf16[1,8,16,3072]{3,2,1,0:T(8,128)(2,1)S(1)} copy-done((bf16[1,8,16,3072]{3,2,1,0:T(8,128)(2,1)S(1)}, bf16[1,8,16,3072]{3,2,1,0:T(8,128)(2,1)}, u32[]{:S(2)}) %copy-start.2) | copy-done | bytes 786456
  9.0 0.6 collective-permute-start.9
  9.7 10.9 %collective-permute-done.5.got_ref = bf16[3,128,768]{2,1,0:T(8,128)(2,1)S(1)} collective-permute-done((bf16[3,128,768]{2,1,0:T(8,128)(2,1)}, bf16[3,128,768]{2,1,0:T(8,128)(2,1)S(1)}, u32[]{:S(2)}, u32[]{:S(2)}) %collective-permute-start.5) | collective-permute-done | bytes 589856 | tf_op jit(solution)/shard_map/ppermute | solution.py:24
  20.7 2.0 %collective-permute-done.1.got_ref = bf16[3,128,768]{2,1,0:T(8,128)(2,1)S(1)} collective-permute-done((bf16[3,128,768]{2,1,0:T(8,128)(2,1)}, bf16[3,128,768]{2,1,0:T(8,128)(2,1)S(1)}, u32[]{:S(2)}, u32[]{:S(2)}) %collective-permute-start.1) | collective-permute-done | bytes 589856 | tf_op jit(solution)/shard_map/ppermute | solution.py:24
  23.0 0.5 collective-permute-start
  23.6 1.6 %collective-permute-start.14 = (bf16[2,256,384]{2,1,0:T(8,128)(2,1)S(1)}, bf16[2,256,384]{2,1,0:T(8,128)(2,1)S(1)}, u32[]{:S(2)}, u32[]{:S(2)}) collective-permute-start(bf16[2,256,384]{2,1,0:T(8,128)(2,1)S(1)} %shard_map.97), channel_id=1, source_target_pairs={{0,2},{1,3},{2,0},{3,1},{4,6},{5,7},{6,4},{7,5},{8,10},{9,11},{10,... | collective-permute-start | bytes 1179656 | tf_op jit(solution)/shard_map/ppermute | solution.py:24
  25.1 3.1 %collective-permute-done.9.got_ref.far_ref = bf16[2,128,768]{2,1,0:T(8,128)(2,1)S(1)} collective-permute-done((bf16[2,128,768]{2,1,0:T(8,128)(2,1)S(1)}, bf16[2,128,768]{2,1,0:T(8,128)(2,1)S(1)}, u32[]{:S(2)}, u32[]{:S(2)}) %collective-permute-start.9) | collective-permute-done | bytes 393248 | tf_op jit(solution)/shard_map/ppermute | solution.py:24
  28.2 0.6 collective-permute-start.10
  28.8 2.3 %collective-permute-done.7.got_ref.far_ref = bf16[2,128,768]{2,1,0:T(8,128)(2,1)S(1)} collective-permute-done((bf16[2,128,768]{2,1,0:T(8,128)(2,1)S(1)}, bf16[2,128,768]{2,1,0:T(8,128)(2,1)S(1)}, u32[]{:S(2)}, u32[]{:S(2)}) %collective-permute-start.7) | collective-permute-done | bytes 393248 | tf_op jit(solution)/shard_map/ppermute | solution.py:24
  31.3 1.8 %shard_map.95 = (f32[512,384]{1,0:T(8,128)S(1)}, f32[512,384]{1,0:T(8,128)S(1)}, f32[512,384]{1,0:T(8,128)S(1)}) custom-call(bf16[128,3072]{1,0:T(8,128)(2,1)S(1)} %bitcast.16, bf16[128,3072]{1,0:T(8,128)(2,1)S(1)} %bitcast.21, bf16[128,3072]{1,0:T(8,128)(2,1)S(1)} %bitcast.9, bf16[3,128,384]{2,1,0:T(8,128)(2,1)S(1)} %collective-permute-done.core_ref, ...), custom_call_target="tpu_custom_call" | custom-call | flops 603979776 | bytes 3145728 | tf_op jit(solution)/shard_map/pallas_call | solution.py:302
  33.1 1.8 %shard_map.93 = (f32[512,384]{1,0:T(8,128)S(1)}, f32[512,384]{1,0:T(8,128)S(1)}, f32[512,384]{1,0:T(8,128)S(1)}) custom-call(bf16[128,3072]{1,0:T(8,128)(2,1)S(1)} %bitcast.17, bf16[128,3072]{1,0:T(8,128)(2,1)S(1)} %bitcast.22, bf16[128,3072]{1,0:T(8,128)(2,1)S(1)} %bitcast.10, bf16[3,128,384]{2,1,0:T(8,128)(2,1)S(1)} %collective-permute-done.4.core_ref, ...), custom_call_target="tpu_custom_call" | custom-call | flops 603979776 | bytes 3145728 | tf_op jit(solution)/shard_map/pallas_call | solution.py:302
  34.9 3.2 %collective-permute-done.14.far_got_ref = bf16[2,256,384]{2,1,0:T(8,128)(2,1)S(1)} collective-permute-done((bf16[2,256,384]{2,1,0:T(8,128)(2,1)S(1)}, bf16[2,256,384]{2,1,0:T(8,128)(2,1)S(1)}, u32[]{:S(2)}, u32[]{:S(2)}) %collective-permute-start.14) | collective-permute-done | bytes 393248 | tf_op jit(solution)/shard_map/ppermute | solution.py:24
  38.1 0.9 %shard_map.98 = (bf16[128,384]{1,0:T(8,128)(2,1)S(1)}, bf16[128,384]{1,0:T(8,128)(2,1)S(1)}, bf16[128,384]{1,0:T(8,128)(2,1)S(1)}, bf16[128,384]{1,0:T(8,128)(2,1)S(1)}) custom-call(bf16[128,3072]{1,0:T(8,128)(2,1)S(1)} %bitcast.11, bf16[3,128,384]{2,1,0:T(8,128)(2,1)S(1)} %collective-permute-done.4.core_ref, ...), custom_call_target="tpu_custom_call" | custom-call | flops 201326592 | bytes 3145728 | tf_op jit(solution)/shard_map/pallas_call | solution.py:344
  39.0 0.4 collective-permute-start.16
  39.5 1.4 %collective-permute-start.17 = (bf16[128,384]{1,0:T(8,128)(2,1)S(1)}, bf16[128,384]{1,0:T(8,128)(2,1)S(1)}, u32[]{:S(2)}, u32[]{:S(2)}) collective-permute-start(bf16[128,384]{1,0:T(8,128)(2,1)S(1)} %get-tuple-element.47), channel_id=1, source_target_pairs={{0,5},{1,4},{2,7},{3,6},{4,1},{5,0},{6,3},{7,2},{8,13},{9,12},{10,... | collective-permute-start | bytes 294920 | tf_op jit(solution)/shard_map/ppermute | solution.py:24
  40.9 0.9 %shard_map.96 = (bf16[128,384]{1,0:T(8,128)(2,1)S(1)}, bf16[128,384]{1,0:T(8,128)(2,1)S(1)}, bf16[128,384]{1,0:T(8,128)(2,1)S(1)}, bf16[128,384]{1,0:T(8,128)(2,1)S(1)}) custom-call(bf16[128,3072]{1,0:T(8,128)(2,1)S(1)} %bitcast.12, bf16[3,128,384]{2,1,0:T(8,128)(2,1)S(1)} %collective-permute-done.core_ref, ...), custom_call_target="tpu_custom_call" | custom-call | flops 201326592 | bytes 3145728 | tf_op jit(solution)/shard_map/pallas_call | solution.py:344
  41.8 0.4 collective-permute-start.11
  42.2 1.5 %collective-permute-start.12 = (bf16[128,384]{1,0:T(8,128)(2,1)S(1)}, bf16[128,384]{1,0:T(8,128)(2,1)S(1)}, u32[]{:S(2)}, u32[]{:S(2)}) collective-permute-start(bf16[128,384]{1,0:T(8,128)(2,1)S(1)} %get-tuple-element.39), channel_id=1, source_target_pairs={{0,2},{1,3},{2,0},{3,1},{4,6},{5,7},{6,4},{7,5},{8,10},{9,11},{10,... | collective-permute-start | bytes 294920 | tf_op jit(solution)/shard_map/ppermute | solution.py:24
  43.8 0.9 %collective-permute-done.16.refs_6_.refs_2_ = bf16[128,384]{1,0:T(8,128)(2,1)S(1)} collective-permute-done((bf16[128,384]{1,0:T(8,128)(2,1)S(1)}, bf16[128,384]{1,0:T(8,128)(2,1)S(1)}, u32[]{:S(2)}, u32[]{:S(2)}) %collective-permute-start.16) | collective-permute-done | bytes 98336 | tf_op jit(solution)/shard_map/ppermute | solution.py:24
  44.7 1.2 %collective-permute-done.17.refs_7_.refs_3_ = bf16[128,384]{1,0:T(8,128)(2,1)S(1)} collective-permute-done((bf16[128,384]{1,0:T(8,128)(2,1)S(1)}, bf16[128,384]{1,0:T(8,128)(2,1)S(1)}, u32[]{:S(2)}, u32[]{:S(2)}) %collective-permute-start.17) | collective-permute-done | bytes 98336 | tf_op jit(solution)/shard_map/ppermute | solution.py:24
  45.9 0.7 %copy-done.6 = s32[4]{0:T(128)S(1)} copy-done((s32[4]{0:T(128)S(1)}, s32[4]{0:T(128)}, u32[]{:S(2)}) %copy-start.6) | copy-done | bytes 40
  46.6 0.6 %shard_map.101 = bf16[32,1536]{1,0:T(8,128)(2,1)S(1)} custom-call(s32[4]{0:T(128)S(1)} %copy-done.6, bf16[128,3072]{1,0:T(8,128)(2,1)S(1)} %bitcast.23, bf16[128,384]{1,0:T(8,128)(2,1)S(1)} %get-tuple-element.44.refs_4_.refs_0_, bf16[128,384]{1,0:T(8,128)(2,1)S(1)} %collective-permute-done.15.refs_5_.refs_1_, ...), custom_call_target="tpu_custom_call" | custom-call | flops 98304 | bytes 294912 | tf_op jit(solution)/shard_map/pallas_call | solution.py:372
  47.2 1.3 %collective-permute-start.19 = (bf16[32,1536]{1,0:T(8,128)(2,1)S(1)}, bf16[32,1536]{1,0:T(8,128)(2,1)S(1)}, u32[]{:S(2)}, u32[]{:S(2)}) collective-permute-start(bf16[32,1536]{1,0:T(8,128)(2,1)S(1)} %shard_map.101), channel_id=1, source_target_pairs={{8,0},{16,8},{24,16},{9,1},{17,9},{25,17},{10,2},{18,10},{26,18},{... | collective-permute-start | bytes 294920 | tf_op jit(solution)/shard_map/ppermute | solution.py:20
  48.8 0.6 %shard_map.100 = bf16[32,1536]{1,0:T(8,128)(2,1)S(1)} custom-call(s32[4]{0:T(128)S(1)} %copy-done.6, bf16[128,3072]{1,0:T(8,128)(2,1)S(1)} %bitcast.24, bf16[128,384]{1,0:T(8,128)(2,1)S(1)} %get-tuple-element.37.refs_0_, bf16[128,384]{1,0:T(8,128)(2,1)S(1)} %collective-permute-done.11.refs_1_, bf16[128,384]{1,0:T(8,128)(2,1)S(1)} %collective-permute-done.12.refs_2_, ...), custom_call_target="tpu_custom_call" | custom-call | flops 98304 | bytes 294912 | tf_op jit(solution)/shard_map/pallas_call | solution.py:372
  49.4 1.3 %collective-permute-start.18 = (bf16[32,1536]{1,0:T(8,128)(2,1)S(1)}, bf16[32,1536]{1,0:T(8,128)(2,1)S(1)}, u32[]{:S(2)}, u32[]{:S(2)}) collective-permute-start(bf16[32,1536]{1,0:T(8,128)(2,1)S(1)} %shard_map.100), channel_id=1, source_target_pairs={{8,0},{16,8},{24,16},{9,1},{17,9},{25,17},{10,2},{18,10},{26,18},{... | collective-permute-start | bytes 294920 | tf_op jit(solution)/shard_map/ppermute | solution.py:20
  51.4 1.8 %shard_map.99 = (bf16[8,16,3072]{2,1,0:T(8,128)(2,1)}, bf16[8,16,3072]{2,1,0:T(8,128)(2,1)}) custom-call(s32[4]{0:T(128)S(1)} %copy-done.6, s32[1]{0:T(128)S(6)} %copy.11.offset_ref, bf16[128,3072]{1,0:T(8,128)(2,1)S(1)} %bitcast.25, bf16[128,384]{1,0:T(8,128)(2,1)S(1)} %get-tuple-element.37.refs_0_, bf16[128,384]{1,0:T(8,128)(2,1)S(1)} %collective-permute-done.11.refs_1_, ...), custom_call_target="tpu_custom_call" | custom-call | flops 786432 | bytes 3145728 | tf_op jit(solution)/shard_map/pallas_call | solution.py:420
  53.2 1.1 %collective-permute-done.19.refs_1_ = bf16[32,1536]{1,0:T(8,128)(2,1)S(1)} collective-permute-done((bf16[32,1536]{1,0:T(8,128)(2,1)S(1)}, bf16[32,1536]{1,0:T(8,128)(2,1)S(1)}, u32[]{:S(2)}, u32[]{:S(2)}) %collective-permute-start.19) | collective-permute-done | bytes 98336 | tf_op jit(solution)/shard_map/ppermute | solution.py:20
  54.3 2.6 %collective-permute-done.18.refs_0_ = bf16[32,1536]{1,0:T(8,128)(2,1)S(1)} collective-permute-done((bf16[32,1536]{1,0:T(8,128)(2,1)S(1)}, bf16[32,1536]{1,0:T(8,128)(2,1)S(1)}, u32[]{:S(2)}, u32[]{:S(2)}) %collective-permute-start.18) | collective-permute-done | bytes 98336 | tf_op jit(solution)/shard_map/ppermute | solution.py:20
  56.9 0.8 %shard_map.102 = bf16[8,16,3072]{2,1,0:T(8,128)(2,1)} custom-call(s32[1]{0:T(128)S(6)} %copy.11.offset_ref, bf16[2,16,3072]{2,1,0:T(8,128)(2,1)S(1)} %copy-done.5, bf16[32,1536]{1,0:T(8,128)(2,1)S(1)} %collective-permute-done.18.refs_0_, bf16[32,1536]{1,0:T(8,128)(2,1)S(1)} %collective-permute-done.19.refs_1_, ...), custom_call_target="tpu_custom_call", output_to_operand_aliasing={{}: (4, {})} | custom-call | bytes 589824 | tf_op jit(solution)/shard_map/pallas_call | solution.py:473
  (39 shorter events, 1.4 us)
Async XLA Ops:
  0.6 7.1 %copy-start = (bf16[1,8,16,3072]{3,2,1,0:T(8,128)(2,1)S(1)}, bf16[1,8,16,3072]{3,2,1,0:T(8,128)(2,1)}, u32[]{:S(2)}) copy-start(bf16[1,8,16,3072]{3,2,1,0:T(8,128)(2,1)} %param.8) | copy-start | bytes 2359300
  0.6 7.1 %copy-start.1 = (bf16[1,8,16,3072]{3,2,1,0:T(8,128)(2,1)S(1)}, bf16[1,8,16,3072]{3,2,1,0:T(8,128)(2,1)}, u32[]{:S(2)}) copy-start(bf16[1,8,16,3072]{3,2,1,0:T(8,128)(2,1)} %param.9) | copy-start | bytes 2359300
  3.2 17.4 %collective-permute-start.5 = (bf16[3,128,768]{2,1,0:T(8,128)(2,1)}, bf16[3,128,768]{2,1,0:T(8,128)(2,1)S(1)}, u32[]{:S(2)}, u32[]{:S(2)}) collective-permute-start(bf16[3,128,768]{2,1,0:T(8,128)(2,1)} %get-tuple-element.29), channel_id=1, source_target_pairs={{0,4},{1,5},{2,6},{3,7},{4,0},{5,1},{6,2},{7,3},{8,12},{9,13},{10,... | collective-permute-start | bytes 1769480 | tf_op jit(solution)/shard_map/ppermute | solution.py:24
  6.2 16.5 %collective-permute-start.1 = (bf16[3,128,768]{2,1,0:T(8,128)(2,1)}, bf16[3,128,768]{2,1,0:T(8,128)(2,1)S(1)}, u32[]{:S(2)}, u32[]{:S(2)}) collective-permute-start(bf16[3,128,768]{2,1,0:T(8,128)(2,1)} %get-tuple-element.27), channel_id=1, source_target_pairs={{0,2},{1,3},{2,0},{3,1},{4,6},{5,7},{6,4},{7,5},{8,10},{9,11},{10,... | collective-permute-start | bytes 1769480 | tf_op jit(solution)/shard_map/ppermute | solution.py:24
  7.7 1.1 %copy-start.2 = (bf16[1,8,16,3072]{3,2,1,0:T(8,128)(2,1)S(1)}, bf16[1,8,16,3072]{3,2,1,0:T(8,128)(2,1)}, u32[]{:S(2)}) copy-start(bf16[1,8,16,3072]{3,2,1,0:T(8,128)(2,1)} %param.10) | copy-start | bytes 2359300
  9.0 19.2 %collective-permute-start.9 = (bf16[2,128,768]{2,1,0:T(8,128)(2,1)S(1)}, bf16[2,128,768]{2,1,0:T(8,128)(2,1)S(1)}, u32[]{:S(2)}, u32[]{:S(2)}) collective-permute-start(bf16[2,128,768]{2,1,0:T(8,128)(2,1)S(1)} %get-tuple-element.33), channel_id=1, source_target_pairs={{0,4},{1,5},{2,6},{3,7},{4,0},{5,1},{6,2},{7,3},{8,12},{9,13},{10,... | collective-permute-start | bytes 1179656 | tf_op jit(solution)/shard_map/ppermute | solution.py:24
  9.6 13.2 %copy-start.3 = (bf16[1,8,16,3072]{3,2,1,0:T(8,128)(2,1)S(1)}, bf16[1,8,16,3072]{3,2,1,0:T(8,128)(2,1)}, u32[]{:S(2)}) copy-start(bf16[1,8,16,3072]{3,2,1,0:T(8,128)(2,1)} %param.10) | copy-start | bytes 2359300
  9.6 21.5 %collective-permute-start.7 = (bf16[2,128,768]{2,1,0:T(8,128)(2,1)S(1)}, bf16[2,128,768]{2,1,0:T(8,128)(2,1)S(1)}, u32[]{:S(2)}, u32[]{:S(2)}) collective-permute-start(bf16[2,128,768]{2,1,0:T(8,128)(2,1)S(1)} %get-tuple-element.30), channel_id=1, source_target_pairs={{0,2},{1,3},{2,0},{3,1},{4,6},{5,7},{6,4},{7,5},{8,10},{9,11},{10,... | collective-permute-start | bytes 1179656 | tf_op jit(solution)/shard_map/ppermute | solution.py:24
  20.6 2.9 %collective-permute-start.6 = (bf16[3,128,384]{2,1,0:T(8,128)(2,1)S(1)}, bf16[3,128,384]{2,1,0:T(8,128)(2,1)S(1)}, u32[]{:S(2)}, u32[]{:S(2)}) collective-permute-start(bf16[3,128,384]{2,1,0:T(8,128)(2,1)S(1)} %shard_map.90), channel_id=1, source_target_pairs={{0,1},{1,0},{2,3},{3,2},{4,5},{5,4},{6,7},{7,6},{8,9},{9,8},{10,11... | collective-permute-start | bytes 884744 | tf_op jit(solution)/shard_map/ppermute | solution.py:24
  22.7 5.5 %collective-permute-start.2 = (bf16[3,128,384]{2,1,0:T(8,128)(2,1)S(1)}, bf16[3,128,384]{2,1,0:T(8,128)(2,1)S(1)}, u32[]{:S(2)}, u32[]{:S(2)}) collective-permute-start(bf16[3,128,384]{2,1,0:T(8,128)(2,1)S(1)} %shard_map.88), channel_id=1, source_target_pairs={{0,1},{1,0},{2,3},{3,2},{4,5},{5,4},{6,7},{7,6},{8,9},{9,8},{10,11... | collective-permute-start | bytes 884744 | tf_op jit(solution)/shard_map/ppermute | solution.py:24
  23.0 8.2 %collective-permute-start = (bf16[3,128,384]{2,1,0:T(8,128)(2,1)S(1)}, bf16[3,128,384]{2,1,0:T(8,128)(2,1)S(1)}, u32[]{:S(2)}, u32[]{:S(2)}) collective-permute-start(bf16[3,128,384]{2,1,0:T(8,128)(2,1)S(1)} %get-tuple-element.26), channel_id=1, source_target_pairs={{0,1},{1,0},{2,3},{3,2},{4,5},{5,4},{6,7},{7,6},{8,9},{9,8},{10,11... | collective-permute-start | bytes 884744 | tf_op jit(solution)/shard_map/ppermute | solution.py:24
  23.6 14.5 %collective-permute-start.14 = (bf16[2,256,384]{2,1,0:T(8,128)(2,1)S(1)}, bf16[2,256,384]{2,1,0:T(8,128)(2,1)S(1)}, u32[]{:S(2)}, u32[]{:S(2)}) collective-permute-start(bf16[2,256,384]{2,1,0:T(8,128)(2,1)S(1)} %shard_map.97), channel_id=1, source_target_pairs={{0,2},{1,3},{2,0},{3,1},{4,6},{5,7},{6,4},{7,5},{8,10},{9,11},{10,... | collective-permute-start | bytes 1179656 | tf_op jit(solution)/shard_map/ppermute | solution.py:24
  28.2 4.9 %collective-permute-start.4 = (bf16[3,128,384]{2,1,0:T(8,128)(2,1)S(1)}, bf16[3,128,384]{2,1,0:T(8,128)(2,1)S(1)}, u32[]{:S(2)}, u32[]{:S(2)}) collective-permute-start(bf16[3,128,384]{2,1,0:T(8,128)(2,1)S(1)} %get-tuple-element.28), channel_id=1, source_target_pairs={{0,1},{1,0},{2,3},{3,2},{4,5},{5,4},{6,7},{7,6},{8,9},{9,8},{10,11... | collective-permute-start | bytes 884744 | tf_op jit(solution)/shard_map/ppermute | solution.py:24
  28.2 3.0 %collective-permute-start.10 = (bf16[2,128,384]{2,1,0:T(8,128)(2,1)S(1)}, bf16[2,128,384]{2,1,0:T(8,128)(2,1)S(1)}, u32[]{:S(2)}, u32[]{:S(2)}) collective-permute-start(bf16[2,128,384]{2,1,0:T(8,128)(2,1)S(1)} %shard_map.94), channel_id=1, source_target_pairs={{0,1},{1,0},{2,3},{3,2},{4,5},{5,4},{6,7},{7,6},{8,9},{9,8},{10,11... | collective-permute-start | bytes 589832 | tf_op jit(solution)/shard_map/ppermute | solution.py:24
  31.1 9.8 %collective-permute-start.3 = (bf16[2,256,384]{2,1,0:T(8,128)(2,1)S(1)}, bf16[2,256,384]{2,1,0:T(8,128)(2,1)S(1)}, u32[]{:S(2)}, u32[]{:S(2)}) collective-permute-start(bf16[2,256,384]{2,1,0:T(8,128)(2,1)S(1)} %shard_map.89), channel_id=1, source_target_pairs={{0,4},{1,5},{2,6},{3,7},{4,0},{5,1},{6,2},{7,3},{8,12},{9,13},{10,... | collective-permute-start | bytes 1179656 | tf_op jit(solution)/shard_map/ppermute | solution.py:24
  31.2 1.9 %collective-permute-start.8 = (bf16[2,128,384]{2,1,0:T(8,128)(2,1)S(1)}, bf16[2,128,384]{2,1,0:T(8,128)(2,1)S(1)}, u32[]{:S(2)}, u32[]{:S(2)}) collective-permute-start(bf16[2,128,384]{2,1,0:T(8,128)(2,1)S(1)} %shard_map.92), channel_id=1, source_target_pairs={{0,1},{1,0},{2,3},{3,2},{4,5},{5,4},{6,7},{7,6},{8,9},{9,8},{10,11... | collective-permute-start | bytes 589832 | tf_op jit(solution)/shard_map/ppermute | solution.py:24
  39.0 4.8 %collective-permute-start.15 = (bf16[128,384]{1,0:T(8,128)(2,1)S(1)}, bf16[128,384]{1,0:T(8,128)(2,1)S(1)}, u32[]{:S(2)}, u32[]{:S(2)}) collective-permute-start(bf16[128,384]{1,0:T(8,128)(2,1)S(1)} %get-tuple-element.45), channel_id=1, source_target_pairs={{0,1},{1,0},{2,3},{3,2},{4,5},{5,4},{6,7},{7,6},{8,9},{9,8},{10,11... | collective-permute-start | bytes 294920 | tf_op jit(solution)/shard_map/ppermute | solution.py:24
  39.0 5.7 %collective-permute-start.16 = (bf16[128,384]{1,0:T(8,128)(2,1)S(1)}, bf16[128,384]{1,0:T(8,128)(2,1)S(1)}, u32[]{:S(2)}, u32[]{:S(2)}) collective-permute-start(bf16[128,384]{1,0:T(8,128)(2,1)S(1)} %get-tuple-element.46), channel_id=1, source_target_pairs={{0,4},{1,5},{2,6},{3,7},{4,0},{5,1},{6,2},{7,3},{8,12},{9,13},{10,... | collective-permute-start | bytes 294920 | tf_op jit(solution)/shard_map/ppermute | solution.py:24
  39.5 6.4 %collective-permute-start.17 = (bf16[128,384]{1,0:T(8,128)(2,1)S(1)}, bf16[128,384]{1,0:T(8,128)(2,1)S(1)}, u32[]{:S(2)}, u32[]{:S(2)}) collective-permute-start(bf16[128,384]{1,0:T(8,128)(2,1)S(1)} %get-tuple-element.47), channel_id=1, source_target_pairs={{0,5},{1,4},{2,7},{3,6},{4,1},{5,0},{6,3},{7,2},{8,13},{9,12},{10,... | collective-permute-start | bytes 294920 | tf_op jit(solution)/shard_map/ppermute | solution.py:24
  40.9 5.0 %copy-start.4 = (bf16[1,8,16,3072]{3,2,1,0:T(8,128)(2,1)S(1)}, bf16[1,8,16,3072]{3,2,1,0:T(8,128)(2,1)}, u32[]{:S(2)}) copy-start(bf16[1,8,16,3072]{3,2,1,0:T(8,128)(2,1)} %param.7) | copy-start | bytes 2359300
  41.8 6.7 %collective-permute-start.11 = (bf16[128,384]{1,0:T(8,128)(2,1)S(1)}, bf16[128,384]{1,0:T(8,128)(2,1)S(1)}, u32[]{:S(2)}, u32[]{:S(2)}) collective-permute-start(bf16[128,384]{1,0:T(8,128)(2,1)S(1)} %get-tuple-element.38), channel_id=1, source_target_pairs={{0,1},{1,0},{2,3},{3,2},{4,5},{5,4},{6,7},{7,6},{8,9},{9,8},{10,11... | collective-permute-start | bytes 294920 | tf_op jit(solution)/shard_map/ppermute | solution.py:24
  42.2 6.3 %collective-permute-start.12 = (bf16[128,384]{1,0:T(8,128)(2,1)S(1)}, bf16[128,384]{1,0:T(8,128)(2,1)S(1)}, u32[]{:S(2)}, u32[]{:S(2)}) collective-permute-start(bf16[128,384]{1,0:T(8,128)(2,1)S(1)} %get-tuple-element.39), channel_id=1, source_target_pairs={{0,2},{1,3},{2,0},{3,1},{4,6},{5,7},{6,4},{7,5},{8,10},{9,11},{10,... | collective-permute-start | bytes 294920 | tf_op jit(solution)/shard_map/ppermute | solution.py:24
  43.7 5.1 %collective-permute-start.13 = (bf16[128,384]{1,0:T(8,128)(2,1)S(1)}, bf16[128,384]{1,0:T(8,128)(2,1)S(1)}, u32[]{:S(2)}, u32[]{:S(2)}) collective-permute-start(bf16[128,384]{1,0:T(8,128)(2,1)S(1)} %get-tuple-element.40), channel_id=1, source_target_pairs={{0,3},{1,2},{2,1},{3,0},{4,7},{5,6},{6,5},{7,4},{8,11},{9,10},{10,... | collective-permute-start | bytes 294920 | tf_op jit(solution)/shard_map/ppermute | solution.py:24
  45.9 0.7 %copy-start.6 = (s32[4]{0:T(128)S(1)}, s32[4]{0:T(128)}, u32[]{:S(2)}) copy-start(s32[4]{0:T(128)} %timesteps_ref.5) | copy-start | bytes 52
  47.2 7.2 %collective-permute-start.19 = (bf16[32,1536]{1,0:T(8,128)(2,1)S(1)}, bf16[32,1536]{1,0:T(8,128)(2,1)S(1)}, u32[]{:S(2)}, u32[]{:S(2)}) collective-permute-start(bf16[32,1536]{1,0:T(8,128)(2,1)S(1)} %shard_map.101), channel_id=1, source_target_pairs={{8,0},{16,8},{24,16},{9,1},{17,9},{25,17},{10,2},{18,10},{26,18},{... | collective-permute-start | bytes 294920 | tf_op jit(solution)/shard_map/ppermute | solution.py:20
  49.4 7.5 %collective-permute-start.18 = (bf16[32,1536]{1,0:T(8,128)(2,1)S(1)}, bf16[32,1536]{1,0:T(8,128)(2,1)S(1)}, u32[]{:S(2)}, u32[]{:S(2)}) collective-permute-start(bf16[32,1536]{1,0:T(8,128)(2,1)S(1)} %shard_map.100), channel_id=1, source_target_pairs={{8,0},{16,8},{24,16},{9,1},{17,9},{25,17},{10,2},{18,10},{26,18},{... | collective-permute-start | bytes 294920 | tf_op jit(solution)/shard_map/ppermute | solution.py:20
  51.4 5.6 %copy-start.5 = (bf16[2,16,3072]{2,1,0:T(8,128)(2,1)S(1)}, bf16[2,16,3072]{2,1,0:T(8,128)(2,1)}, u32[]{:S(2)}) copy-start(bf16[2,16,3072]{2,1,0:T(8,128)(2,1)} %fresh_ref.1) | copy-start | bytes 589828

commit v4 on v3

--- a/solution.py
+++ b/solution.py
@@ -106,14 +106,12 @@
 
 
 VMEM_LIMIT = 16 * 1024 * 1024
-PACK_LIMIT = 249 * 256 * 1024
 VMEM = pl.BlockSpec(memory_space=pltpu.VMEM)
 SMEM = pl.BlockSpec(memory_space=pltpu.SMEM)
 HBM = pl.BlockSpec(memory_space=pltpu.HBM)
 
 
 def call(kernel, out_shape, in_specs, out_specs, scratch_shapes=(), cost=(0, 0, 0), **options):
-    limit = options.pop("limit", VMEM_LIMIT)
     return pl.pallas_call(
         kernel,
         out_shape=out_shape,
@@ -123,7 +121,7 @@
         cost_estimate=pl.CostEstimate(
             flops=cost[0], bytes_accessed=cost[1], transcendentals=cost[2]
         ),
-        compiler_params=pltpu.CompilerParams(vmem_limit_bytes=limit),
+        compiler_params=pltpu.CompilerParams(vmem_limit_bytes=VMEM_LIMIT),
         **options,
     )
 
@@ -151,11 +149,15 @@
     return (CORE, side[0], side[0] | CORE)
 
 
-def step_size(timesteps_ref):
+def step_kernel(timesteps_ref, out_ref):
     position, queue_count = lax.axis_index("queue"), lax.axis_size("queue")
-    step = jnp.full((1, HEAD_SIZE), timesteps_ref[position], jnp.int32)
-    delta = 8.0 * (level(step - 1, 8 * queue_count) - level(step, 8 * queue_count))
-    return delta[:, :1]
+    step = jnp.full(out_ref.shape, timesteps_ref[position], jnp.int32)
+    out_ref[...] = 8.0 * (level(step - 1, 8 * queue_count) - level(step, 8 * queue_count))
+
+
+def step_size(timesteps):
+    out = jax.ShapeDtypeStruct((1, HEAD_SIZE), jnp.float32)
+    return call(step_kernel, out, [SMEM], VMEM)(timesteps)
 
 
 def pack_kernel(cuts, *refs):
@@ -172,7 +174,7 @@
         copy.wait()
 
 
-def pack(cuts, arrays, limit):
+def pack(cuts, arrays):
     rows, width = arrays[0].shape
     outs = tuple(
         jax.ShapeDtypeStruct(
@@ -187,8 +189,7 @@
         (VMEM,) * len(outs),
         [pltpu.SemaphoreType.DMA((len(outs), 3))],
         (0, sum(4 * out.size for out in outs), 0),
-        limit=limit,
-    )(*arrays)
+    )(*[pltpu.with_memory_space_constraint(array, pltpu.HBM) for array in arrays])
 
 
 def split_kernel(got_ref, out_ref):
@@ -355,33 +356,33 @@
     return (latents.astype(jnp.float32) + change).astype(jnp.bfloat16)
 
 
-def lead_kernel(places, timesteps_ref, latents_ref, *refs):
+def lead_kernel(places, delta_ref, latents_ref, *refs):
     pieces, out_ref = refs[:-1], refs[-1]
-    rows, width = out_ref.shape[0], latents_ref.shape[1]
-    delta = step_size(timesteps_ref)
+    rows, width = latents_ref.shape
+    delta = delta_ref[:, :1]
     at = 0
     for place, piece in zip(places, pieces):
         size = piece.shape[1]
         cols = columns(*place, width)
-        out_ref[:, at : at + size] = moved(latents_ref[:rows, cols], piece[:rows], delta)
+        out_ref[:, at : at + size] = moved(latents_ref[:, cols], piece[:rows], delta)
         at += size
 
 
-def lead(places, rows, timesteps, latents, pieces):
-    size = sum(piece.shape[1] for piece in pieces)
+def lead(places, delta, latents, pieces):
+    rows, size = latents.shape[0], sum(piece.shape[1] for piece in pieces)
     return call(
         functools.partial(lead_kernel, places),
         jax.ShapeDtypeStruct((rows, size), jnp.bfloat16),
-        [SMEM] + [VMEM] * (1 + len(pieces)),
+        [VMEM] * (2 + len(pieces)),
         VMEM,
         cost=(2 * rows * size, 6 * rows * size, 0),
-    )(timesteps, latents, *pieces)
-
-
-def finish_kernel(places, timesteps_ref, offset_ref, latents_ref, *refs):
+    )(delta, latents, *pieces)
+
+
+def finish_kernel(places, offset_ref, delta_ref, latents_ref, *refs):
     pieces = refs[: len(places)]
     attended_ref, advanced_ref, whole_ref, updated_ref, out_sem, move_sem = refs[len(places) :]
-    offset, delta = offset_ref[0], step_size(timesteps_ref)
+    offset, delta = offset_ref[0], delta_ref[:, :1]
     frames, rows, width = attended_ref.shape
     out_copies, move_copies = [], []
     for frame in range(frames):
@@ -415,12 +416,12 @@
             copy.wait()
 
 
-def finish(shape, places, timesteps, offsets, latents, pieces):
+def finish(shape, places, offsets, delta, latents, pieces):
     out = jax.ShapeDtypeStruct(shape, jnp.bfloat16)
     return call(
         functools.partial(finish_kernel, places),
         (out, out),
-        [SMEM] * 2 + [VMEM] * (1 + len(pieces)),
+        [SMEM] + [VMEM] * (2 + len(pieces)),
         (HBM, HBM),
         [
             pltpu.VMEM(shape, jnp.bfloat16),
@@ -429,7 +430,7 @@
             pltpu.SemaphoreType.DMA((shape[0],)),
         ],
         (2 * latents.size, 8 * latents.size, 0),
-    )(timesteps, offsets, latents, *pieces)
+    )(offsets, delta, latents, *pieces)
 
 
 def fill_kernel(groups, offset_ref, fresh_ref, *refs):
@@ -491,9 +492,13 @@
     )
     sides = ((ACROSS, DOWN, 0), (DOWN, ACROSS, width // 2))
     arrays = (keys, values, queries)
-    sends = pack([(half_columns, side, side[0], 3) for side in sides], arrays, PACK_LIMIT)
-    owns = pack([(half_columns, side, 0, 2) for side in sides], arrays, VMEM_LIMIT)
-    cores = pack([(columns, side, CORE, 3) for side in sides], arrays, VMEM_LIMIT)
+    sends = pack([(half_columns, side, side[0], 3) for side in sides], arrays)
+    owns = pack(
+        [(half_columns, side, 0, 2) for side in sides]
+        + [(columns, side, CORE, 3) for side in sides],
+        arrays,
+    )
+    owns, cores = owns[: len(sides)], owns[len(sides) :]
     gots = [swapped(send, side[0]) for side, send in zip(sides, sends)]
     fars = [swapped(own, side[1]) for side, own in zip(sides, owns)]
     cores = [swapped(core, CORE) for core in cores]
@@ -504,7 +509,9 @@
     ]
     received = list(zip(cores, gots, got_cores, fars, far_cores))
     states = [attend(side, *arrays, *parts) for side, parts in zip(sides, received)]
-    far_gots = [after(far, states[1 - index][0]) for index, far in enumerate(far_gots)]
+    delta = step_size(timesteps)
+    first_latents = latents[:first_rows]
+    far_gots = [after(far, states[1 - index][0], delta) for index, far in enumerate(far_gots)]
     pieces, places, groups, leads = [], [], [], []
     for index, side in enumerate(sides):
         own, *backs = complete(
@@ -518,11 +525,11 @@
         )
         groups.append([(side, mask) for mask in (0, *peers(side))])
         parts = [own] + [swapped(back, mask) for back, mask in zip(backs, peers(side))]
-        head = lead(groups[-1], first_rows, timesteps, latents, parts)
+        head = lead(groups[-1], delta, first_latents, parts)
         leads.append(shifted(head, "queue", -1))
         pieces += parts
         places += groups[-1]
-    attended, advanced = finish(shape, places, timesteps, offsets, latents, pieces)
+    attended, advanced = finish(shape, places, offsets, delta, latents, pieces)
     advanced = fill(groups, offsets, fresh_frames, leads, advanced)
     return (attended[None], advanced[None])
 

time: 57.9 us -> 55.4 us (0.957)
  local copies, waits for them, and re-layouts: 1.81 us -> 0.05 us
  Pallas kernels: 12.2 us -> 11.3 us
    unnamed x14 -> x12, local copies, waits for them, and re-layouts: 1.81 us -> 0.03 us
    pallas_call x2, Pallas kernels: 1.2 us -> 0.2 us  [lead(): call(functools.partial(lead_kernel, places), jax.ShapeDtypeStruct((rows,...]
    pallas_call x3 -> x2, Pallas kernels: 2.87 us -> 2.92 us  [pack(): call(functools.partial(pack_kernel, cuts), outs, [HBM] * 3, (VMEM,) * len...]
    pallas_call x1 -> x2, Pallas kernels: 1.84 us -> 1.88 us  [the longest x1 1.32 us: finish(): call(functools.partial(finish_kernel, places), (out, out), [SMEM] + [VMEM...]
  transfers between devices with their start and end apart: 20 -> 20, of which waited for: 10 -> 11; matrix products, arithmetic and copies ran while one was open for 0% -> 0% of each run, Pallas kernels for 15% -> 17%
where the time goes in v4:
time: 55.4 us; the launch traced here: 55.1 us
  waiting for transfers between devices  27.7 us (50%)
  starting transfers between devices  14.5 us (26%)
  Pallas kernels  11.3 us (20%)
  between operations  1.54 us (3%)
    ppermute x18, waiting for transfers between devices, swapped(): lax.ppermute(block, 'seq', [(i, i ^ bit) for i in range(lax.axis_size('se...  24.2 us
    ppermute x18, starting transfers between devices, swapped(): lax.ppermute(block, 'seq', [(i, i ^ bit) for i in range(lax.axis_size('se...  12 us
    pallas_call x2, Pallas kernels, attend(): call(functools.partial(attend_kernel, side), (out,) * 3, [VMEM] * 8, (VME...  3.6 us
    ppermute x2, waiting for transfers between devices, shifted(): return lax.ppermute(block, axis, route)  3.53 us
    pallas_call x2, Pallas kernels, pack(): call(functools.partial(pack_kernel, cuts), outs, [HBM] * 3, (VMEM,) * len...  2.92 us
    ppermute x2, starting transfers between devices, shifted(): return lax.ppermute(block, axis, route)  2.58 us
    pallas_call x2, Pallas kernels, complete(): call(functools.partial(complete_kernel, side), (out,) * 4, [VMEM] * 8, (V...  1.8 us
    pallas_call x1, Pallas kernels, finish(): call(functools.partial(finish_kernel, places), (out, out), [SMEM] + [VMEM...  1.32 us
  transfers between devices with their start and end apart: 20, of which 11 were waited for; matrix products, arithmetic and copies ran while one was open for 0% of the time, Pallas kernels for 17%

profile of v4, /device:TPU:0, one launch (start us, length us, event | category | flops | bytes accessed | tf_op | source)
XLA Modules:
  0.0 55.1 jit_solution(114796096419652019)
XLA Ops:
  0.6 1.4 %shard_map.88 = (bf16[3,128,768]{2,1,0:T(8,128)(2,1)S(1)}, bf16[3,128,768]{2,1,0:T(8,128)(2,1)S(1)}) custom-call(bf16[128,3072]{1,0:T(8,128)(2,1)} %bitcast.13, bf16[128,3072]{1,0:T(8,128)(2,1)} %bitcast.17, bf16[128,3072]{1,0:T(8,128)(2,1)} %bitcast.7), custom_call_target="tpu_custom_call" | custom-call | bytes 2359296 | tf_op jit(solution)/shard_map/pallas_call | solution.py:185
  2.1 3.0 %collective-permute-start.5 = (bf16[3,128,768]{2,1,0:T(8,128)(2,1)S(1)}, bf16[3,128,768]{2,1,0:T(8,128)(2,1)S(1)}, u32[]{:S(2)}, u32[]{:S(2)}) collective-permute-start(bf16[3,128,768]{2,1,0:T(8,128)(2,1)S(1)} %get-tuple-element.29), channel_id=1, source_target_pairs={{0,4},{1,5},{2,6},{3,7},{4,0},{5,1},{6,2},{7,3},{8,12},{9,13},{10,... | collective-permute-start | bytes 1769480 | tf_op jit(solution)/shard_map/ppermute | solution.py:24
  5.1 1.5 %collective-permute-start.1 = (bf16[3,128,768]{2,1,0:T(8,128)(2,1)S(1)}, bf16[3,128,768]{2,1,0:T(8,128)(2,1)S(1)}, u32[]{:S(2)}, u32[]{:S(2)}) collective-permute-start(bf16[3,128,768]{2,1,0:T(8,128)(2,1)S(1)} %get-tuple-element.27), channel_id=1, source_target_pairs={{0,2},{1,3},{2,0},{3,1},{4,6},{5,7},{6,4},{7,5},{8,10},{9,11},{10,... | collective-permute-start | bytes 1769480 | tf_op jit(solution)/shard_map/ppermute | solution.py:24
  6.6 1.5 %shard_map.87 = (bf16[2,128,768]{2,1,0:T(8,128)(2,1)S(1)}, bf16[2,128,768]{2,1,0:T(8,128)(2,1)S(1)}, bf16[3,128,384]{2,1,0:T(8,128)(2,1)S(1)}, bf16[3,128,384]{2,1,0:T(8,128)(2,1)S(1)}) custom-call(bf16[128,3072]{1,0:T(8,128)(2,1)} %bitcast.14, bf16[128,3072]{1,0:T(8,128)(2,1)} %bitcast.18, bf16[128,3072]{1,0:T(8,128)(2,1)} %bitcast.8), custom_call_target="tpu_custom_call" | custom-call | bytes 2752512 | tf_op jit(solution)/shard_map/pallas_call | solution.py:185
  8.1 0.6 %collective-permute-start.9 = (bf16[2,128,768]{2,1,0:T(8,128)(2,1)S(1)}, bf16[2,128,768]{2,1,0:T(8,128)(2,1)S(1)}, u32[]{:S(2)}, u32[]{:S(2)}) collective-permute-start(bf16[2,128,768]{2,1,0:T(8,128)(2,1)S(1)} %get-tuple-element.33), channel_id=1, source_target_pairs={{0,4},{1,5},{2,6},{3,7},{4,0},{5,1},{6,2},{7,3},{8,12},{9,13},{10,... | collective-permute-start | bytes 1179656 | tf_op jit(solution)/shard_map/ppermute | solution.py:24
  8.8 10.5 %collective-permute-done.5.got_ref = bf16[3,128,768]{2,1,0:T(8,128)(2,1)S(1)} collective-permute-done((bf16[3,128,768]{2,1,0:T(8,128)(2,1)S(1)}, bf16[3,128,768]{2,1,0:T(8,128)(2,1)S(1)}, u32[]{:S(2)}, u32[]{:S(2)}) %collective-permute-start.5) | collective-permute-done | bytes 589856 | tf_op jit(solution)/shard_map/ppermute | solution.py:24
  19.4 2.0 %collective-permute-done.1.got_ref = bf16[3,128,768]{2,1,0:T(8,128)(2,1)S(1)} collective-permute-done((bf16[3,128,768]{2,1,0:T(8,128)(2,1)S(1)}, bf16[3,128,768]{2,1,0:T(8,128)(2,1)S(1)}, u32[]{:S(2)}, u32[]{:S(2)}) %collective-permute-start.1) | collective-permute-done | bytes 589856 | tf_op jit(solution)/shard_map/ppermute | solution.py:24
  21.4 0.5 collective-permute-start
  22.0 1.6 %collective-permute-start.14 = (bf16[2,256,384]{2,1,0:T(8,128)(2,1)S(1)}, bf16[2,256,384]{2,1,0:T(8,128)(2,1)S(1)}, u32[]{:S(2)}, u32[]{:S(2)}) collective-permute-start(bf16[2,256,384]{2,1,0:T(8,128)(2,1)S(1)} %shard_map.97), channel_id=1, source_target_pairs={{0,2},{1,3},{2,0},{3,1},{4,6},{5,7},{6,4},{7,5},{8,10},{9,11},{10,... | collective-permute-start | bytes 1179656 | tf_op jit(solution)/shard_map/ppermute | solution.py:24
  23.5 3.3 %collective-permute-done.9.got_ref.far_ref = bf16[2,128,768]{2,1,0:T(8,128)(2,1)S(1)} collective-permute-done((bf16[2,128,768]{2,1,0:T(8,128)(2,1)S(1)}, bf16[2,128,768]{2,1,0:T(8,128)(2,1)S(1)}, u32[]{:S(2)}, u32[]{:S(2)}) %collective-permute-start.9) | collective-permute-done | bytes 393248 | tf_op jit(solution)/shard_map/ppermute | solution.py:24
  26.9 0.6 %collective-permute-start.10 = (bf16[2,128,384]{2,1,0:T(8,128)(2,1)S(1)}, bf16[2,128,384]{2,1,0:T(8,128)(2,1)S(1)}, u32[]{:S(2)}, u32[]{:S(2)}) collective-permute-start(bf16[2,128,384]{2,1,0:T(8,128)(2,1)S(1)} %shard_map.94), channel_id=1, source_target_pairs={{0,1},{1,0},{2,3},{3,2},{4,5},{5,4},{6,7},{7,6},{8,9},{9,8},{10,11... | collective-permute-start | bytes 589832 | tf_op jit(solution)/shard_map/ppermute | solution.py:24
  27.5 2.2 %collective-permute-done.7.got_ref.far_ref = bf16[2,128,768]{2,1,0:T(8,128)(2,1)S(1)} collective-permute-done((bf16[2,128,768]{2,1,0:T(8,128)(2,1)S(1)}, bf16[2,128,768]{2,1,0:T(8,128)(2,1)S(1)}, u32[]{:S(2)}, u32[]{:S(2)}) %collective-permute-start.7) | collective-permute-done | bytes 393248 | tf_op jit(solution)/shard_map/ppermute | solution.py:24
  29.9 0.6 %shard_map.86.delta_ref = f32[1,128]{1,0:T(1,128)S(1)} custom-call(s32[4]{0:T(128)S(1)} %copy-done.5), custom_call_target="tpu_custom_call" | custom-call | tf_op jit(solution)/shard_map/pallas_call | solution.py:160
  30.5 1.8 %shard_map.95 = (f32[512,384]{1,0:T(8,128)S(1)}, f32[512,384]{1,0:T(8,128)S(1)}, f32[512,384]{1,0:T(8,128)S(1)}) custom-call(bf16[128,3072]{1,0:T(8,128)(2,1)S(1)} %bitcast.15, bf16[128,3072]{1,0:T(8,128)(2,1)S(1)} %bitcast.19, bf16[128,3072]{1,0:T(8,128)(2,1)S(1)} %bitcast.9, bf16[3,128,384]{2,1,0:T(8,128)(2,1)S(1)} %collective-permute-done.core_ref, ...), custom_call_target="tpu_custom_call" | custom-call | flops 603979776 | bytes 3145728 | tf_op jit(solution)/shard_map/pallas_call | solution.py:303
  32.4 1.8 %shard_map.93 = (f32[512,384]{1,0:T(8,128)S(1)}, f32[512,384]{1,0:T(8,128)S(1)}, f32[512,384]{1,0:T(8,128)S(1)}) custom-call(bf16[128,3072]{1,0:T(8,128)(2,1)S(1)} %bitcast.16, bf16[128,3072]{1,0:T(8,128)(2,1)S(1)} %bitcast.20, bf16[128,3072]{1,0:T(8,128)(2,1)S(1)} %bitcast.10, bf16[3,128,384]{2,1,0:T(8,128)(2,1)S(1)} %collective-permute-done.4.core_ref, ...), custom_call_target="tpu_custom_call" | custom-call | flops 603979776 | bytes 3145728 | tf_op jit(solution)/shard_map/pallas_call | solution.py:303
  34.2 2.6 %collective-permute-done.14.far_got_ref = bf16[2,256,384]{2,1,0:T(8,128)(2,1)S(1)} collective-permute-done((bf16[2,256,384]{2,1,0:T(8,128)(2,1)S(1)}, bf16[2,256,384]{2,1,0:T(8,128)(2,1)S(1)}, u32[]{:S(2)}, u32[]{:S(2)}) %collective-permute-start.14) | collective-permute-done | bytes 393248 | tf_op jit(solution)/shard_map/ppermute | solution.py:24
  36.7 0.9 %shard_map.98 = (bf16[128,384]{1,0:T(8,128)(2,1)S(1)}, bf16[128,384]{1,0:T(8,128)(2,1)S(1)}, bf16[128,384]{1,0:T(8,128)(2,1)S(1)}, bf16[128,384]{1,0:T(8,128)(2,1)S(1)}) custom-call(bf16[128,3072]{1,0:T(8,128)(2,1)S(1)} %bitcast.11, bf16[3,128,384]{2,1,0:T(8,128)(2,1)S(1)} %collective-permute-done.4.core_ref, ...), custom_call_target="tpu_custom_call" | custom-call | flops 201326592 | bytes 3145728 | tf_op jit(solution)/shard_map/pallas_call | solution.py:345
  37.7 0.4 collective-permute-start.16
  38.1 1.4 %collective-permute-start.17 = (bf16[128,384]{1,0:T(8,128)(2,1)S(1)}, bf16[128,384]{1,0:T(8,128)(2,1)S(1)}, u32[]{:S(2)}, u32[]{:S(2)}) collective-permute-start(bf16[128,384]{1,0:T(8,128)(2,1)S(1)} %get-tuple-element.47), channel_id=1, source_target_pairs={{0,5},{1,4},{2,7},{3,6},{4,1},{5,0},{6,3},{7,2},{8,13},{9,12},{10,... | collective-permute-start | bytes 294920 | tf_op jit(solution)/shard_map/ppermute | solution.py:24
  39.6 0.9 %shard_map.96 = (bf16[128,384]{1,0:T(8,128)(2,1)S(1)}, bf16[128,384]{1,0:T(8,128)(2,1)S(1)}, bf16[128,384]{1,0:T(8,128)(2,1)S(1)}, bf16[128,384]{1,0:T(8,128)(2,1)S(1)}) custom-call(bf16[128,3072]{1,0:T(8,128)(2,1)S(1)} %bitcast.12, bf16[3,128,384]{2,1,0:T(8,128)(2,1)S(1)} %collective-permute-done.core_ref, ...), custom_call_target="tpu_custom_call" | custom-call | flops 201326592 | bytes 3145728 | tf_op jit(solution)/shard_map/pallas_call | solution.py:345
  40.5 0.4 collective-permute-start.11
  40.9 1.5 %collective-permute-start.12 = (bf16[128,384]{1,0:T(8,128)(2,1)S(1)}, bf16[128,384]{1,0:T(8,128)(2,1)S(1)}, u32[]{:S(2)}, u32[]{:S(2)}) collective-permute-start(bf16[128,384]{1,0:T(8,128)(2,1)S(1)} %get-tuple-element.39), channel_id=1, source_target_pairs={{0,2},{1,3},{2,0},{3,1},{4,6},{5,7},{6,4},{7,5},{8,10},{9,11},{10,... | collective-permute-start | bytes 294920 | tf_op jit(solution)/shard_map/ppermute | solution.py:24
  42.5 0.9 %collective-permute-done.16.refs_6_.refs_2_ = bf16[128,384]{1,0:T(8,128)(2,1)S(1)} collective-permute-done((bf16[128,384]{1,0:T(8,128)(2,1)S(1)}, bf16[128,384]{1,0:T(8,128)(2,1)S(1)}, u32[]{:S(2)}, u32[]{:S(2)}) %collective-permute-start.16) | collective-permute-done | bytes 98336 | tf_op jit(solution)/shard_map/ppermute | solution.py:24
  43.4 1.2 %collective-permute-done.17.refs_7_.refs_3_ = bf16[128,384]{1,0:T(8,128)(2,1)S(1)} collective-permute-done((bf16[128,384]{1,0:T(8,128)(2,1)S(1)}, bf16[128,384]{1,0:T(8,128)(2,1)S(1)}, u32[]{:S(2)}, u32[]{:S(2)}) %collective-permute-start.17) | collective-permute-done | bytes 98336 | tf_op jit(solution)/shard_map/ppermute | solution.py:24
  44.7 1.3 %collective-permute-start.19 = (bf16[32,1536]{1,0:T(8,128)(2,1)S(1)}, bf16[32,1536]{1,0:T(8,128)(2,1)S(1)}, u32[]{:S(2)}, u32[]{:S(2)}) collective-permute-start(bf16[32,1536]{1,0:T(8,128)(2,1)S(1)} %shard_map.101), channel_id=1, source_target_pairs={{8,0},{16,8},{24,16},{9,1},{17,9},{25,17},{10,2},{18,10},{26,18},{... | collective-permute-start | bytes 294920 | tf_op jit(solution)/shard_map/ppermute | solution.py:20
  46.0 0.2 collective-permute-done.12.refs_2_
  46.2 1.3 %collective-permute-done.13.refs_3_ = bf16[128,384]{1,0:T(8,128)(2,1)S(1)} collective-permute-done((bf16[128,384]{1,0:T(8,128)(2,1)S(1)}, bf16[128,384]{1,0:T(8,128)(2,1)S(1)}, u32[]{:S(2)}, u32[]{:S(2)}) %collective-permute-start.13) | collective-permute-done | bytes 98336 | tf_op jit(solution)/shard_map/ppermute | solution.py:24
  47.6 1.3 %collective-permute-start.18 = (bf16[32,1536]{1,0:T(8,128)(2,1)S(1)}, bf16[32,1536]{1,0:T(8,128)(2,1)S(1)}, u32[]{:S(2)}, u32[]{:S(2)}) collective-permute-start(bf16[32,1536]{1,0:T(8,128)(2,1)S(1)} %shard_map.100), channel_id=1, source_target_pairs={{8,0},{16,8},{24,16},{9,1},{17,9},{25,17},{10,2},{18,10},{26,18},{... | collective-permute-start | bytes 294920 | tf_op jit(solution)/shard_map/ppermute | solution.py:20
  49.5 1.3 %shard_map.99 = (bf16[8,16,3072]{2,1,0:T(8,128)(2,1)}, bf16[8,16,3072]{2,1,0:T(8,128)(2,1)}) custom-call(s32[1]{0:T(128)S(6)} %copy.11.offset_ref, f32[1,128]{1,0:T(1,128)S(1)} %shard_map.86.delta_ref, bf16[128,3072]{1,0:T(8,128)(2,1)S(1)} %bitcast.23, bf16[128,384]{1,0:T(8,128)(2,1)S(1)} %get-tuple-element.37.refs_0_, ...), custom_call_target="tpu_custom_call" | custom-call | flops 786432 | bytes 3145728 | tf_op jit(solution)/shard_map/pallas_call | solution.py:421
  50.9 1.0 %collective-permute-done.19.refs_1_ = bf16[32,1536]{1,0:T(8,128)(2,1)S(1)} collective-permute-done((bf16[32,1536]{1,0:T(8,128)(2,1)S(1)}, bf16[32,1536]{1,0:T(8,128)(2,1)S(1)}, u32[]{:S(2)}, u32[]{:S(2)}) %collective-permute-start.19) | collective-permute-done | bytes 98336 | tf_op jit(solution)/shard_map/ppermute | solution.py:20
  51.8 2.5 %collective-permute-done.18.refs_0_ = bf16[32,1536]{1,0:T(8,128)(2,1)S(1)} collective-permute-done((bf16[32,1536]{1,0:T(8,128)(2,1)S(1)}, bf16[32,1536]{1,0:T(8,128)(2,1)S(1)}, u32[]{:S(2)}, u32[]{:S(2)}) %collective-permute-start.18) | collective-permute-done | bytes 98336 | tf_op jit(solution)/shard_map/ppermute | solution.py:20
  54.4 0.7 %shard_map.102 = bf16[8,16,3072]{2,1,0:T(8,128)(2,1)} custom-call(s32[1]{0:T(128)S(6)} %copy.11.offset_ref, bf16[2,16,3072]{2,1,0:T(8,128)(2,1)S(1)} %copy-done.4, bf16[32,1536]{1,0:T(8,128)(2,1)S(1)} %collective-permute-done.18.refs_0_, bf16[32,1536]{1,0:T(8,128)(2,1)S(1)} %collective-permute-done.19.refs_1_, ...), custom_call_target="tpu_custom_call", output_to_operand_aliasing={{}: (4, {})} | custom-call | bytes 589824 | tf_op jit(solution)/shard_map/pallas_call | solution.py:474
  (38 shorter events, 0.9 us)
Async XLA Ops:
  2.1 17.2 %collective-permute-start.5 = (bf16[3,128,768]{2,1,0:T(8,128)(2,1)S(1)}, bf16[3,128,768]{2,1,0:T(8,128)(2,1)S(1)}, u32[]{:S(2)}, u32[]{:S(2)}) collective-permute-start(bf16[3,128,768]{2,1,0:T(8,128)(2,1)S(1)} %get-tuple-element.29), channel_id=1, source_target_pairs={{0,4},{1,5},{2,6},{3,7},{4,0},{5,1},{6,2},{7,3},{8,12},{9,13},{10,... | collective-permute-start | bytes 1769480 | tf_op jit(solution)/shard_map/ppermute | solution.py:24
  5.1 16.3 %collective-permute-start.1 = (bf16[3,128,768]{2,1,0:T(8,128)(2,1)S(1)}, bf16[3,128,768]{2,1,0:T(8,128)(2,1)S(1)}, u32[]{:S(2)}, u32[]{:S(2)}) collective-permute-start(bf16[3,128,768]{2,1,0:T(8,128)(2,1)S(1)} %get-tuple-element.27), channel_id=1, source_target_pairs={{0,2},{1,3},{2,0},{3,1},{4,6},{5,7},{6,4},{7,5},{8,10},{9,11},{10,... | collective-permute-start | bytes 1769480 | tf_op jit(solution)/shard_map/ppermute | solution.py:24
  8.1 18.8 %collective-permute-start.9 = (bf16[2,128,768]{2,1,0:T(8,128)(2,1)S(1)}, bf16[2,128,768]{2,1,0:T(8,128)(2,1)S(1)}, u32[]{:S(2)}, u32[]{:S(2)}) collective-permute-start(bf16[2,128,768]{2,1,0:T(8,128)(2,1)S(1)} %get-tuple-element.33), channel_id=1, source_target_pairs={{0,4},{1,5},{2,6},{3,7},{4,0},{5,1},{6,2},{7,3},{8,12},{9,13},{10,... | collective-permute-start | bytes 1179656 | tf_op jit(solution)/shard_map/ppermute | solution.py:24
  8.7 21.1 %collective-permute-start.7 = (bf16[2,128,768]{2,1,0:T(8,128)(2,1)S(1)}, bf16[2,128,768]{2,1,0:T(8,128)(2,1)S(1)}, u32[]{:S(2)}, u32[]{:S(2)}) collective-permute-start(bf16[2,128,768]{2,1,0:T(8,128)(2,1)S(1)} %get-tuple-element.30), channel_id=1, source_target_pairs={{0,2},{1,3},{2,0},{3,1},{4,6},{5,7},{6,4},{7,5},{8,10},{9,11},{10,... | collective-permute-start | bytes 1179656 | tf_op jit(solution)/shard_map/ppermute | solution.py:24
  19.3 2.7 %collective-permute-start.6 = (bf16[3,128,384]{2,1,0:T(8,128)(2,1)S(1)}, bf16[3,128,384]{2,1,0:T(8,128)(2,1)S(1)}, u32[]{:S(2)}, u32[]{:S(2)}) collective-permute-start(bf16[3,128,384]{2,1,0:T(8,128)(2,1)S(1)} %shard_map.91), channel_id=1, source_target_pairs={{0,1},{1,0},{2,3},{3,2},{4,5},{5,4},{6,7},{7,6},{8,9},{9,8},{10,11... | collective-permute-start | bytes 884744 | tf_op jit(solution)/shard_map/ppermute | solution.py:24
  21.4 5.5 %collective-permute-start.2 = (bf16[3,128,384]{2,1,0:T(8,128)(2,1)S(1)}, bf16[3,128,384]{2,1,0:T(8,128)(2,1)S(1)}, u32[]{:S(2)}, u32[]{:S(2)}) collective-permute-start(bf16[3,128,384]{2,1,0:T(8,128)(2,1)S(1)} %shard_map.89), channel_id=1, source_target_pairs={{0,1},{1,0},{2,3},{3,2},{4,5},{5,4},{6,7},{7,6},{8,9},{9,8},{10,11... | collective-permute-start | bytes 884744 | tf_op jit(solution)/shard_map/ppermute | solution.py:24
  21.4 8.4 %collective-permute-start = (bf16[3,128,384]{2,1,0:T(8,128)(2,1)S(1)}, bf16[3,128,384]{2,1,0:T(8,128)(2,1)S(1)}, u32[]{:S(2)}, u32[]{:S(2)}) collective-permute-start(bf16[3,128,384]{2,1,0:T(8,128)(2,1)S(1)} %get-tuple-element.26), channel_id=1, source_target_pairs={{0,1},{1,0},{2,3},{3,2},{4,5},{5,4},{6,7},{7,6},{8,9},{9,8},{10,11... | collective-permute-start | bytes 884744 | tf_op jit(solution)/shard_map/ppermute | solution.py:24
  22.0 14.7 %collective-permute-start.14 = (bf16[2,256,384]{2,1,0:T(8,128)(2,1)S(1)}, bf16[2,256,384]{2,1,0:T(8,128)(2,1)S(1)}, u32[]{:S(2)}, u32[]{:S(2)}) collective-permute-start(bf16[2,256,384]{2,1,0:T(8,128)(2,1)S(1)} %shard_map.97), channel_id=1, source_target_pairs={{0,2},{1,3},{2,0},{3,1},{4,6},{5,7},{6,4},{7,5},{8,10},{9,11},{10,... | collective-permute-start | bytes 1179656 | tf_op jit(solution)/shard_map/ppermute | solution.py:24
  26.8 5.5 %collective-permute-start.4 = (bf16[3,128,384]{2,1,0:T(8,128)(2,1)S(1)}, bf16[3,128,384]{2,1,0:T(8,128)(2,1)S(1)}, u32[]{:S(2)}, u32[]{:S(2)}) collective-permute-start(bf16[3,128,384]{2,1,0:T(8,128)(2,1)S(1)} %get-tuple-element.28), channel_id=1, source_target_pairs={{0,1},{1,0},{2,3},{3,2},{4,5},{5,4},{6,7},{7,6},{8,9},{9,8},{10,11... | collective-permute-start | bytes 884744 | tf_op jit(solution)/shard_map/ppermute | solution.py:24
  26.8 3.7 %copy-start.2 = (bf16[1,8,16,3072]{3,2,1,0:T(8,128)(2,1)S(1)}, bf16[1,8,16,3072]{3,2,1,0:T(8,128)(2,1)}, u32[]{:S(2)}) copy-start(bf16[1,8,16,3072]{3,2,1,0:T(8,128)(2,1)} %param.10) | copy-start | bytes 2359300
  26.9 3.6 %copy-start = (bf16[1,8,16,3072]{3,2,1,0:T(8,128)(2,1)S(1)}, bf16[1,8,16,3072]{3,2,1,0:T(8,128)(2,1)}, u32[]{:S(2)}) copy-start(bf16[1,8,16,3072]{3,2,1,0:T(8,128)(2,1)} %param.8) | copy-start | bytes 2359300
  26.9 3.6 %copy-start.1 = (bf16[1,8,16,3072]{3,2,1,0:T(8,128)(2,1)S(1)}, bf16[1,8,16,3072]{3,2,1,0:T(8,128)(2,1)}, u32[]{:S(2)}) copy-start(bf16[1,8,16,3072]{3,2,1,0:T(8,128)(2,1)} %param.9) | copy-start | bytes 2359300
  26.9 3.6 %collective-permute-start.10 = (bf16[2,128,384]{2,1,0:T(8,128)(2,1)S(1)}, bf16[2,128,384]{2,1,0:T(8,128)(2,1)S(1)}, u32[]{:S(2)}, u32[]{:S(2)}) collective-permute-start(bf16[2,128,384]{2,1,0:T(8,128)(2,1)S(1)} %shard_map.94), channel_id=1, source_target_pairs={{0,1},{1,0},{2,3},{3,2},{4,5},{5,4},{6,7},{7,6},{8,9},{9,8},{10,11... | collective-permute-start | bytes 589832 | tf_op jit(solution)/shard_map/ppermute | solution.py:24
  27.5 2.4 %copy-start.5 = (s32[4]{0:T(128)S(1)}, s32[4]{0:T(128)}, u32[]{:S(2)}) copy-start(s32[4]{0:T(128)} %timesteps_ref.1) | copy-start | bytes 52
  29.8 9.8 %collective-permute-start.3 = (bf16[2,256,384]{2,1,0:T(8,128)(2,1)S(1)}, bf16[2,256,384]{2,1,0:T(8,128)(2,1)S(1)}, u32[]{:S(2)}, u32[]{:S(2)}) collective-permute-start(bf16[2,256,384]{2,1,0:T(8,128)(2,1)S(1)} %shard_map.90), channel_id=1, source_target_pairs={{0,4},{1,5},{2,6},{3,7},{4,0},{5,1},{6,2},{7,3},{8,12},{9,13},{10,... | collective-permute-start | bytes 1179656 | tf_op jit(solution)/shard_map/ppermute | solution.py:24
  29.8 2.5 %collective-permute-start.8 = (bf16[2,128,384]{2,1,0:T(8,128)(2,1)S(1)}, bf16[2,128,384]{2,1,0:T(8,128)(2,1)S(1)}, u32[]{:S(2)}, u32[]{:S(2)}) collective-permute-start(bf16[2,128,384]{2,1,0:T(8,128)(2,1)S(1)} %shard_map.92), channel_id=1, source_target_pairs={{0,1},{1,0},{2,3},{3,2},{4,5},{5,4},{6,7},{7,6},{8,9},{9,8},{10,11... | collective-permute-start | bytes 589832 | tf_op jit(solution)/shard_map/ppermute | solution.py:24
  37.6 4.7 %collective-permute-start.15 = (bf16[128,384]{1,0:T(8,128)(2,1)S(1)}, bf16[128,384]{1,0:T(8,128)(2,1)S(1)}, u32[]{:S(2)}, u32[]{:S(2)}) collective-permute-start(bf16[128,384]{1,0:T(8,128)(2,1)S(1)} %get-tuple-element.45), channel_id=1, source_target_pairs={{0,1},{1,0},{2,3},{3,2},{4,5},{5,4},{6,7},{7,6},{8,9},{9,8},{10,11... | collective-permute-start | bytes 294920 | tf_op jit(solution)/shard_map/ppermute | solution.py:24
  37.7 5.7 %collective-permute-start.16 = (bf16[128,384]{1,0:T(8,128)(2,1)S(1)}, bf16[128,384]{1,0:T(8,128)(2,1)S(1)}, u32[]{:S(2)}, u32[]{:S(2)}) collective-permute-start(bf16[128,384]{1,0:T(8,128)(2,1)S(1)} %get-tuple-element.46), channel_id=1, source_target_pairs={{0,4},{1,5},{2,6},{3,7},{4,0},{5,1},{6,2},{7,3},{8,12},{9,13},{10,... | collective-permute-start | bytes 294920 | tf_op jit(solution)/shard_map/ppermute | solution.py:24
  38.1 6.4 %collective-permute-start.17 = (bf16[128,384]{1,0:T(8,128)(2,1)S(1)}, bf16[128,384]{1,0:T(8,128)(2,1)S(1)}, u32[]{:S(2)}, u32[]{:S(2)}) collective-permute-start(bf16[128,384]{1,0:T(8,128)(2,1)S(1)} %get-tuple-element.47), channel_id=1, source_target_pairs={{0,5},{1,4},{2,7},{3,6},{4,1},{5,0},{6,3},{7,2},{8,13},{9,12},{10,... | collective-permute-start | bytes 294920 | tf_op jit(solution)/shard_map/ppermute | solution.py:24
  39.6 2.9 %copy-start.3 = (bf16[1,8,16,3072]{3,2,1,0:T(8,128)(2,1)S(1)}, bf16[1,8,16,3072]{3,2,1,0:T(8,128)(2,1)}, u32[]{:S(2)}) copy-start(bf16[1,8,16,3072]{3,2,1,0:T(8,128)(2,1)} %param.7) | copy-start | bytes 2359300
  40.5 5.5 %collective-permute-start.11 = (bf16[128,384]{1,0:T(8,128)(2,1)S(1)}, bf16[128,384]{1,0:T(8,128)(2,1)S(1)}, u32[]{:S(2)}, u32[]{:S(2)}) collective-permute-start(bf16[128,384]{1,0:T(8,128)(2,1)S(1)} %get-tuple-element.38), channel_id=1, source_target_pairs={{0,1},{1,0},{2,3},{3,2},{4,5},{5,4},{6,7},{7,6},{8,9},{9,8},{10,11... | collective-permute-start | bytes 294920 | tf_op jit(solution)/shard_map/ppermute | solution.py:24
  40.9 5.3 %collective-permute-start.12 = (bf16[128,384]{1,0:T(8,128)(2,1)S(1)}, bf16[128,384]{1,0:T(8,128)(2,1)S(1)}, u32[]{:S(2)}, u32[]{:S(2)}) collective-permute-start(bf16[128,384]{1,0:T(8,128)(2,1)S(1)} %get-tuple-element.39), channel_id=1, source_target_pairs={{0,2},{1,3},{2,0},{3,1},{4,6},{5,7},{6,4},{7,5},{8,10},{9,11},{10,... | collective-permute-start | bytes 294920 | tf_op jit(solution)/shard_map/ppermute | solution.py:24
  42.4 5.1 %collective-permute-start.13 = (bf16[128,384]{1,0:T(8,128)(2,1)S(1)}, bf16[128,384]{1,0:T(8,128)(2,1)S(1)}, u32[]{:S(2)}, u32[]{:S(2)}) collective-permute-start(bf16[128,384]{1,0:T(8,128)(2,1)S(1)} %get-tuple-element.40), channel_id=1, source_target_pairs={{0,3},{1,2},{2,1},{3,0},{4,7},{5,6},{6,5},{7,4},{8,11},{9,10},{10,... | collective-permute-start | bytes 294920 | tf_op jit(solution)/shard_map/ppermute | solution.py:24
  44.7 7.2 %collective-permute-start.19 = (bf16[32,1536]{1,0:T(8,128)(2,1)S(1)}, bf16[32,1536]{1,0:T(8,128)(2,1)S(1)}, u32[]{:S(2)}, u32[]{:S(2)}) collective-permute-start(bf16[32,1536]{1,0:T(8,128)(2,1)S(1)} %shard_map.101), channel_id=1, source_target_pairs={{8,0},{16,8},{24,16},{9,1},{17,9},{25,17},{10,2},{18,10},{26,18},{... | collective-permute-start | bytes 294920 | tf_op jit(solution)/shard_map/ppermute | solution.py:20
  47.6 6.8 %collective-permute-start.18 = (bf16[32,1536]{1,0:T(8,128)(2,1)S(1)}, bf16[32,1536]{1,0:T(8,128)(2,1)S(1)}, u32[]{:S(2)}, u32[]{:S(2)}) collective-permute-start(bf16[32,1536]{1,0:T(8,128)(2,1)S(1)} %shard_map.100), channel_id=1, source_target_pairs={{8,0},{16,8},{24,16},{9,1},{17,9},{25,17},{10,2},{18,10},{26,18},{... | collective-permute-start | bytes 294920 | tf_op jit(solution)/shard_map/ppermute | solution.py:20
  49.5 4.9 %copy-start.4 = (bf16[2,16,3072]{2,1,0:T(8,128)(2,1)S(1)}, bf16[2,16,3072]{2,1,0:T(8,128)(2,1)}, u32[]{:S(2)}) copy-start(bf16[2,16,3072]{2,1,0:T(8,128)(2,1)} %fresh_ref.1) | copy-start | bytes 589828

commit v5 on v4

--- a/solution.py
+++ b/solution.py
@@ -338,17 +338,31 @@
         scores = following
 
 
-def complete(side, queries, core, got, far_core, far_got, old):
+def complete_both_kernel(sides, queries_ref, *refs):
+    count = 7
+    inputs, outs = refs[: count * len(sides)], refs[count * len(sides) :]
+    core_ref, outs = outs[0], outs[1:]
+    rows = queries_ref.shape[0]
+    for index, side in enumerate(sides):
+        own, *backs = outs[3 * index : 3 * index + 3]
+        core = core_ref.at[index * rows : (index + 1) * rows]
+        parts = inputs[count * index : count * (index + 1)]
+        complete_kernel(side, queries_ref, *parts, own, core, *backs)
+
+
+def complete(sides, queries, received):
     rows, width = queries.shape
     size = width // 8
     out = jax.ShapeDtypeStruct((rows, size), jnp.bfloat16)
-    return call(
-        functools.partial(complete_kernel, side),
-        (out,) * 4,
-        [VMEM] * 8,
-        (VMEM,) * 4,
-        cost=(32 * rows * rows * size, 64 * rows * size, 8 * rows * rows * size // HEAD_SIZE),
-    )(queries, core, got, far_core, far_got, *old)
+    core = jax.ShapeDtypeStruct((len(sides) * rows, size), jnp.bfloat16)
+    outs = call(
+        functools.partial(complete_both_kernel, sides),
+        (core,) + (out,) * (3 * len(sides)),
+        [VMEM] * (1 + 7 * len(sides)),
+        (VMEM,) * (1 + 3 * len(sides)),
+        cost=(64 * rows * rows * size, 128 * rows * size, 16 * rows * rows * size // HEAD_SIZE),
+    )(queries, *[part for parts in received for part in parts])
+    return outs[0], [outs[3 * index + 1 : 3 * index + 4] for index in range(len(sides))]
 
 
 def moved(latents, attended, delta):
@@ -379,11 +393,37 @@
     )(delta, latents, *pieces)
 
 
-def finish_kernel(places, offset_ref, delta_ref, latents_ref, *refs):
+def arrive(places, offset, part_ref, advanced_ref, sems):
+    frames, rows, width = advanced_ref.shape
+    size = width // 8
+    copies = []
+    for index, place in enumerate(places):
+        for frame in range(MAX_SHIFT):
+            source = part_ref.at[
+                frame * rows : (frame + 1) * rows, index * size : (index + 1) * size
+            ]
+            target = advanced_ref.at[
+                jnp.minimum(frames - offset + frame, frames - 1), :, columns(*place, width)
+            ]
+            copy = pltpu.make_async_copy(source, target, sems.at[index, frame])
+            copies.append((frame < offset, copy))
+    return copies
+
+
+def newest():
+    return lax.axis_index("queue") == lax.axis_size("queue") - 1
+
+
+def finish_kernel(places, early, offset_ref, delta_ref, latents_ref, lead_ref, *refs):
     pieces = refs[: len(places)]
-    attended_ref, advanced_ref, whole_ref, updated_ref, out_sem, move_sem = refs[len(places) :]
+    attended_ref, advanced_ref, whole_ref, updated_ref, out_sem, move_sem, lead_sem = refs[
+        len(places) :
+    ]
     offset, delta = offset_ref[0], delta_ref[:, :1]
     frames, rows, width = attended_ref.shape
+    coming = arrive(early, offset, lead_ref, advanced_ref, lead_sem)
+    for due, copy in coming:
+        pl.when(jnp.logical_and(due, jnp.logical_not(newest())))(copy.start)
     out_copies, move_copies = [], []
     for frame in range(frames):
         span = slice(frame * rows, (frame + 1) * rows)
@@ -414,60 +454,48 @@
             pl.when(frame >= offset)(copy.wait)
         else:
             copy.wait()
-
-
-def finish(shape, places, offsets, delta, latents, pieces):
+    for due, copy in coming:
+        pl.when(jnp.logical_and(due, jnp.logical_not(newest())))(copy.wait)
+
+
+def finish(shape, places, early, offsets, delta, latents, lead_part, pieces):
     out = jax.ShapeDtypeStruct(shape, jnp.bfloat16)
     return call(
-        functools.partial(finish_kernel, places),
+        functools.partial(finish_kernel, places, early),
         (out, out),
-        [SMEM] + [VMEM] * (2 + len(pieces)),
+        [SMEM] + [VMEM] * (3 + len(pieces)),
         (HBM, HBM),
         [
             pltpu.VMEM(shape, jnp.bfloat16),
             pltpu.VMEM(shape, jnp.bfloat16),
             pltpu.SemaphoreType.DMA((shape[0],)),
             pltpu.SemaphoreType.DMA((shape[0],)),
+            pltpu.SemaphoreType.DMA((len(early), MAX_SHIFT)),
         ],
         (2 * latents.size, 8 * latents.size, 0),
-    )(offsets, delta, latents, *pieces)
+    )(offsets, delta, latents, lead_part, *pieces)
 
 
 def fill_kernel(groups, offset_ref, fresh_ref, *refs):
-    leads = refs[: len(groups)]
-    _, advanced_ref, coming_ref, sem = refs[len(groups) :]
+    leads, refs = refs[: len(groups)], refs[len(groups) :]
+    _, advanced_ref, sems, fresh_sem = refs
     offset = offset_ref[0]
-    frames, rows, width = advanced_ref.shape
-    newest = lax.axis_index("queue") == lax.axis_size("queue") - 1
-
-    @pl.when(newest)
-    def _():
-        coming_ref[...] = fresh_ref[...]
-
-    @pl.when(jnp.logical_not(newest))
-    def _():
-        for places, part in zip(groups, leads):
-            at = 0
-            size = part.shape[1] // len(places)
-            for place in places:
-                cols = columns(*place, width)
-                for frame in range(MAX_SHIFT):
-                    span = slice(frame * rows, (frame + 1) * rows)
-                    coming_ref[frame, :, cols] = part[span, at : at + size]
-                at += size
-
-    copies = [
-        pltpu.make_async_copy(
-            coming_ref.at[frame],
+    frames = advanced_ref.shape[0]
+    copies = []
+    for index, (places, part) in enumerate(zip(groups, leads)):
+        for due, copy in arrive(places, offset, part, advanced_ref, sems.at[index]):
+            copies.append((jnp.logical_and(due, jnp.logical_not(newest())), copy))
+    for frame in range(MAX_SHIFT):
+        copy = pltpu.make_async_copy(
+            fresh_ref.at[frame],
             advanced_ref.at[jnp.minimum(frames - offset + frame, frames - 1)],
-            sem.at[frame],
+            fresh_sem.at[frame],
         )
-        for frame in range(MAX_SHIFT)
-    ]
-    for frame, copy in enumerate(copies):
-        pl.when(frame < offset)(copy.start)
-    for frame, copy in enumerate(copies):
-        pl.when(frame < offset)(copy.wait)
+        copies.append((jnp.logical_and(frame < offset, newest()), copy))
+    for due, copy in copies:
+        pl.when(due)(copy.start)
+    for due, copy in copies:
+        pl.when(due)(copy.wait)
 
 
 def fill(groups, offsets, fresh, leads, advanced):
@@ -476,7 +504,10 @@
         jax.ShapeDtypeStruct(advanced.shape, advanced.dtype),
         [SMEM] + [VMEM] * (1 + len(leads)) + [HBM],
         HBM,
-        [pltpu.VMEM(fresh.shape, jnp.bfloat16), pltpu.SemaphoreType.DMA((MAX_SHIFT,))],
+        [
+            pltpu.SemaphoreType.DMA((len(groups), len(groups[0]), MAX_SHIFT)),
+            pltpu.SemaphoreType.DMA((MAX_SHIFT,)),
+        ],
         (0, 6 * fresh.size, 0),
         input_output_aliases={2 + len(leads): 0},
     )(offsets, fresh, *leads, advanced)
@@ -499,38 +530,51 @@
         arrays,
     )
     owns, cores = owns[: len(sides)], owns[len(sides) :]
-    gots = [swapped(send, side[0]) for side, send in zip(sides, sends)]
+    gots = [swapped(send, side[0]) for send, side in zip(sends, sides)]
+    cores = [swapped(core, CORE) for core in cores]
+    got_cores = [swapped(split(got), CORE) for got in gots]
     fars = [swapped(own, side[1]) for side, own in zip(sides, owns)]
-    cores = [swapped(core, CORE) for core in cores]
     far_cores = [swapped(split(far), CORE) for far in fars]
-    got_cores = [swapped(split(got), CORE) for got in gots]
     far_gots = [
         swapped(join(got, core), side[1]) for side, got, core in zip(sides, gots, got_cores)
     ]
-    received = list(zip(cores, gots, got_cores, fars, far_cores))
+    received = zip(cores, gots, got_cores, fars, far_cores)
     states = [attend(side, *arrays, *parts) for side, parts in zip(sides, received)]
     delta = step_size(timesteps)
     first_latents = latents[:first_rows]
     far_gots = [after(far, states[1 - index][0], delta) for index, far in enumerate(far_gots)]
-    pieces, places, groups, leads = [], [], [], []
-    for index, side in enumerate(sides):
-        own, *backs = complete(
-            side,
-            queries,
-            cores[index],
-            gots[index],
-            got_cores[index],
-            far_gots[index],
-            states[index],
-        )
-        groups.append([(side, mask) for mask in (0, *peers(side))])
-        parts = [own] + [swapped(back, mask) for back, mask in zip(backs, peers(side))]
-        head = lead(groups[-1], delta, first_latents, parts)
-        leads.append(shifted(head, "queue", -1))
-        pieces += parts
-        places += groups[-1]
-    attended, advanced = finish(shape, places, offsets, delta, latents, pieces)
-    advanced = fill(groups, offsets, fresh_frames, leads, advanced)
+    core_out, results = complete(
+        sides,
+        queries,
+        [
+            (cores[index], gots[index], got_cores[index], far_gots[index], *states[index])
+            for index in range(len(sides))
+        ],
+    )
+    core_back = swapped(core_out, CORE)
+    near_places, near_pieces, far_places, far_pieces = [], [], [], []
+    for index, (side, (own, *backs)) in enumerate(zip(sides, results)):
+        near_places += [(side, 0), (side, CORE)]
+        near_pieces += [own, core_back[index * rows : (index + 1) * rows]]
+        far_places += [(side, mask) for mask in peers(side)[1:]]
+        far_pieces += [swapped(back, mask) for back, mask in zip(backs, peers(side)[1:])]
+    early = shifted(lead(near_places, delta, first_latents, near_pieces), "queue", -1)
+    groups = [far_places[:2], far_places[2:]]
+    late = [
+        shifted(lead(group, delta, first_latents, far_pieces[at : at + 2]), "queue", -1)
+        for group, at in zip(groups, (0, 2))
+    ]
+    attended, advanced = finish(
+        shape,
+        near_places + far_places,
+        near_places,
+        offsets,
+        delta,
+        latents,
+        early,
+        near_pieces + far_pieces,
+    )
+    advanced = fill(groups, offsets, fresh_frames, late, advanced)
     return (attended[None], advanced[None])
 
 

time: 55.4 us -> 54.6 us (0.986)
  waiting for transfers between devices: 27.7 us -> 25 us
  starting transfers between devices: 14.5 us -> 16.6 us
    ppermute x18 -> x17, waiting for transfers between devices: 24.2 us -> 21.7 us  [swapped(): lax.ppermute(block, 'seq', [(i, i ^ bit) for i in range(lax.axis_size('se...]
    ppermute x2 -> x3, starting transfers between devices: 2.58 us -> 3.88 us  [shifted(): return lax.ppermute(block, axis, route)]
    ppermute x18 -> x17, starting transfers between devices: 12 us -> 12.7 us  [swapped(): lax.ppermute(block, 'seq', [(i, i ^ bit) for i in range(lax.axis_size('se...]
    ppermute x2 -> x3, waiting for transfers between devices: 3.53 us -> 3.22 us  [shifted(): return lax.ppermute(block, axis, route)]
    pallas_call x3 -> x2, Pallas kernels: 3.12 us -> 3.03 us  [the longest x1 1.63 us: complete(): call(functools.partial(complete_both_kernel, sides), (core,) + (out,) * (...]
  transfers between devices with their start and end apart: 20 -> 20, of which waited for: 11 -> 12; matrix products, arithmetic and copies ran while one was open for 0% -> 0% of each run, Pallas kernels for 17% -> 14%
where the time goes in v5:
time: 54.6 us; the launch traced here: 54.3 us
  waiting for transfers between devices  25 us (46%)
  starting transfers between devices  16.6 us (30%)
  Pallas kernels  11.2 us (21%)
  between operations  1.5 us (3%)
    ppermute x17, waiting for transfers between devices, swapped(): lax.ppermute(block, 'seq', [(i, i ^ bit) for i in range(lax.axis_size('se...  21.7 us
    ppermute x17, starting transfers between devices, swapped(): lax.ppermute(block, 'seq', [(i, i ^ bit) for i in range(lax.axis_size('se...  12.7 us
    ppermute x3, starting transfers between devices, shifted(): return lax.ppermute(block, axis, route)  3.88 us
    pallas_call x2, Pallas kernels, attend(): call(functools.partial(attend_kernel, side), (out,) * 3, [VMEM] * 8, (VME...  3.6 us
    ppermute x3, waiting for transfers between devices, shifted(): return lax.ppermute(block, axis, route)  3.22 us
    pallas_call x2, Pallas kernels, pack(): call(functools.partial(pack_kernel, cuts), outs, [HBM] * 3, (VMEM,) * len...  2.92 us
    pallas_call x1, Pallas kernels, complete(): call(functools.partial(complete_both_kernel, sides), (core,) + (out,) * (...  1.63 us
    pallas_call x1, Pallas kernels, finish(): call(functools.partial(finish_kernel, places, early), (out, out), [SMEM]...  1.4 us
  transfers between devices with their start and end apart: 20, of which 12 were waited for; matrix products, arithmetic and copies ran while one was open for 0% of the time, Pallas kernels for 14%

profile of v5, /device:TPU:0, one launch (start us, length us, event | category | flops | bytes accessed | tf_op | source)
XLA Modules:
  0.0 54.3 jit_solution(12780573461626382282)
XLA Ops:
  0.6 1.4 %shard_map.88 = (bf16[3,128,768]{2,1,0:T(8,128)(2,1)S(1)}, bf16[3,128,768]{2,1,0:T(8,128)(2,1)S(1)}) custom-call(bf16[128,3072]{1,0:T(8,128)(2,1)} %bitcast.12, bf16[128,3072]{1,0:T(8,128)(2,1)} %bitcast.16, bf16[128,3072]{1,0:T(8,128)(2,1)} %bitcast.7), custom_call_target="tpu_custom_call" | custom-call | bytes 2359296 | tf_op jit(solution)/shard_map/pallas_call | solution.py:185
  2.1 3.0 %collective-permute-start.5 = (bf16[3,128,768]{2,1,0:T(8,128)(2,1)S(1)}, bf16[3,128,768]{2,1,0:T(8,128)(2,1)S(1)}, u32[]{:S(2)}, u32[]{:S(2)}) collective-permute-start(bf16[3,128,768]{2,1,0:T(8,128)(2,1)S(1)} %get-tuple-element.28), channel_id=1, source_target_pairs={{0,4},{1,5},{2,6},{3,7},{4,0},{5,1},{6,2},{7,3},{8,12},{9,13},{10,... | collective-permute-start | bytes 1769480 | tf_op jit(solution)/shard_map/ppermute | solution.py:24
  5.1 1.5 %collective-permute-start.1 = (bf16[3,128,768]{2,1,0:T(8,128)(2,1)S(1)}, bf16[3,128,768]{2,1,0:T(8,128)(2,1)S(1)}, u32[]{:S(2)}, u32[]{:S(2)}) collective-permute-start(bf16[3,128,768]{2,1,0:T(8,128)(2,1)S(1)} %get-tuple-element.26), channel_id=1, source_target_pairs={{0,2},{1,3},{2,0},{3,1},{4,6},{5,7},{6,4},{7,5},{8,10},{9,11},{10,... | collective-permute-start | bytes 1769480 | tf_op jit(solution)/shard_map/ppermute | solution.py:24
  6.6 1.5 %shard_map.87 = (bf16[2,128,768]{2,1,0:T(8,128)(2,1)S(1)}, bf16[2,128,768]{2,1,0:T(8,128)(2,1)S(1)}, bf16[3,128,384]{2,1,0:T(8,128)(2,1)S(1)}, bf16[3,128,384]{2,1,0:T(8,128)(2,1)S(1)}) custom-call(bf16[128,3072]{1,0:T(8,128)(2,1)} %bitcast.13, bf16[128,3072]{1,0:T(8,128)(2,1)} %bitcast.17, bf16[128,3072]{1,0:T(8,128)(2,1)} %bitcast.8), custom_call_target="tpu_custom_call" | custom-call | bytes 2752512 | tf_op jit(solution)/shard_map/pallas_call | solution.py:185
  8.1 0.6 %collective-permute-start.9 = (bf16[2,128,768]{2,1,0:T(8,128)(2,1)S(1)}, bf16[2,128,768]{2,1,0:T(8,128)(2,1)S(1)}, u32[]{:S(2)}, u32[]{:S(2)}) collective-permute-start(bf16[2,128,768]{2,1,0:T(8,128)(2,1)S(1)} %get-tuple-element.32), channel_id=1, source_target_pairs={{0,4},{1,5},{2,6},{3,7},{4,0},{5,1},{6,2},{7,3},{8,12},{9,13},{10,... | collective-permute-start | bytes 1179656 | tf_op jit(solution)/shard_map/ppermute | solution.py:24
  8.8 10.5 %collective-permute-done.5.got_ref.refs_8_ = bf16[3,128,768]{2,1,0:T(8,128)(2,1)S(1)} collective-permute-done((bf16[3,128,768]{2,1,0:T(8,128)(2,1)S(1)}, bf16[3,128,768]{2,1,0:T(8,128)(2,1)S(1)}, u32[]{:S(2)}, u32[]{:S(2)}) %collective-permute-start.5) | collective-permute-done | bytes 589856 | tf_op jit(solution)/shard_map/ppermute | solution.py:24
  19.4 2.0 %collective-permute-done.1.got_ref.refs_1_ = bf16[3,128,768]{2,1,0:T(8,128)(2,1)S(1)} collective-permute-done((bf16[3,128,768]{2,1,0:T(8,128)(2,1)S(1)}, bf16[3,128,768]{2,1,0:T(8,128)(2,1)S(1)}, u32[]{:S(2)}, u32[]{:S(2)}) %collective-permute-start.1) | collective-permute-done | bytes 589856 | tf_op jit(solution)/shard_map/ppermute | solution.py:24
  21.4 0.5 collective-permute-start
  22.0 1.6 %collective-permute-start.11 = (bf16[2,256,384]{2,1,0:T(8,128)(2,1)S(1)}, bf16[2,256,384]{2,1,0:T(8,128)(2,1)S(1)}, u32[]{:S(2)}, u32[]{:S(2)}) collective-permute-start(bf16[2,256,384]{2,1,0:T(8,128)(2,1)S(1)} %shard_map.96), channel_id=1, source_target_pairs={{0,2},{1,3},{2,0},{3,1},{4,6},{5,7},{6,4},{7,5},{8,10},{9,11},{10,... | collective-permute-start | bytes 1179656 | tf_op jit(solution)/shard_map/ppermute | solution.py:24
  23.6 1.1 %collective-permute-start.3 = (bf16[2,256,384]{2,1,0:T(8,128)(2,1)S(1)}, bf16[2,256,384]{2,1,0:T(8,128)(2,1)S(1)}, u32[]{:S(2)}, u32[]{:S(2)}) collective-permute-start(bf16[2,256,384]{2,1,0:T(8,128)(2,1)S(1)} %shard_map.90), channel_id=1, source_target_pairs={{0,4},{1,5},{2,6},{3,7},{4,0},{5,1},{6,2},{7,3},{8,12},{9,13},{10,... | collective-permute-start | bytes 1179656 | tf_op jit(solution)/shard_map/ppermute | solution.py:24
  24.7 2.8 %collective-permute-done.9.got_ref.far_ref = bf16[2,128,768]{2,1,0:T(8,128)(2,1)S(1)} collective-permute-done((bf16[2,128,768]{2,1,0:T(8,128)(2,1)S(1)}, bf16[2,128,768]{2,1,0:T(8,128)(2,1)S(1)}, u32[]{:S(2)}, u32[]{:S(2)}) %collective-permute-start.9) | collective-permute-done | bytes 393248 | tf_op jit(solution)/shard_map/ppermute | solution.py:24
  27.6 2.2 %collective-permute-done.7.got_ref.far_ref = bf16[2,128,768]{2,1,0:T(8,128)(2,1)S(1)} collective-permute-done((bf16[2,128,768]{2,1,0:T(8,128)(2,1)S(1)}, bf16[2,128,768]{2,1,0:T(8,128)(2,1)S(1)}, u32[]{:S(2)}, u32[]{:S(2)}) %collective-permute-start.7) | collective-permute-done | bytes 393248 | tf_op jit(solution)/shard_map/ppermute | solution.py:24
  29.8 0.6 %collective-permute-start.8 = (bf16[2,128,384]{2,1,0:T(8,128)(2,1)S(1)}, bf16[2,128,384]{2,1,0:T(8,128)(2,1)S(1)}, u32[]{:S(2)}, u32[]{:S(2)}) collective-permute-start(bf16[2,128,384]{2,1,0:T(8,128)(2,1)S(1)} %shard_map.92), channel_id=1, source_target_pairs={{0,1},{1,0},{2,3},{3,2},{4,5},{5,4},{6,7},{7,6},{8,9},{9,8},{10,11... | collective-permute-start | bytes 589832 | tf_op jit(solution)/shard_map/ppermute | solution.py:24
  30.4 0.6 %shard_map.86.delta_ref = f32[1,128]{1,0:T(1,128)S(1)} custom-call(s32[4]{0:T(128)S(1)} %copy-done.5), custom_call_target="tpu_custom_call" | custom-call | tf_op jit(solution)/shard_map/pallas_call | solution.py:160
  30.9 0.3 collective-permute-done.10.far_core_ref
  31.2 1.8 %shard_map.95 = (f32[512,384]{1,0:T(8,128)S(1)}, f32[512,384]{1,0:T(8,128)S(1)}, f32[512,384]{1,0:T(8,128)S(1)}) custom-call(bf16[128,3072]{1,0:T(8,128)(2,1)S(1)} %bitcast.14, bf16[128,3072]{1,0:T(8,128)(2,1)S(1)} %bitcast.18, bf16[128,3072]{1,0:T(8,128)(2,1)S(1)} %bitcast.9, bf16[3,128,384]{2,1,0:T(8,128)(2,1)S(1)} %collective-permute-done.core_ref.refs_0_, ...), custom_call_target="tpu_custom_call" | custom-call | flops 603979776 | bytes 3145728 | tf_op jit(solution)/shard_map/pallas_call | solution.py:303
  33.0 1.8 %shard_map.93 = (f32[512,384]{1,0:T(8,128)S(1)}, f32[512,384]{1,0:T(8,128)S(1)}, f32[512,384]{1,0:T(8,128)S(1)}) custom-call(bf16[128,3072]{1,0:T(8,128)(2,1)S(1)} %bitcast.15, bf16[128,3072]{1,0:T(8,128)(2,1)S(1)} %bitcast.19, bf16[128,3072]{1,0:T(8,128)(2,1)S(1)} %bitcast.10, bf16[3,128,384]{2,1,0:T(8,128)(2,1)S(1)} %collective-permute-done.4.core_ref.refs_7_, ...), custom_call_target="tpu_custom_call" | custom-call | flops 603979776 | bytes 3145728 | tf_op jit(solution)/shard_map/pallas_call | solution.py:303
  34.8 1.9 %collective-permute-done.11.refs_10_ = bf16[2,256,384]{2,1,0:T(8,128)(2,1)S(1)} collective-permute-done((bf16[2,256,384]{2,1,0:T(8,128)(2,1)S(1)}, bf16[2,256,384]{2,1,0:T(8,128)(2,1)S(1)}, u32[]{:S(2)}, u32[]{:S(2)}) %collective-permute-start.11) | collective-permute-done | bytes 393248 | tf_op jit(solution)/shard_map/ppermute | solution.py:24
  36.7 1.6 %shard_map.97 = (bf16[256,384]{1,0:T(8,128)(2,1)S(1)}, bf16[128,384]{1,0:T(8,128)(2,1)S(1)}, bf16[128,384]{1,0:T(8,128)(2,1)S(1)}, bf16[128,384]{1,0:T(8,128)(2,...) custom-call(bf16[128,3072]{1,0:T(8,128)(2,1)S(1)} %bitcast.11, ...), custom_call_target="tpu_custom_call" | custom-call | flops 402653184 | bytes 6291456 | tf_op jit(solution)/shard_map/pallas_call | solution.py:358
  38.5 0.4 collective-permute-start.16
  38.9 1.5 %collective-permute-start.17 = (bf16[128,384]{1,0:T(8,128)(2,1)S(1)}, bf16[128,384]{1,0:T(8,128)(2,1)S(1)}, u32[]{:S(2)}, u32[]{:S(2)}) collective-permute-start(bf16[128,384]{1,0:T(8,128)(2,1)S(1)} %get-tuple-element.45), channel_id=1, source_target_pairs={{0,5},{1,4},{2,7},{3,6},{4,1},{5,0},{6,3},{7,2},{8,13},{9,12},{10,... | collective-permute-start | bytes 294920 | tf_op jit(solution)/shard_map/ppermute | solution.py:24
  40.4 1.5 %collective-permute-start.14 = (bf16[128,384]{1,0:T(8,128)(2,1)S(1)}, bf16[128,384]{1,0:T(8,128)(2,1)S(1)}, u32[]{:S(2)}, u32[]{:S(2)}) collective-permute-start(bf16[128,384]{1,0:T(8,128)(2,1)S(1)} %get-tuple-element.42), channel_id=1, source_target_pairs={{0,2},{1,3},{2,0},{3,1},{4,6},{5,7},{6,4},{7,5},{8,10},{9,11},{10,... | collective-permute-start | bytes 294920 | tf_op jit(solution)/shard_map/ppermute | solution.py:24
  42.2 1.3 %collective-permute-start.13 = (bf16[32,1536]{1,0:T(8,128)(2,1)S(1)}, bf16[32,1536]{1,0:T(8,128)(2,1)S(1)}, u32[]{:S(2)}, u32[]{:S(2)}) collective-permute-start(bf16[32,1536]{1,0:T(8,128)(2,1)S(1)} %shard_map.98), channel_id=1, source_target_pairs={{8,0},{16,8},{24,16},{9,1},{17,9},{25,17},{10,2},{18,10},{26,18},{... | collective-permute-start | bytes 294920 | tf_op jit(solution)/shard_map/ppermute | solution.py:20
  43.5 0.7 %collective-permute-done.16.refs_6_.refs_0_ = bf16[128,384]{1,0:T(8,128)(2,1)S(1)} collective-permute-done((bf16[128,384]{1,0:T(8,128)(2,1)S(1)}, bf16[128,384]{1,0:T(8,128)(2,1)S(1)}, u32[]{:S(2)}, u32[]{:S(2)}) %collective-permute-start.16) | collective-permute-done | bytes 98336 | tf_op jit(solution)/shard_map/ppermute | solution.py:24
  44.1 1.3 %collective-permute-done.17.refs_7_.refs_1_ = bf16[128,384]{1,0:T(8,128)(2,1)S(1)} collective-permute-done((bf16[128,384]{1,0:T(8,128)(2,1)S(1)}, bf16[128,384]{1,0:T(8,128)(2,1)S(1)}, u32[]{:S(2)}, u32[]{:S(2)}) %collective-permute-start.17) | collective-permute-done | bytes 98336 | tf_op jit(solution)/shard_map/ppermute | solution.py:24
  45.5 1.3 %collective-permute-start.19 = (bf16[32,768]{1,0:T(8,128)(2,1)S(1)}, bf16[32,768]{1,0:T(8,128)(2,1)S(1)}, u32[]{:S(2)}, u32[]{:S(2)}) collective-permute-start(bf16[32,768]{1,0:T(8,128)(2,1)S(1)} %shard_map.101), channel_id=1, source_target_pairs={{8,0},{16,8},{24,16},{9,1},{17,9},{25,17},{10,2},{18,10},{26,18},{... | collective-permute-start | bytes 147464 | tf_op jit(solution)/shard_map/ppermute | solution.py:20
  47.0 1.3 %collective-permute-start.18 = (bf16[32,768]{1,0:T(8,128)(2,1)S(1)}, bf16[32,768]{1,0:T(8,128)(2,1)S(1)}, u32[]{:S(2)}, u32[]{:S(2)}) collective-permute-start(bf16[32,768]{1,0:T(8,128)(2,1)S(1)} %shard_map.100), channel_id=1, source_target_pairs={{8,0},{16,8},{24,16},{9,1},{17,9},{25,17},{10,2},{18,10},{26,18},{... | collective-permute-start | bytes 147464 | tf_op jit(solution)/shard_map/ppermute | solution.py:20
  49.0 0.3 collective-permute-done.13.lead_ref
  49.3 1.4 %shard_map.99 = (bf16[8,16,3072]{2,1,0:T(8,128)(2,1)}, bf16[8,16,3072]{2,1,0:T(8,128)(2,1)}) custom-call(s32[1]{0:T(128)S(6)} %copy.11.offset_ref, f32[1,128]{1,0:T(1,128)S(1)} %shard_map.86.delta_ref, bf16[128,3072]{1,0:T(8,128)(2,1)S(1)} %bitcast.23, bf16[32,1536]{1,0:T(8,128)(2,1)S(1)} %collective-permute-done.13.lead_ref, ...), custom_call_target="tpu_custom_call" | custom-call | flops 786432 | bytes 3145728 | tf_op jit(solution)/shard_map/pallas_call | solution.py:463
  50.7 0.9 %collective-permute-done.19.refs_1_ = bf16[32,768]{1,0:T(8,128)(2,1)S(1)} collective-permute-done((bf16[32,768]{1,0:T(8,128)(2,1)S(1)}, bf16[32,768]{1,0:T(8,128)(2,1)S(1)}, u32[]{:S(2)}, u32[]{:S(2)}) %collective-permute-start.19) | collective-permute-done | bytes 49184 | tf_op jit(solution)/shard_map/ppermute | solution.py:20
  51.6 2.0 %collective-permute-done.18.refs_0_ = bf16[32,768]{1,0:T(8,128)(2,1)S(1)} collective-permute-done((bf16[32,768]{1,0:T(8,128)(2,1)S(1)}, bf16[32,768]{1,0:T(8,128)(2,1)S(1)}, u32[]{:S(2)}, u32[]{:S(2)}) %collective-permute-start.18) | collective-permute-done | bytes 49184 | tf_op jit(solution)/shard_map/ppermute | solution.py:20
  53.6 0.7 %shard_map.102 = bf16[8,16,3072]{2,1,0:T(8,128)(2,1)} custom-call(s32[1]{0:T(128)S(6)} %copy.11.offset_ref, bf16[2,16,3072]{2,1,0:T(8,128)(2,1)S(1)} %copy-done.4, bf16[32,768]{1,0:T(8,128)(2,1)S(1)} %collective-permute-done.18.refs_0_, bf16[32,768]{1,0:T(8,128)(2,1)S(1)} %collective-permute-done.19.refs_1_, ...), custom_call_target="tpu_custom_call", output_to_operand_aliasing={{}: (4, {})} | custom-call | bytes 589824 | tf_op jit(solution)/shard_map/pallas_call | solution.py:502
  (39 shorter events, 1.1 us)
Async XLA Ops:
  2.1 17.2 %collective-permute-start.5 = (bf16[3,128,768]{2,1,0:T(8,128)(2,1)S(1)}, bf16[3,128,768]{2,1,0:T(8,128)(2,1)S(1)}, u32[]{:S(2)}, u32[]{:S(2)}) collective-permute-start(bf16[3,128,768]{2,1,0:T(8,128)(2,1)S(1)} %get-tuple-element.28), channel_id=1, source_target_pairs={{0,4},{1,5},{2,6},{3,7},{4,0},{5,1},{6,2},{7,3},{8,12},{9,13},{10,... | collective-permute-start | bytes 1769480 | tf_op jit(solution)/shard_map/ppermute | solution.py:24
  5.1 16.3 %collective-permute-start.1 = (bf16[3,128,768]{2,1,0:T(8,128)(2,1)S(1)}, bf16[3,128,768]{2,1,0:T(8,128)(2,1)S(1)}, u32[]{:S(2)}, u32[]{:S(2)}) collective-permute-start(bf16[3,128,768]{2,1,0:T(8,128)(2,1)S(1)} %get-tuple-element.26), channel_id=1, source_target_pairs={{0,2},{1,3},{2,0},{3,1},{4,6},{5,7},{6,4},{7,5},{8,10},{9,11},{10,... | collective-permute-start | bytes 1769480 | tf_op jit(solution)/shard_map/ppermute | solution.py:24
  8.1 19.5 %collective-permute-start.9 = (bf16[2,128,768]{2,1,0:T(8,128)(2,1)S(1)}, bf16[2,128,768]{2,1,0:T(8,128)(2,1)S(1)}, u32[]{:S(2)}, u32[]{:S(2)}) collective-permute-start(bf16[2,128,768]{2,1,0:T(8,128)(2,1)S(1)} %get-tuple-element.32), channel_id=1, source_target_pairs={{0,4},{1,5},{2,6},{3,7},{4,0},{5,1},{6,2},{7,3},{8,12},{9,13},{10,... | collective-permute-start | bytes 1179656 | tf_op jit(solution)/shard_map/ppermute | solution.py:24
  8.7 21.1 %collective-permute-start.7 = (bf16[2,128,768]{2,1,0:T(8,128)(2,1)S(1)}, bf16[2,128,768]{2,1,0:T(8,128)(2,1)S(1)}, u32[]{:S(2)}, u32[]{:S(2)}) collective-permute-start(bf16[2,128,768]{2,1,0:T(8,128)(2,1)S(1)} %get-tuple-element.29), channel_id=1, source_target_pairs={{0,2},{1,3},{2,0},{3,1},{4,6},{5,7},{6,4},{7,5},{8,10},{9,11},{10,... | collective-permute-start | bytes 1179656 | tf_op jit(solution)/shard_map/ppermute | solution.py:24
  19.3 2.7 %collective-permute-start.6 = (bf16[3,128,384]{2,1,0:T(8,128)(2,1)S(1)}, bf16[3,128,384]{2,1,0:T(8,128)(2,1)S(1)}, u32[]{:S(2)}, u32[]{:S(2)}) collective-permute-start(bf16[3,128,384]{2,1,0:T(8,128)(2,1)S(1)} %shard_map.91), channel_id=1, source_target_pairs={{0,1},{1,0},{2,3},{3,2},{4,5},{5,4},{6,7},{7,6},{8,9},{9,8},{10,11... | collective-permute-start | bytes 884744 | tf_op jit(solution)/shard_map/ppermute | solution.py:24
  21.4 2.2 %collective-permute-start.2 = (bf16[3,128,384]{2,1,0:T(8,128)(2,1)S(1)}, bf16[3,128,384]{2,1,0:T(8,128)(2,1)S(1)}, u32[]{:S(2)}, u32[]{:S(2)}) collective-permute-start(bf16[3,128,384]{2,1,0:T(8,128)(2,1)S(1)} %shard_map.89), channel_id=1, source_target_pairs={{0,1},{1,0},{2,3},{3,2},{4,5},{5,4},{6,7},{7,6},{8,9},{9,8},{10,11... | collective-permute-start | bytes 884744 | tf_op jit(solution)/shard_map/ppermute | solution.py:24
  21.4 8.3 %collective-permute-start = (bf16[3,128,384]{2,1,0:T(8,128)(2,1)S(1)}, bf16[3,128,384]{2,1,0:T(8,128)(2,1)S(1)}, u32[]{:S(2)}, u32[]{:S(2)}) collective-permute-start(bf16[3,128,384]{2,1,0:T(8,128)(2,1)S(1)} %get-tuple-element.25), channel_id=1, source_target_pairs={{0,1},{1,0},{2,3},{3,2},{4,5},{5,4},{6,7},{7,6},{8,9},{9,8},{10,11... | collective-permute-start | bytes 884744 | tf_op jit(solution)/shard_map/ppermute | solution.py:24
  22.0 14.7 %collective-permute-start.11 = (bf16[2,256,384]{2,1,0:T(8,128)(2,1)S(1)}, bf16[2,256,384]{2,1,0:T(8,128)(2,1)S(1)}, u32[]{:S(2)}, u32[]{:S(2)}) collective-permute-start(bf16[2,256,384]{2,1,0:T(8,128)(2,1)S(1)} %shard_map.96), channel_id=1, source_target_pairs={{0,2},{1,3},{2,0},{3,1},{4,6},{5,7},{6,4},{7,5},{8,10},{9,11},{10,... | collective-permute-start | bytes 1179656 | tf_op jit(solution)/shard_map/ppermute | solution.py:24
  23.6 7.7 %copy-start.1 = (bf16[1,8,16,3072]{3,2,1,0:T(8,128)(2,1)S(1)}, bf16[1,8,16,3072]{3,2,1,0:T(8,128)(2,1)}, u32[]{:S(2)}) copy-start(bf16[1,8,16,3072]{3,2,1,0:T(8,128)(2,1)} %param.9) | copy-start | bytes 2359300
  23.6 7.7 %copy-start.2 = (bf16[1,8,16,3072]{3,2,1,0:T(8,128)(2,1)S(1)}, bf16[1,8,16,3072]{3,2,1,0:T(8,128)(2,1)}, u32[]{:S(2)}) copy-start(bf16[1,8,16,3072]{3,2,1,0:T(8,128)(2,1)} %param.10) | copy-start | bytes 2359300
  23.6 7.6 %copy-start = (bf16[1,8,16,3072]{3,2,1,0:T(8,128)(2,1)S(1)}, bf16[1,8,16,3072]{3,2,1,0:T(8,128)(2,1)}, u32[]{:S(2)}) copy-start(bf16[1,8,16,3072]{3,2,1,0:T(8,128)(2,1)} %param.8) | copy-start | bytes 2359300
  23.6 13.1 %collective-permute-start.3 = (bf16[2,256,384]{2,1,0:T(8,128)(2,1)S(1)}, bf16[2,256,384]{2,1,0:T(8,128)(2,1)S(1)}, u32[]{:S(2)}, u32[]{:S(2)}) collective-permute-start(bf16[2,256,384]{2,1,0:T(8,128)(2,1)S(1)} %shard_map.90), channel_id=1, source_target_pairs={{0,4},{1,5},{2,6},{3,7},{4,0},{5,1},{6,2},{7,3},{8,12},{9,13},{10,... | collective-permute-start | bytes 1179656 | tf_op jit(solution)/shard_map/ppermute | solution.py:24
  27.5 5.5 %collective-permute-start.4 = (bf16[3,128,384]{2,1,0:T(8,128)(2,1)S(1)}, bf16[3,128,384]{2,1,0:T(8,128)(2,1)S(1)}, u32[]{:S(2)}, u32[]{:S(2)}) collective-permute-start(bf16[3,128,384]{2,1,0:T(8,128)(2,1)S(1)} %get-tuple-element.27), channel_id=1, source_target_pairs={{0,1},{1,0},{2,3},{3,2},{4,5},{5,4},{6,7},{7,6},{8,9},{9,8},{10,11... | collective-permute-start | bytes 884744 | tf_op jit(solution)/shard_map/ppermute | solution.py:24
  27.6 2.8 %copy-start.5 = (s32[4]{0:T(128)S(1)}, s32[4]{0:T(128)}, u32[]{:S(2)}) copy-start(s32[4]{0:T(128)} %timesteps_ref.1) | copy-start | bytes 52
  29.8 1.4 %collective-permute-start.10 = (bf16[2,128,384]{2,1,0:T(8,128)(2,1)S(1)}, bf16[2,128,384]{2,1,0:T(8,128)(2,1)S(1)}, u32[]{:S(2)}, u32[]{:S(2)}) collective-permute-start(bf16[2,128,384]{2,1,0:T(8,128)(2,1)S(1)} %shard_map.94), channel_id=1, source_target_pairs={{0,1},{1,0},{2,3},{3,2},{4,5},{5,4},{6,7},{7,6},{8,9},{9,8},{10,11... | collective-permute-start | bytes 589832 | tf_op jit(solution)/shard_map/ppermute | solution.py:24
  29.8 3.2 %collective-permute-start.8 = (bf16[2,128,384]{2,1,0:T(8,128)(2,1)S(1)}, bf16[2,128,384]{2,1,0:T(8,128)(2,1)S(1)}, u32[]{:S(2)}, u32[]{:S(2)}) collective-permute-start(bf16[2,128,384]{2,1,0:T(8,128)(2,1)S(1)} %shard_map.92), channel_id=1, source_target_pairs={{0,1},{1,0},{2,3},{3,2},{4,5},{5,4},{6,7},{7,6},{8,9},{9,8},{10,11... | collective-permute-start | bytes 589832 | tf_op jit(solution)/shard_map/ppermute | solution.py:24
  36.7 1.7 %copy-start.3 = (bf16[1,8,16,3072]{3,2,1,0:T(8,128)(2,1)S(1)}, bf16[1,8,16,3072]{3,2,1,0:T(8,128)(2,1)}, u32[]{:S(2)}) copy-start(bf16[1,8,16,3072]{3,2,1,0:T(8,128)(2,1)} %param.7) | copy-start | bytes 2359300
  38.4 3.7 %collective-permute-start.12 = (bf16[256,384]{1,0:T(8,128)(2,1)S(1)}, bf16[256,384]{1,0:T(8,128)(2,1)S(1)}, u32[]{:S(2)}, u32[]{:S(2)}) collective-permute-start(bf16[256,384]{1,0:T(8,128)(2,1)S(1)} %get-tuple-element.40), channel_id=1, source_target_pairs={{0,1},{1,0},{2,3},{3,2},{4,5},{5,4},{6,7},{7,6},{8,9},{9,8},{10,11... | collective-permute-start | bytes 589832 | tf_op jit(solution)/shard_map/ppermute | solution.py:24
  38.5 5.7 %collective-permute-start.16 = (bf16[128,384]{1,0:T(8,128)(2,1)S(1)}, bf16[128,384]{1,0:T(8,128)(2,1)S(1)}, u32[]{:S(2)}, u32[]{:S(2)}) collective-permute-start(bf16[128,384]{1,0:T(8,128)(2,1)S(1)} %get-tuple-element.44), channel_id=1, source_target_pairs={{0,4},{1,5},{2,6},{3,7},{4,0},{5,1},{6,2},{7,3},{8,12},{9,13},{10,... | collective-permute-start | bytes 294920 | tf_op jit(solution)/shard_map/ppermute | solution.py:24
  38.9 6.5 %collective-permute-start.17 = (bf16[128,384]{1,0:T(8,128)(2,1)S(1)}, bf16[128,384]{1,0:T(8,128)(2,1)S(1)}, u32[]{:S(2)}, u32[]{:S(2)}) collective-permute-start(bf16[128,384]{1,0:T(8,128)(2,1)S(1)} %get-tuple-element.45), channel_id=1, source_target_pairs={{0,5},{1,4},{2,7},{3,6},{4,1},{5,0},{6,3},{7,2},{8,13},{9,12},{10,... | collective-permute-start | bytes 294920 | tf_op jit(solution)/shard_map/ppermute | solution.py:24
  40.4 6.4 %collective-permute-start.14 = (bf16[128,384]{1,0:T(8,128)(2,1)S(1)}, bf16[128,384]{1,0:T(8,128)(2,1)S(1)}, u32[]{:S(2)}, u32[]{:S(2)}) collective-permute-start(bf16[128,384]{1,0:T(8,128)(2,1)S(1)} %get-tuple-element.42), channel_id=1, source_target_pairs={{0,2},{1,3},{2,0},{3,1},{4,6},{5,7},{6,4},{7,5},{8,10},{9,11},{10,... | collective-permute-start | bytes 294920 | tf_op jit(solution)/shard_map/ppermute | solution.py:24
  41.9 5.1 %collective-permute-start.15 = (bf16[128,384]{1,0:T(8,128)(2,1)S(1)}, bf16[128,384]{1,0:T(8,128)(2,1)S(1)}, u32[]{:S(2)}, u32[]{:S(2)}) collective-permute-start(bf16[128,384]{1,0:T(8,128)(2,1)S(1)} %get-tuple-element.43), channel_id=1, source_target_pairs={{0,3},{1,2},{2,1},{3,0},{4,7},{5,6},{6,5},{7,4},{8,11},{9,10},{10,... | collective-permute-start | bytes 294920 | tf_op jit(solution)/shard_map/ppermute | solution.py:24
  42.2 7.1 %collective-permute-start.13 = (bf16[32,1536]{1,0:T(8,128)(2,1)S(1)}, bf16[32,1536]{1,0:T(8,128)(2,1)S(1)}, u32[]{:S(2)}, u32[]{:S(2)}) collective-permute-start(bf16[32,1536]{1,0:T(8,128)(2,1)S(1)} %shard_map.98), channel_id=1, source_target_pairs={{8,0},{16,8},{24,16},{9,1},{17,9},{25,17},{10,2},{18,10},{26,18},{... | collective-permute-start | bytes 294920 | tf_op jit(solution)/shard_map/ppermute | solution.py:20
  45.5 6.1 %collective-permute-start.19 = (bf16[32,768]{1,0:T(8,128)(2,1)S(1)}, bf16[32,768]{1,0:T(8,128)(2,1)S(1)}, u32[]{:S(2)}, u32[]{:S(2)}) collective-permute-start(bf16[32,768]{1,0:T(8,128)(2,1)S(1)} %shard_map.101), channel_id=1, source_target_pairs={{8,0},{16,8},{24,16},{9,1},{17,9},{25,17},{10,2},{18,10},{26,18},{... | collective-permute-start | bytes 147464 | tf_op jit(solution)/shard_map/ppermute | solution.py:20
  47.0 6.6 %collective-permute-start.18 = (bf16[32,768]{1,0:T(8,128)(2,1)S(1)}, bf16[32,768]{1,0:T(8,128)(2,1)S(1)}, u32[]{:S(2)}, u32[]{:S(2)}) collective-permute-start(bf16[32,768]{1,0:T(8,128)(2,1)S(1)} %shard_map.100), channel_id=1, source_target_pairs={{8,0},{16,8},{24,16},{9,1},{17,9},{25,17},{10,2},{18,10},{26,18},{... | collective-permute-start | bytes 147464 | tf_op jit(solution)/shard_map/ppermute | solution.py:20
  49.3 4.4 %copy-start.4 = (bf16[2,16,3072]{2,1,0:T(8,128)(2,1)S(1)}, bf16[2,16,3072]{2,1,0:T(8,128)(2,1)}, u32[]{:S(2)}) copy-start(bf16[2,16,3072]{2,1,0:T(8,128)(2,1)} %fresh_ref.1) | copy-start | bytes 589828

commit v6 on v5

--- a/solution.py
+++ b/solution.py
@@ -22,6 +22,12 @@
 
 def swapped(block, bit):
     return lax.ppermute(block, "seq", [(i, i ^ bit) for i in range(lax.axis_size("seq"))])
+
+
+def crossed(block, turn, other=0):
+    bits = (ACROSS, DOWN) if turn == 0 else (DOWN, ACROSS)
+    devices = range(lax.axis_size("seq"))
+    return lax.ppermute(block, "seq", [(i, i ^ bits[i % 2] ^ other) for i in devices])
 
 
 def after(block, *others):
@@ -127,16 +133,36 @@
 
 
 def columns(side, mask, width):
+    if side is None:
+        return turn_columns(*mask, width)
     bit, _, base = side
     index = lax.bitwise_xor(lax.axis_index("seq"), mask)
     start = base + (index // bit) % 2 * (width // 4) + index % 2 * (width // 8)
     return pl.ds(pl.multiple_of(start, HEAD_SIZE), width // 8)
 
 
+def turn_columns(turn, other, width):
+    index = lax.axis_index("seq")
+    first = (index + other) % 2 == turn
+    index = lax.bitwise_xor(index, jnp.where(first, ACROSS, DOWN))
+    index = lax.bitwise_xor(index, other)
+    half = jnp.where(first, index // ACROSS % 2, 2 + index // DOWN % 2)
+    start = half * (width // 4) + index % 2 * (width // 8)
+    return pl.ds(pl.multiple_of(start, HEAD_SIZE), width // 8)
+
+
 def half_columns(side, mask, width):
     bit, _, base = side
     index = lax.bitwise_xor(lax.axis_index("seq"), mask)
     start = base + (index // bit) % 2 * (width // 4)
+    return pl.ds(pl.multiple_of(start, HEAD_SIZE), width // 4)
+
+
+def send_columns(turn, mask, width):
+    index = lax.axis_index("seq")
+    first = 1 - (index // ACROSS) % 2
+    second = 1 - (index // DOWN) % 2
+    start = jnp.where(index % 2 == turn, first, 2 + second) * (width // 4)
     return pl.ds(pl.multiple_of(start, HEAD_SIZE), width // 4)
 
 
@@ -178,7 +204,7 @@
     rows, width = arrays[0].shape
     outs = tuple(
         jax.ShapeDtypeStruct(
-            (count, rows, width // (4 if cut is half_columns else 8)), jnp.bfloat16
+            (count, rows, width // (8 if cut is columns else 4)), jnp.bfloat16
         )
         for cut, _, _, count in cuts
     )
@@ -190,6 +216,27 @@
         [pltpu.SemaphoreType.DMA((len(outs), 3))],
         (0, sum(4 * out.size for out in outs), 0),
     )(*[pltpu.with_memory_space_constraint(array, pltpu.HBM) for array in arrays])
+
+
+def sort_kernel(*refs):
+    turns, outs = refs[:2], refs[2:]
+    core = lax.axis_index("seq") % 2
+    for parity in range(2):
+
+        @pl.when(core == parity)
+        def _():
+            for index, out in enumerate(outs):
+                out[...] = turns[(index + parity) % 2][...]
+
+
+def sort(*turns):
+    return call(
+        sort_kernel,
+        tuple(jax.ShapeDtypeStruct(turn.shape, turn.dtype) for turn in turns),
+        [VMEM] * 2,
+        (VMEM,) * 2,
+        cost=(0, 8 * turns[0].size, 0),
+    )(*turns)
 
 
 def split_kernel(got_ref, out_ref):
@@ -341,13 +388,14 @@
 def complete_both_kernel(sides, queries_ref, *refs):
     count = 7
     inputs, outs = refs[: count * len(sides)], refs[count * len(sides) :]
-    core_ref, outs = outs[0], outs[1:]
+    core_ref, *turn_refs = outs[:3]
     rows = queries_ref.shape[0]
     for index, side in enumerate(sides):
-        own, *backs = outs[3 * index : 3 * index + 3]
+        turn = (lax.axis_index("seq") + index) % 2
         core = core_ref.at[index * rows : (index + 1) * rows]
         parts = inputs[count * index : count * (index + 1)]
-        complete_kernel(side, queries_ref, *parts, own, core, *backs)
+        backs = [ref.at[turn] for ref in turn_refs]
+        complete_kernel(side, queries_ref, *parts, outs[3 + index], core, *backs)
 
 
 def complete(sides, queries, received):
@@ -355,14 +403,14 @@
     size = width // 8
     out = jax.ShapeDtypeStruct((rows, size), jnp.bfloat16)
     core = jax.ShapeDtypeStruct((len(sides) * rows, size), jnp.bfloat16)
-    outs = call(
+    turn = jax.ShapeDtypeStruct((len(sides), rows, size), jnp.bfloat16)
+    return call(
         functools.partial(complete_both_kernel, sides),
-        (core,) + (out,) * (3 * len(sides)),
+        (core, turn, turn) + (out,) * len(sides),
         [VMEM] * (1 + 7 * len(sides)),
-        (VMEM,) * (1 + 3 * len(sides)),
+        (VMEM,) * (3 + len(sides)),
         cost=(64 * rows * rows * size, 128 * rows * size, 16 * rows * rows * size // HEAD_SIZE),
     )(queries, *[part for parts in received for part in parts])
-    return outs[0], [outs[3 * index + 1 : 3 * index + 4] for index in range(len(sides))]
 
 
 def moved(latents, attended, delta):
@@ -523,14 +571,15 @@
     )
     sides = ((ACROSS, DOWN, 0), (DOWN, ACROSS, width // 2))
     arrays = (keys, values, queries)
-    sends = pack([(half_columns, side, side[0], 3) for side in sides], arrays)
+    sends = pack([(send_columns, turn, 0, 3) for turn in range(len(sides))], arrays)
     owns = pack(
         [(half_columns, side, 0, 2) for side in sides]
         + [(columns, side, CORE, 3) for side in sides],
         arrays,
     )
     owns, cores = owns[: len(sides)], owns[len(sides) :]
-    gots = [swapped(send, side[0]) for send, side in zip(sends, sides)]
+    turns = [crossed(send, turn) for turn, send in enumerate(sends)]
+    gots = sort(*turns)
     cores = [swapped(core, CORE) for core in cores]
     got_cores = [swapped(split(got), CORE) for got in gots]
     fars = [swapped(own, side[1]) for side, own in zip(sides, owns)]
@@ -543,7 +592,7 @@
     delta = step_size(timesteps)
     first_latents = latents[:first_rows]
     far_gots = [after(far, states[1 - index][0], delta) for index, far in enumerate(far_gots)]
-    core_out, results = complete(
+    core_out, alike, unlike, *results = complete(
         sides,
         queries,
         [
@@ -553,11 +602,11 @@
     )
     core_back = swapped(core_out, CORE)
     near_places, near_pieces, far_places, far_pieces = [], [], [], []
-    for index, (side, (own, *backs)) in enumerate(zip(sides, results)):
+    for index, (side, own) in enumerate(zip(sides, results)):
         near_places += [(side, 0), (side, CORE)]
         near_pieces += [own, core_back[index * rows : (index + 1) * rows]]
-        far_places += [(side, mask) for mask in peers(side)[1:]]
-        far_pieces += [swapped(back, mask) for back, mask in zip(backs, peers(side)[1:])]
+        far_places += [(None, (index, 0)), (None, (index, CORE))]
+        far_pieces += [crossed(alike[index], index), crossed(unlike[index], index, CORE)]
     early = shifted(lead(near_places, delta, first_latents, near_pieces), "queue", -1)
     groups = [far_places[:2], far_places[2:]]
     late = [

time: 54.6 us -> 53.5 us (0.980)
  waiting for transfers between devices: 25 us -> 22.6 us
  starting transfers between devices: 16.6 us -> 17.6 us
    ppermute x17 -> x11, waiting for transfers between devices: 21.7 us -> 5.8 us  [swapped(): lax.ppermute(block, 'seq', [(i, i ^ bit) for i in range(lax.axis_size('se...]
    ppermute x0 -> x6, waiting for transfers between devices: none -> 13.8 us  [crossed(): lax.ppermute(block, 'seq', [(i, i ^ bits[i % 2] ^ other) for i in devices])]
    ppermute x0 -> x6, starting transfers between devices: none -> 8.51 us  [crossed(): lax.ppermute(block, 'seq', [(i, i ^ bits[i % 2] ^ other) for i in devices])]
    ppermute x17 -> x11, starting transfers between devices: 12.7 us -> 5.22 us  [swapped(): lax.ppermute(block, 'seq', [(i, i ^ bit) for i in range(lax.axis_size('se...]
    pallas_call x1 -> x2, Pallas kernels: 1.63 us -> 1.73 us  [the longest x1 1.65 us: complete(): call(functools.partial(complete_both_kernel, sides), (core, turn, turn) +...]
  transfers between devices with their start and end apart: 20 -> 20, of which waited for: 12 -> 11; matrix products, arithmetic and copies ran while one was open for 0% -> 0% of each run, Pallas kernels for 14% -> 14%
where the time goes in v6:
time: 53.5 us; the launch traced here: 53.3 us
  waiting for transfers between devices  22.6 us (42%)
  starting transfers between devices  17.6 us (33%)
  Pallas kernels  11.4 us (21%)
  between operations  1.54 us (3%)
    ppermute x6, waiting for transfers between devices, crossed(): lax.ppermute(block, 'seq', [(i, i ^ bits[i % 2] ^ other) for i in devices])  13.8 us
    ppermute x6, starting transfers between devices, crossed(): lax.ppermute(block, 'seq', [(i, i ^ bits[i % 2] ^ other) for i in devices])  8.51 us
    ppermute x11, waiting for transfers between devices, swapped(): lax.ppermute(block, 'seq', [(i, i ^ bit) for i in range(lax.axis_size('se...  5.8 us
    ppermute x11, starting transfers between devices, swapped(): lax.ppermute(block, 'seq', [(i, i ^ bit) for i in range(lax.axis_size('se...  5.22 us
    ppermute x3, starting transfers between devices, shifted(): return lax.ppermute(block, axis, route)  3.88 us
    pallas_call x2, Pallas kernels, attend(): call(functools.partial(attend_kernel, side), (out,) * 3, [VMEM] * 8, (VME...  3.6 us
    ppermute x3, waiting for transfers between devices, shifted(): return lax.ppermute(block, axis, route)  3.07 us
    pallas_call x2, Pallas kernels, pack(): call(functools.partial(pack_kernel, cuts), outs, [HBM] * 3, (VMEM,) * len...  2.92 us
  transfers between devices with their start and end apart: 20, of which 11 were waited for; matrix products, arithmetic and copies ran while one was open for 0% of the time, Pallas kernels for 14%

profile of v6, /device:TPU:0, one launch (start us, length us, event | category | flops | bytes accessed | tf_op | source)
XLA Modules:
  0.0 53.3 jit_solution(15791992683505666256)
XLA Ops:
  0.6 1.4 %shard_map.88 = (bf16[3,128,768]{2,1,0:T(8,128)(2,1)S(1)}, bf16[3,128,768]{2,1,0:T(8,128)(2,1)S(1)}) custom-call(bf16[128,3072]{1,0:T(8,128)(2,1)} %bitcast.20, bf16[128,3072]{1,0:T(8,128)(2,1)} %bitcast.24, bf16[128,3072]{1,0:T(8,128)(2,1)} %bitcast.15), custom_call_target="tpu_custom_call" | custom-call | bytes 2359296 | tf_op jit(solution)/shard_map/pallas_call | solution.py:211
  2.1 3.0 %collective-permute-start.1 = (bf16[3,128,768]{2,1,0:T(8,128)(2,1)S(1)}, bf16[3,128,768]{2,1,0:T(8,128)(2,1)S(1)}, u32[]{:S(2)}, u32[]{:S(2)}) collective-permute-start(bf16[3,128,768]{2,1,0:T(8,128)(2,1)S(1)} %get-tuple-element.26), channel_id=1, source_target_pairs={{0,2},{1,5},{2,0},{3,7},{4,6},{5,1},{6,4},{7,3},{8,10},{9,13},{10,... | collective-permute-start | bytes 1769480 | tf_op jit(solution)/shard_map/ppermute | solution.py:30
  5.1 1.5 %collective-permute-start.2 = (bf16[3,128,768]{2,1,0:T(8,128)(2,1)S(1)}, bf16[3,128,768]{2,1,0:T(8,128)(2,1)S(1)}, u32[]{:S(2)}, u32[]{:S(2)}) collective-permute-start(bf16[3,128,768]{2,1,0:T(8,128)(2,1)S(1)} %get-tuple-element.27), channel_id=1, source_target_pairs={{0,4},{1,3},{2,6},{3,1},{4,0},{5,7},{6,2},{7,5},{8,12},{9,11},{10,... | collective-permute-start | bytes 1769480 | tf_op jit(solution)/shard_map/ppermute | solution.py:30
  6.6 1.5 %shard_map.87 = (bf16[2,128,768]{2,1,0:T(8,128)(2,1)S(1)}, bf16[2,128,768]{2,1,0:T(8,128)(2,1)S(1)}, bf16[3,128,384]{2,1,0:T(8,128)(2,1)S(1)}, bf16[3,128,384]{2,1,0:T(8,128)(2,1)S(1)}) custom-call(bf16[128,3072]{1,0:T(8,128)(2,1)} %bitcast.21, bf16[128,3072]{1,0:T(8,128)(2,1)} %bitcast.25, bf16[128,3072]{1,0:T(8,128)(2,1)} %bitcast.16), custom_call_target="tpu_custom_call" | custom-call | bytes 2752512 | tf_op jit(solution)/shard_map/pallas_call | solution.py:211
  8.1 0.6 %collective-permute-start.9 = (bf16[2,128,768]{2,1,0:T(8,128)(2,1)S(1)}, bf16[2,128,768]{2,1,0:T(8,128)(2,1)S(1)}, u32[]{:S(2)}, u32[]{:S(2)}) collective-permute-start(bf16[2,128,768]{2,1,0:T(8,128)(2,1)S(1)} %get-tuple-element.34), channel_id=1, source_target_pairs={{0,4},{1,5},{2,6},{3,7},{4,0},{5,1},{6,2},{7,3},{8,12},{9,13},{10,... | collective-permute-start | bytes 1179656 | tf_op jit(solution)/shard_map/ppermute | solution.py:24
  8.7 0.1 collective-permute-start.7
  8.8 9.9 %collective-permute-done.1.refs_0_ = bf16[3,128,768]{2,1,0:T(8,128)(2,1)S(1)} collective-permute-done((bf16[3,128,768]{2,1,0:T(8,128)(2,1)S(1)}, bf16[3,128,768]{2,1,0:T(8,128)(2,1)S(1)}, u32[]{:S(2)}, u32[]{:S(2)}) %collective-permute-start.1) | collective-permute-done | bytes 589856 | tf_op jit(solution)/shard_map/ppermute | solution.py:30
  18.7 2.7 %collective-permute-done.2.refs_1_ = bf16[3,128,768]{2,1,0:T(8,128)(2,1)S(1)} collective-permute-done((bf16[3,128,768]{2,1,0:T(8,128)(2,1)S(1)}, bf16[3,128,768]{2,1,0:T(8,128)(2,1)S(1)}, u32[]{:S(2)}, u32[]{:S(2)}) %collective-permute-start.2) | collective-permute-done | bytes 589856 | tf_op jit(solution)/shard_map/ppermute | solution.py:30
  21.6 0.5 %collective-permute-start.3 = (bf16[3,128,384]{2,1,0:T(8,128)(2,1)S(1)}, bf16[3,128,384]{2,1,0:T(8,128)(2,1)S(1)}, u32[]{:S(2)}, u32[]{:S(2)}) collective-permute-start(bf16[3,128,384]{2,1,0:T(8,128)(2,1)S(1)} %shard_map.90), channel_id=1, source_target_pairs={{0,1},{1,0},{2,3},{3,2},{4,5},{5,4},{6,7},{7,6},{8,9},{9,8},{10,11... | collective-permute-start | bytes 884744 | tf_op jit(solution)/shard_map/ppermute | solution.py:24
  22.2 0.9 %collective-permute-done.6.got_core_ref.core_ref.refs_9_ = bf16[3,128,384]{2,1,0:T(8,128)(2,1)S(1)} collective-permute-done((bf16[3,128,384]{2,1,0:T(8,128)(2,1)S(1)}, bf16[3,128,384]{2,1,0:T(8,128)(2,1)S(1)}, u32[]{:S(2)}, u32[]{:S(2)}) %collective-permute-start.6) | collective-permute-done | bytes 294944 | tf_op jit(solution)/shard_map/ppermute | solution.py:24
  23.3 0.3 collective-permute-done.3.core_ref.got_core_ref.refs_2_
  23.6 1.8 %collective-permute-start.4 = (bf16[2,256,384]{2,1,0:T(8,128)(2,1)S(1)}, bf16[2,256,384]{2,1,0:T(8,128)(2,1)S(1)}, u32[]{:S(2)}, u32[]{:S(2)}) collective-permute-start(bf16[2,256,384]{2,1,0:T(8,128)(2,1)S(1)} %shard_map.91), channel_id=1, source_target_pairs={{0,4},{1,5},{2,6},{3,7},{4,0},{5,1},{6,2},{7,3},{8,12},{9,13},{10,... | collective-permute-start | bytes 1179656 | tf_op jit(solution)/shard_map/ppermute | solution.py:24
  25.4 1.8 %collective-permute-done.9.got_ref.far_ref = bf16[2,128,768]{2,1,0:T(8,128)(2,1)S(1)} collective-permute-done((bf16[2,128,768]{2,1,0:T(8,128)(2,1)S(1)}, bf16[2,128,768]{2,1,0:T(8,128)(2,1)S(1)}, u32[]{:S(2)}, u32[]{:S(2)}) %collective-permute-start.9) | collective-permute-done | bytes 393248 | tf_op jit(solution)/shard_map/ppermute | solution.py:24
  27.2 1.1 %collective-permute-start.10 = (bf16[2,128,384]{2,1,0:T(8,128)(2,1)S(1)}, bf16[2,128,384]{2,1,0:T(8,128)(2,1)S(1)}, u32[]{:S(2)}, u32[]{:S(2)}) collective-permute-start(bf16[2,128,384]{2,1,0:T(8,128)(2,1)S(1)} %shard_map.95), channel_id=1, source_target_pairs={{0,1},{1,0},{2,3},{3,2},{4,5},{5,4},{6,7},{7,6},{8,9},{9,8},{10,11... | collective-permute-start | bytes 589832 | tf_op jit(solution)/shard_map/ppermute | solution.py:24
  28.5 0.6 %shard_map.86.delta_ref = f32[1,128]{1,0:T(1,128)S(1)} custom-call(s32[4]{0:T(128)S(1)} %copy-done.5), custom_call_target="tpu_custom_call" | custom-call | tf_op jit(solution)/shard_map/pallas_call | solution.py:186
  29.1 0.4 collective-permute-done.10.far_core_ref
  29.4 1.8 %shard_map.96 = (f32[512,384]{1,0:T(8,128)S(1)}, f32[512,384]{1,0:T(8,128)S(1)}, f32[512,384]{1,0:T(8,128)S(1)}) custom-call(bf16[128,3072]{1,0:T(8,128)(2,1)S(1)} %bitcast.22, bf16[128,3072]{1,0:T(8,128)(2,1)S(1)} %bitcast.26, bf16[128,3072]{1,0:T(8,128)(2,1)S(1)} %bitcast.17, bf16[3,128,384]{2,1,0:T(8,128)(2,1)S(1)} %collective-permute-done.core_ref.refs_0_, ...), custom_call_target="tpu_custom_call" | custom-call | flops 603979776 | bytes 3145728 | tf_op jit(solution)/shard_map/pallas_call | solution.py:350
  31.3 1.8 %shard_map.94 = (f32[512,384]{1,0:T(8,128)S(1)}, f32[512,384]{1,0:T(8,128)S(1)}, f32[512,384]{1,0:T(8,128)S(1)}) custom-call(bf16[128,3072]{1,0:T(8,128)(2,1)S(1)} %bitcast.23, bf16[128,3072]{1,0:T(8,128)(2,1)S(1)} %bitcast.27, bf16[128,3072]{1,0:T(8,128)(2,1)S(1)} %bitcast.18, bf16[3,128,384]{2,1,0:T(8,128)(2,1)S(1)} %collective-permute-done.5.core_ref.refs_7_, ...), custom_call_target="tpu_custom_call" | custom-call | flops 603979776 | bytes 3145728 | tf_op jit(solution)/shard_map/pallas_call | solution.py:350
  33.1 2.5 %collective-permute-done.11.refs_10_ = bf16[2,256,384]{2,1,0:T(8,128)(2,1)S(1)} collective-permute-done((bf16[2,256,384]{2,1,0:T(8,128)(2,1)S(1)}, bf16[2,256,384]{2,1,0:T(8,128)(2,1)S(1)}, u32[]{:S(2)}, u32[]{:S(2)}) %collective-permute-start.11) | collective-permute-done | bytes 393248 | tf_op jit(solution)/shard_map/ppermute | solution.py:24
  35.5 1.6 %shard_map.98 = (bf16[256,384]{1,0:T(8,128)(2,1)S(1)}, bf16[2,128,384]{2,1,0:T(8,128)(2,1)S(1)}, bf16[2,128,384]{2,1,0:T(8,128)(2,1)S(1)}, bf16[128,384]{1,0:T(8,128)(2,1)S(1)}, bf16[128,384]{1,0:T(8,128)(2,1)S(1)}) custom-call(bf16[128,3072]{1,0:T(8,128)(2,1)S(1)} %bitcast.19, bf16[3,128,384]{2,1,0:T(8,128)(2,1)S(1)} %collective-permute-done.core_ref.refs_0_, ...), custom_call_target="tpu_custom_call" | custom-call | flops 402653184 | bytes 6291456 | tf_op jit(solution)/shard_map/pallas_call | solution.py:407
  37.2 1.6 %collective-permute-start.16 = (bf16[128,384]{1,0:T(8,128)(2,1)S(1)}, bf16[128,384]{1,0:T(8,128)(2,1)S(1)}, u32[]{:S(2)}, u32[]{:S(2)}) collective-permute-start(bf16[128,384]{1,0:T(8,128)(2,1)S(1)} %get-tuple-element.50), channel_id=1, source_target_pairs={{0,4},{1,3},{2,6},{3,1},{4,0},{5,7},{6,2},{7,5},{8,12},{9,11},{10,... | collective-permute-start | bytes 294920 | tf_op jit(solution)/shard_map/ppermute | solution.py:30
  38.8 0.7 %collective-permute-start.12 = (bf16[256,384]{1,0:T(8,128)(2,1)S(1)}, bf16[256,384]{1,0:T(8,128)(2,1)S(1)}, u32[]{:S(2)}, u32[]{:S(2)}) collective-permute-start(bf16[256,384]{1,0:T(8,128)(2,1)S(1)} %get-tuple-element.42), channel_id=1, source_target_pairs={{0,1},{1,0},{2,3},{3,2},{4,5},{5,4},{6,7},{7,6},{8,9},{9,8},{10,11... | collective-permute-start | bytes 589832 | tf_op jit(solution)/shard_map/ppermute | solution.py:24
  39.7 2.3 %collective-permute-start.14 = (bf16[128,384]{1,0:T(8,128)(2,1)S(1)}, bf16[128,384]{1,0:T(8,128)(2,1)S(1)}, u32[]{:S(2)}, u32[]{:S(2)}) collective-permute-start(bf16[128,384]{1,0:T(8,128)(2,1)S(1)} %get-tuple-element.51), channel_id=1, source_target_pairs={{0,2},{1,5},{2,0},{3,7},{4,6},{5,1},{6,4},{7,3},{8,10},{9,13},{10,... | collective-permute-start | bytes 294920 | tf_op jit(solution)/shard_map/ppermute | solution.py:30
  42.1 1.3 %collective-permute-start.13 = (bf16[32,1536]{1,0:T(8,128)(2,1)S(1)}, bf16[32,1536]{1,0:T(8,128)(2,1)S(1)}, u32[]{:S(2)}, u32[]{:S(2)}) collective-permute-start(bf16[32,1536]{1,0:T(8,128)(2,1)S(1)} %shard_map.99), channel_id=1, source_target_pairs={{8,0},{16,8},{24,16},{9,1},{17,9},{25,17},{10,2},{18,10},{26,18},{... | collective-permute-start | bytes 294920 | tf_op jit(solution)/shard_map/ppermute | solution.py:20
  43.4 0.5 collective-permute-done.17.refs_7_.refs_1_
  44.0 1.3 %collective-permute-start.19 = (bf16[32,768]{1,0:T(8,128)(2,1)S(1)}, bf16[32,768]{1,0:T(8,128)(2,1)S(1)}, u32[]{:S(2)}, u32[]{:S(2)}) collective-permute-start(bf16[32,768]{1,0:T(8,128)(2,1)S(1)} %shard_map.102), channel_id=1, source_target_pairs={{8,0},{16,8},{24,16},{9,1},{17,9},{25,17},{10,2},{18,10},{26,18},{... | collective-permute-start | bytes 147464 | tf_op jit(solution)/shard_map/ppermute | solution.py:20
  45.3 0.7 %collective-permute-done.15.refs_5_.refs_1_ = bf16[128,384]{1,0:T(8,128)(2,1)S(1)} collective-permute-done((bf16[128,384]{1,0:T(8,128)(2,1)S(1)}, bf16[128,384]{1,0:T(8,128)(2,1)S(1)}, u32[]{:S(2)}, u32[]{:S(2)}) %collective-permute-start.15) | collective-permute-done | bytes 98336 | tf_op jit(solution)/shard_map/ppermute | solution.py:30
  46.1 1.3 %collective-permute-start.18 = (bf16[32,768]{1,0:T(8,128)(2,1)S(1)}, bf16[32,768]{1,0:T(8,128)(2,1)S(1)}, u32[]{:S(2)}, u32[]{:S(2)}) collective-permute-start(bf16[32,768]{1,0:T(8,128)(2,1)S(1)} %shard_map.101), channel_id=1, source_target_pairs={{8,0},{16,8},{24,16},{9,1},{17,9},{25,17},{10,2},{18,10},{26,18},{... | collective-permute-start | bytes 147464 | tf_op jit(solution)/shard_map/ppermute | solution.py:20
  48.1 1.5 %collective-permute-done.13.lead_ref = bf16[32,1536]{1,0:T(8,128)(2,1)S(1)} collective-permute-done((bf16[32,1536]{1,0:T(8,128)(2,1)S(1)}, bf16[32,1536]{1,0:T(8,128)(2,1)S(1)}, u32[]{:S(2)}, u32[]{:S(2)}) %collective-permute-start.13) | collective-permute-done | bytes 98336 | tf_op jit(solution)/shard_map/ppermute | solution.py:20
  49.6 1.4 %shard_map.100 = (bf16[8,16,3072]{2,1,0:T(8,128)(2,1)}, bf16[8,16,3072]{2,1,0:T(8,128)(2,1)}) custom-call(s32[1]{0:T(128)S(6)} %copy.11.offset_ref, f32[1,128]{1,0:T(1,128)S(1)} %shard_map.86.delta_ref, bf16[128,3072]{1,0:T(8,128)(2,1)S(1)} %bitcast.31, bf16[32,1536]{1,0:T(8,128)(2,1)S(1)} %collective-permute-done.13.lead_ref, ...), custom_call_target="tpu_custom_call" | custom-call | flops 786432 | bytes 3145728 | tf_op jit(solution)/shard_map/pallas_call | solution.py:511
  51.0 1.6 %collective-permute-done.18.refs_0_ = bf16[32,768]{1,0:T(8,128)(2,1)S(1)} collective-permute-done((bf16[32,768]{1,0:T(8,128)(2,1)S(1)}, bf16[32,768]{1,0:T(8,128)(2,1)S(1)}, u32[]{:S(2)}, u32[]{:S(2)}) %collective-permute-start.18) | collective-permute-done | bytes 49184 | tf_op jit(solution)/shard_map/ppermute | solution.py:20
  52.6 0.7 %shard_map.103 = bf16[8,16,3072]{2,1,0:T(8,128)(2,1)} custom-call(s32[1]{0:T(128)S(6)} %copy.11.offset_ref, bf16[2,16,3072]{2,1,0:T(8,128)(2,1)S(1)} %copy-done.4, bf16[32,768]{1,0:T(8,128)(2,1)S(1)} %collective-permute-done.18.refs_0_, bf16[32,768]{1,0:T(8,128)(2,1)S(1)} %collective-permute-done.19.refs_1_, ...), custom_call_target="tpu_custom_call", output_to_operand_aliasing={{}: (4, {})} | custom-call | bytes 589824 | tf_op jit(solution)/shard_map/pallas_call | solution.py:550
  (42 shorter events, 1.1 us)
Async XLA Ops:
  2.1 16.6 %collective-permute-start.1 = (bf16[3,128,768]{2,1,0:T(8,128)(2,1)S(1)}, bf16[3,128,768]{2,1,0:T(8,128)(2,1)S(1)}, u32[]{:S(2)}, u32[]{:S(2)}) collective-permute-start(bf16[3,128,768]{2,1,0:T(8,128)(2,1)S(1)} %get-tuple-element.26), channel_id=1, source_target_pairs={{0,2},{1,5},{2,0},{3,7},{4,6},{5,1},{6,4},{7,3},{8,10},{9,13},{10,... | collective-permute-start | bytes 1769480 | tf_op jit(solution)/shard_map/ppermute | solution.py:30
  5.1 16.3 %collective-permute-start.2 = (bf16[3,128,768]{2,1,0:T(8,128)(2,1)S(1)}, bf16[3,128,768]{2,1,0:T(8,128)(2,1)S(1)}, u32[]{:S(2)}, u32[]{:S(2)}) collective-permute-start(bf16[3,128,768]{2,1,0:T(8,128)(2,1)S(1)} %get-tuple-element.27), channel_id=1, source_target_pairs={{0,4},{1,3},{2,6},{3,1},{4,0},{5,7},{6,2},{7,5},{8,12},{9,11},{10,... | collective-permute-start | bytes 1769480 | tf_op jit(solution)/shard_map/ppermute | solution.py:30
  8.1 19.1 %collective-permute-start.9 = (bf16[2,128,768]{2,1,0:T(8,128)(2,1)S(1)}, bf16[2,128,768]{2,1,0:T(8,128)(2,1)S(1)}, u32[]{:S(2)}, u32[]{:S(2)}) collective-permute-start(bf16[2,128,768]{2,1,0:T(8,128)(2,1)S(1)} %get-tuple-element.34), channel_id=1, source_target_pairs={{0,4},{1,5},{2,6},{3,7},{4,0},{5,1},{6,2},{7,3},{8,12},{9,13},{10,... | collective-permute-start | bytes 1179656 | tf_op jit(solution)/shard_map/ppermute | solution.py:24
  8.7 18.6 %collective-permute-start.7 = (bf16[2,128,768]{2,1,0:T(8,128)(2,1)S(1)}, bf16[2,128,768]{2,1,0:T(8,128)(2,1)S(1)}, u32[]{:S(2)}, u32[]{:S(2)}) collective-permute-start(bf16[2,128,768]{2,1,0:T(8,128)(2,1)S(1)} %get-tuple-element.31), channel_id=1, source_target_pairs={{0,2},{1,3},{2,0},{3,1},{4,6},{5,7},{6,4},{7,5},{8,10},{9,11},{10,... | collective-permute-start | bytes 1179656 | tf_op jit(solution)/shard_map/ppermute | solution.py:24
  21.5 1.6 %collective-permute-start.6 = (bf16[3,128,384]{2,1,0:T(8,128)(2,1)S(1)}, bf16[3,128,384]{2,1,0:T(8,128)(2,1)S(1)}, u32[]{:S(2)}, u32[]{:S(2)}) collective-permute-start(bf16[3,128,384]{2,1,0:T(8,128)(2,1)S(1)} %shard_map.92), channel_id=1, source_target_pairs={{0,1},{1,0},{2,3},{3,2},{4,5},{5,4},{6,7},{7,6},{8,9},{9,8},{10,11... | collective-permute-start | bytes 884744 | tf_op jit(solution)/shard_map/ppermute | solution.py:24
  21.6 1.9 %collective-permute-start.3 = (bf16[3,128,384]{2,1,0:T(8,128)(2,1)S(1)}, bf16[3,128,384]{2,1,0:T(8,128)(2,1)S(1)}, u32[]{:S(2)}, u32[]{:S(2)}) collective-permute-start(bf16[3,128,384]{2,1,0:T(8,128)(2,1)S(1)} %shard_map.90), channel_id=1, source_target_pairs={{0,1},{1,0},{2,3},{3,2},{4,5},{5,4},{6,7},{7,6},{8,9},{9,8},{10,11... | collective-permute-start | bytes 884744 | tf_op jit(solution)/shard_map/ppermute | solution.py:24
  22.1 6.2 %collective-permute-start = (bf16[3,128,384]{2,1,0:T(8,128)(2,1)S(1)}, bf16[3,128,384]{2,1,0:T(8,128)(2,1)S(1)}, u32[]{:S(2)}, u32[]{:S(2)}) collective-permute-start(bf16[3,128,384]{2,1,0:T(8,128)(2,1)S(1)} %get-tuple-element.25), channel_id=1, source_target_pairs={{0,1},{1,0},{2,3},{3,2},{4,5},{5,4},{6,7},{7,6},{8,9},{9,8},{10,11... | collective-permute-start | bytes 884744 | tf_op jit(solution)/shard_map/ppermute | solution.py:24
  23.1 5.9 %copy-start.3 = (bf16[1,8,16,3072]{3,2,1,0:T(8,128)(2,1)S(1)}, bf16[1,8,16,3072]{3,2,1,0:T(8,128)(2,1)}, u32[]{:S(2)}) copy-start(bf16[1,8,16,3072]{3,2,1,0:T(8,128)(2,1)} %param.7) | copy-start | bytes 2359300
  23.2 12.4 %collective-permute-start.11 = (bf16[2,256,384]{2,1,0:T(8,128)(2,1)S(1)}, bf16[2,256,384]{2,1,0:T(8,128)(2,1)S(1)}, u32[]{:S(2)}, u32[]{:S(2)}) collective-permute-start(bf16[2,256,384]{2,1,0:T(8,128)(2,1)S(1)} %shard_map.97), channel_id=1, source_target_pairs={{0,2},{1,3},{2,0},{3,1},{4,6},{5,7},{6,4},{7,5},{8,10},{9,11},{10,... | collective-permute-start | bytes 1179656 | tf_op jit(solution)/shard_map/ppermute | solution.py:24
  23.5 4.9 %copy-start.5 = (s32[4]{0:T(128)S(1)}, s32[4]{0:T(128)}, u32[]{:S(2)}) copy-start(s32[4]{0:T(128)} %timesteps_ref.1) | copy-start | bytes 52
  23.5 5.9 %copy-start.2 = (bf16[1,8,16,3072]{3,2,1,0:T(8,128)(2,1)S(1)}, bf16[1,8,16,3072]{3,2,1,0:T(8,128)(2,1)}, u32[]{:S(2)}) copy-start(bf16[1,8,16,3072]{3,2,1,0:T(8,128)(2,1)} %param.10) | copy-start | bytes 2359300
  23.6 11.9 %collective-permute-start.4 = (bf16[2,256,384]{2,1,0:T(8,128)(2,1)S(1)}, bf16[2,256,384]{2,1,0:T(8,128)(2,1)S(1)}, u32[]{:S(2)}, u32[]{:S(2)}) collective-permute-start(bf16[2,256,384]{2,1,0:T(8,128)(2,1)S(1)} %shard_map.91), channel_id=1, source_target_pairs={{0,4},{1,5},{2,6},{3,7},{4,0},{5,1},{6,2},{7,3},{8,12},{9,13},{10,... | collective-permute-start | bytes 1179656 | tf_op jit(solution)/shard_map/ppermute | solution.py:24
  27.2 2.2 %copy-start = (bf16[1,8,16,3072]{3,2,1,0:T(8,128)(2,1)S(1)}, bf16[1,8,16,3072]{3,2,1,0:T(8,128)(2,1)}, u32[]{:S(2)}) copy-start(bf16[1,8,16,3072]{3,2,1,0:T(8,128)(2,1)} %param.8) | copy-start | bytes 2359300
  27.2 2.2 %copy-start.1 = (bf16[1,8,16,3072]{3,2,1,0:T(8,128)(2,1)S(1)}, bf16[1,8,16,3072]{3,2,1,0:T(8,128)(2,1)}, u32[]{:S(2)}) copy-start(bf16[1,8,16,3072]{3,2,1,0:T(8,128)(2,1)} %param.9) | copy-start | bytes 2359300
  27.2 4.0 %collective-permute-start.5 = (bf16[3,128,384]{2,1,0:T(8,128)(2,1)S(1)}, bf16[3,128,384]{2,1,0:T(8,128)(2,1)S(1)}, u32[]{:S(2)}, u32[]{:S(2)}) collective-permute-start(bf16[3,128,384]{2,1,0:T(8,128)(2,1)S(1)} %get-tuple-element.29), channel_id=1, source_target_pairs={{0,1},{1,0},{2,3},{3,2},{4,5},{5,4},{6,7},{7,6},{8,9},{9,8},{10,11... | collective-permute-start | bytes 884744 | tf_op jit(solution)/shard_map/ppermute | solution.py:24
  27.2 2.2 %collective-permute-start.10 = (bf16[2,128,384]{2,1,0:T(8,128)(2,1)S(1)}, bf16[2,128,384]{2,1,0:T(8,128)(2,1)S(1)}, u32[]{:S(2)}, u32[]{:S(2)}) collective-permute-start(bf16[2,128,384]{2,1,0:T(8,128)(2,1)S(1)} %shard_map.95), channel_id=1, source_target_pairs={{0,1},{1,0},{2,3},{3,2},{4,5},{5,4},{6,7},{7,6},{8,9},{9,8},{10,11... | collective-permute-start | bytes 589832 | tf_op jit(solution)/shard_map/ppermute | solution.py:24
  28.4 2.9 %collective-permute-start.8 = (bf16[2,128,384]{2,1,0:T(8,128)(2,1)S(1)}, bf16[2,128,384]{2,1,0:T(8,128)(2,1)S(1)}, u32[]{:S(2)}, u32[]{:S(2)}) collective-permute-start(bf16[2,128,384]{2,1,0:T(8,128)(2,1)S(1)} %shard_map.93), channel_id=1, source_target_pairs={{0,1},{1,0},{2,3},{3,2},{4,5},{5,4},{6,7},{7,6},{8,9},{9,8},{10,11... | collective-permute-start | bytes 589832 | tf_op jit(solution)/shard_map/ppermute | solution.py:24
  37.2 6.2 %collective-permute-start.16 = (bf16[128,384]{1,0:T(8,128)(2,1)S(1)}, bf16[128,384]{1,0:T(8,128)(2,1)S(1)}, u32[]{:S(2)}, u32[]{:S(2)}) collective-permute-start(bf16[128,384]{1,0:T(8,128)(2,1)S(1)} %get-tuple-element.50), channel_id=1, source_target_pairs={{0,4},{1,3},{2,6},{3,1},{4,0},{5,7},{6,2},{7,5},{8,12},{9,11},{10,... | collective-permute-start | bytes 294920 | tf_op jit(solution)/shard_map/ppermute | solution.py:30
  38.8 3.1 %collective-permute-start.12 = (bf16[256,384]{1,0:T(8,128)(2,1)S(1)}, bf16[256,384]{1,0:T(8,128)(2,1)S(1)}, u32[]{:S(2)}, u32[]{:S(2)}) collective-permute-start(bf16[256,384]{1,0:T(8,128)(2,1)S(1)} %get-tuple-element.42), channel_id=1, source_target_pairs={{0,1},{1,0},{2,3},{3,2},{4,5},{5,4},{6,7},{7,6},{8,9},{9,8},{10,11... | collective-permute-start | bytes 589832 | tf_op jit(solution)/shard_map/ppermute | solution.py:24
  39.6 4.3 %collective-permute-start.17 = (bf16[128,384]{1,0:T(8,128)(2,1)S(1)}, bf16[128,384]{1,0:T(8,128)(2,1)S(1)}, u32[]{:S(2)}, u32[]{:S(2)}) collective-permute-start(bf16[128,384]{1,0:T(8,128)(2,1)S(1)} %get-tuple-element.48), channel_id=1, source_target_pairs={{0,5},{1,2},{2,7},{3,0},{4,1},{5,6},{6,3},{7,4},{8,13},{9,10},{10,... | collective-permute-start | bytes 294920 | tf_op jit(solution)/shard_map/ppermute | solution.py:30
  39.7 5.6 %collective-permute-start.14 = (bf16[128,384]{1,0:T(8,128)(2,1)S(1)}, bf16[128,384]{1,0:T(8,128)(2,1)S(1)}, u32[]{:S(2)}, u32[]{:S(2)}) collective-permute-start(bf16[128,384]{1,0:T(8,128)(2,1)S(1)} %get-tuple-element.51), channel_id=1, source_target_pairs={{0,2},{1,5},{2,0},{3,7},{4,6},{5,1},{6,4},{7,3},{8,10},{9,13},{10,... | collective-permute-start | bytes 294920 | tf_op jit(solution)/shard_map/ppermute | solution.py:30
  42.0 4.0 %collective-permute-start.15 = (bf16[128,384]{1,0:T(8,128)(2,1)S(1)}, bf16[128,384]{1,0:T(8,128)(2,1)S(1)}, u32[]{:S(2)}, u32[]{:S(2)}) collective-permute-start(bf16[128,384]{1,0:T(8,128)(2,1)S(1)} %get-tuple-element.49), channel_id=1, source_target_pairs={{0,3},{1,4},{2,1},{3,6},{4,7},{5,0},{6,5},{7,2},{8,11},{9,12},{10,... | collective-permute-start | bytes 294920 | tf_op jit(solution)/shard_map/ppermute | solution.py:30
  42.1 7.4 %collective-permute-start.13 = (bf16[32,1536]{1,0:T(8,128)(2,1)S(1)}, bf16[32,1536]{1,0:T(8,128)(2,1)S(1)}, u32[]{:S(2)}, u32[]{:S(2)}) collective-permute-start(bf16[32,1536]{1,0:T(8,128)(2,1)S(1)} %shard_map.99), channel_id=1, source_target_pairs={{8,0},{16,8},{24,16},{9,1},{17,9},{25,17},{10,2},{18,10},{26,18},{... | collective-permute-start | bytes 294920 | tf_op jit(solution)/shard_map/ppermute | solution.py:20
  44.0 7.0 %collective-permute-start.19 = (bf16[32,768]{1,0:T(8,128)(2,1)S(1)}, bf16[32,768]{1,0:T(8,128)(2,1)S(1)}, u32[]{:S(2)}, u32[]{:S(2)}) collective-permute-start(bf16[32,768]{1,0:T(8,128)(2,1)S(1)} %shard_map.102), channel_id=1, source_target_pairs={{8,0},{16,8},{24,16},{9,1},{17,9},{25,17},{10,2},{18,10},{26,18},{... | collective-permute-start | bytes 147464 | tf_op jit(solution)/shard_map/ppermute | solution.py:20
  46.1 6.5 %collective-permute-start.18 = (bf16[32,768]{1,0:T(8,128)(2,1)S(1)}, bf16[32,768]{1,0:T(8,128)(2,1)S(1)}, u32[]{:S(2)}, u32[]{:S(2)}) collective-permute-start(bf16[32,768]{1,0:T(8,128)(2,1)S(1)} %shard_map.101), channel_id=1, source_target_pairs={{8,0},{16,8},{24,16},{9,1},{17,9},{25,17},{10,2},{18,10},{26,18},{... | collective-permute-start | bytes 147464 | tf_op jit(solution)/shard_map/ppermute | solution.py:20
  49.5 3.0 %copy-start.4 = (bf16[2,16,3072]{2,1,0:T(8,128)(2,1)S(1)}, bf16[2,16,3072]{2,1,0:T(8,128)(2,1)}, u32[]{:S(2)}) copy-start(bf16[2,16,3072]{2,1,0:T(8,128)(2,1)} %fresh_ref.1) | copy-start | bytes 589828

commit v7 on v6

--- a/solution.py
+++ b/solution.py
@@ -281,12 +281,16 @@
         top = jnp.maximum(top, before[1])
     tops = jnp.concatenate([top] * (scores[0].shape[1] // HEAD_SIZE), axis=1)
     weights = [jnp.exp2((part - tops) * factor) for part in scores]
-    total = jnp.sum(functools.reduce(jnp.add, weights), axis=-1, keepdims=True)
-    total = jnp.broadcast_to(total, shape)
+    ones = jnp.ones(values[0].shape, jnp.bfloat16)
     mixed = sum(
-        jnp.dot(weight.astype(jnp.bfloat16), value, preferred_element_type=jnp.float32)
+        jnp.dot(
+            weight.astype(jnp.bfloat16),
+            jnp.concatenate([value, ones], axis=1),
+            preferred_element_type=jnp.float32,
+        )
         for weight, value in zip(weights, values)
     )
+    mixed, total = mixed[:, :HEAD_SIZE], mixed[:, HEAD_SIZE:]
     if before is not None:
         keep = jnp.exp2((before[1] - top) * factor)
         mixed = mixed + keep * before[0]

time: 53.5 us -> 53.4 us (level)
  no operation moved by 1% of the time
where the time goes in v7:
time: 53.4 us; the launch traced here: 53.2 us
  waiting for transfers between devices  22.7 us (43%)
  starting transfers between devices  17.6 us (33%)
  Pallas kernels  11.2 us (21%)
  between operations  1.54 us (3%)
    ppermute x6, waiting for transfers between devices, crossed(): lax.ppermute(block, 'seq', [(i, i ^ bits[i % 2] ^ other) for i in devices])  13.8 us
    ppermute x6, starting transfers between devices, crossed(): lax.ppermute(block, 'seq', [(i, i ^ bits[i % 2] ^ other) for i in devices])  8.51 us
    ppermute x11, waiting for transfers between devices, swapped(): lax.ppermute(block, 'seq', [(i, i ^ bit) for i in range(lax.axis_size('se...  5.87 us
    ppermute x11, starting transfers between devices, swapped(): lax.ppermute(block, 'seq', [(i, i ^ bit) for i in range(lax.axis_size('se...  5.22 us
    ppermute x3, starting transfers between devices, shifted(): return lax.ppermute(block, axis, route)  3.88 us
    pallas_call x2, Pallas kernels, attend(): call(functools.partial(attend_kernel, side), (out,) * 3, [VMEM] * 8, (VME...  3.52 us
    ppermute x3, waiting for transfers between devices, shifted(): return lax.ppermute(block, axis, route)  3.06 us
    pallas_call x2, Pallas kernels, pack(): call(functools.partial(pack_kernel, cuts), outs, [HBM] * 3, (VMEM,) * len...  2.92 us
  transfers between devices with their start and end apart: 20, of which 11 were waited for; matrix products, arithmetic and copies ran while one was open for 0% of the time, Pallas kernels for 14%

profile of v7, /device:TPU:0, one launch (start us, length us, event | category | flops | bytes accessed | tf_op | source)
XLA Modules:
  0.0 53.2 jit_solution(5039558508596303591)
XLA Ops:
  0.6 1.4 %shard_map.88 = (bf16[3,128,768]{2,1,0:T(8,128)(2,1)S(1)}, bf16[3,128,768]{2,1,0:T(8,128)(2,1)S(1)}) custom-call(bf16[128,3072]{1,0:T(8,128)(2,1)} %bitcast.20, bf16[128,3072]{1,0:T(8,128)(2,1)} %bitcast.24, bf16[128,3072]{1,0:T(8,128)(2,1)} %bitcast.15), custom_call_target="tpu_custom_call" | custom-call | bytes 2359296 | tf_op jit(solution)/shard_map/pallas_call | solution.py:211
  2.1 3.0 %collective-permute-start.1 = (bf16[3,128,768]{2,1,0:T(8,128)(2,1)S(1)}, bf16[3,128,768]{2,1,0:T(8,128)(2,1)S(1)}, u32[]{:S(2)}, u32[]{:S(2)}) collective-permute-start(bf16[3,128,768]{2,1,0:T(8,128)(2,1)S(1)} %get-tuple-element.26), channel_id=1, source_target_pairs={{0,2},{1,5},{2,0},{3,7},{4,6},{5,1},{6,4},{7,3},{8,10},{9,13},{10,... | collective-permute-start | bytes 1769480 | tf_op jit(solution)/shard_map/ppermute | solution.py:30
  5.1 1.5 %collective-permute-start.2 = (bf16[3,128,768]{2,1,0:T(8,128)(2,1)S(1)}, bf16[3,128,768]{2,1,0:T(8,128)(2,1)S(1)}, u32[]{:S(2)}, u32[]{:S(2)}) collective-permute-start(bf16[3,128,768]{2,1,0:T(8,128)(2,1)S(1)} %get-tuple-element.27), channel_id=1, source_target_pairs={{0,4},{1,3},{2,6},{3,1},{4,0},{5,7},{6,2},{7,5},{8,12},{9,11},{10,... | collective-permute-start | bytes 1769480 | tf_op jit(solution)/shard_map/ppermute | solution.py:30
  6.6 1.5 %shard_map.87 = (bf16[2,128,768]{2,1,0:T(8,128)(2,1)S(1)}, bf16[2,128,768]{2,1,0:T(8,128)(2,1)S(1)}, bf16[3,128,384]{2,1,0:T(8,128)(2,1)S(1)}, bf16[3,128,384]{2,1,0:T(8,128)(2,1)S(1)}) custom-call(bf16[128,3072]{1,0:T(8,128)(2,1)} %bitcast.21, bf16[128,3072]{1,0:T(8,128)(2,1)} %bitcast.25, bf16[128,3072]{1,0:T(8,128)(2,1)} %bitcast.16), custom_call_target="tpu_custom_call" | custom-call | bytes 2752512 | tf_op jit(solution)/shard_map/pallas_call | solution.py:211
  8.1 0.6 %collective-permute-start.9 = (bf16[2,128,768]{2,1,0:T(8,128)(2,1)S(1)}, bf16[2,128,768]{2,1,0:T(8,128)(2,1)S(1)}, u32[]{:S(2)}, u32[]{:S(2)}) collective-permute-start(bf16[2,128,768]{2,1,0:T(8,128)(2,1)S(1)} %get-tuple-element.34), channel_id=1, source_target_pairs={{0,4},{1,5},{2,6},{3,7},{4,0},{5,1},{6,2},{7,3},{8,12},{9,13},{10,... | collective-permute-start | bytes 1179656 | tf_op jit(solution)/shard_map/ppermute | solution.py:24
  8.7 0.1 collective-permute-start.7
  8.8 9.9 %collective-permute-done.1.refs_0_ = bf16[3,128,768]{2,1,0:T(8,128)(2,1)S(1)} collective-permute-done((bf16[3,128,768]{2,1,0:T(8,128)(2,1)S(1)}, bf16[3,128,768]{2,1,0:T(8,128)(2,1)S(1)}, u32[]{:S(2)}, u32[]{:S(2)}) %collective-permute-start.1) | collective-permute-done | bytes 589856 | tf_op jit(solution)/shard_map/ppermute | solution.py:30
  18.7 2.7 %collective-permute-done.2.refs_1_ = bf16[3,128,768]{2,1,0:T(8,128)(2,1)S(1)} collective-permute-done((bf16[3,128,768]{2,1,0:T(8,128)(2,1)S(1)}, bf16[3,128,768]{2,1,0:T(8,128)(2,1)S(1)}, u32[]{:S(2)}, u32[]{:S(2)}) %collective-permute-start.2) | collective-permute-done | bytes 589856 | tf_op jit(solution)/shard_map/ppermute | solution.py:30
  21.6 0.5 %collective-permute-start.3 = (bf16[3,128,384]{2,1,0:T(8,128)(2,1)S(1)}, bf16[3,128,384]{2,1,0:T(8,128)(2,1)S(1)}, u32[]{:S(2)}, u32[]{:S(2)}) collective-permute-start(bf16[3,128,384]{2,1,0:T(8,128)(2,1)S(1)} %shard_map.90), channel_id=1, source_target_pairs={{0,1},{1,0},{2,3},{3,2},{4,5},{5,4},{6,7},{7,6},{8,9},{9,8},{10,11... | collective-permute-start | bytes 884744 | tf_op jit(solution)/shard_map/ppermute | solution.py:24
  22.2 0.9 %collective-permute-done.6.got_core_ref.core_ref.refs_9_ = bf16[3,128,384]{2,1,0:T(8,128)(2,1)S(1)} collective-permute-done((bf16[3,128,384]{2,1,0:T(8,128)(2,1)S(1)}, bf16[3,128,384]{2,1,0:T(8,128)(2,1)S(1)}, u32[]{:S(2)}, u32[]{:S(2)}) %collective-permute-start.6) | collective-permute-done | bytes 294944 | tf_op jit(solution)/shard_map/ppermute | solution.py:24
  23.3 0.3 collective-permute-done.3.core_ref.got_core_ref.refs_2_
  23.6 1.8 %collective-permute-start.4 = (bf16[2,256,384]{2,1,0:T(8,128)(2,1)S(1)}, bf16[2,256,384]{2,1,0:T(8,128)(2,1)S(1)}, u32[]{:S(2)}, u32[]{:S(2)}) collective-permute-start(bf16[2,256,384]{2,1,0:T(8,128)(2,1)S(1)} %shard_map.91), channel_id=1, source_target_pairs={{0,4},{1,5},{2,6},{3,7},{4,0},{5,1},{6,2},{7,3},{8,12},{9,13},{10,... | collective-permute-start | bytes 1179656 | tf_op jit(solution)/shard_map/ppermute | solution.py:24
  25.4 1.8 %collective-permute-done.9.got_ref.far_ref = bf16[2,128,768]{2,1,0:T(8,128)(2,1)S(1)} collective-permute-done((bf16[2,128,768]{2,1,0:T(8,128)(2,1)S(1)}, bf16[2,128,768]{2,1,0:T(8,128)(2,1)S(1)}, u32[]{:S(2)}, u32[]{:S(2)}) %collective-permute-start.9) | collective-permute-done | bytes 393248 | tf_op jit(solution)/shard_map/ppermute | solution.py:24
  27.2 1.1 %collective-permute-start.10 = (bf16[2,128,384]{2,1,0:T(8,128)(2,1)S(1)}, bf16[2,128,384]{2,1,0:T(8,128)(2,1)S(1)}, u32[]{:S(2)}, u32[]{:S(2)}) collective-permute-start(bf16[2,128,384]{2,1,0:T(8,128)(2,1)S(1)} %shard_map.95), channel_id=1, source_target_pairs={{0,1},{1,0},{2,3},{3,2},{4,5},{5,4},{6,7},{7,6},{8,9},{9,8},{10,11... | collective-permute-start | bytes 589832 | tf_op jit(solution)/shard_map/ppermute | solution.py:24
  28.5 0.6 %shard_map.86.delta_ref = f32[1,128]{1,0:T(1,128)S(1)} custom-call(s32[4]{0:T(128)S(1)} %copy-done.5), custom_call_target="tpu_custom_call" | custom-call | tf_op jit(solution)/shard_map/pallas_call | solution.py:186
  29.1 0.4 collective-permute-done.10.far_core_ref
  29.4 1.8 %shard_map.96 = (f32[512,384]{1,0:T(8,128)S(1)}, f32[512,384]{1,0:T(8,128)S(1)}, f32[512,384]{1,0:T(8,128)S(1)}) custom-call(bf16[128,3072]{1,0:T(8,128)(2,1)S(1)} %bitcast.22, bf16[128,3072]{1,0:T(8,128)(2,1)S(1)} %bitcast.26, bf16[128,3072]{1,0:T(8,128)(2,1)S(1)} %bitcast.17, bf16[3,128,384]{2,1,0:T(8,128)(2,1)S(1)} %collective-permute-done.core_ref.refs_0_, ...), custom_call_target="tpu_custom_call" | custom-call | flops 603979776 | bytes 3145728 | tf_op jit(solution)/shard_map/pallas_call | solution.py:354
  31.2 1.8 %shard_map.94 = (f32[512,384]{1,0:T(8,128)S(1)}, f32[512,384]{1,0:T(8,128)S(1)}, f32[512,384]{1,0:T(8,128)S(1)}) custom-call(bf16[128,3072]{1,0:T(8,128)(2,1)S(1)} %bitcast.23, bf16[128,3072]{1,0:T(8,128)(2,1)S(1)} %bitcast.27, bf16[128,3072]{1,0:T(8,128)(2,1)S(1)} %bitcast.18, bf16[3,128,384]{2,1,0:T(8,128)(2,1)S(1)} %collective-permute-done.5.core_ref.refs_7_, ...), custom_call_target="tpu_custom_call" | custom-call | flops 603979776 | bytes 3145728 | tf_op jit(solution)/shard_map/pallas_call | solution.py:354
  33.0 2.5 %collective-permute-done.11.refs_10_ = bf16[2,256,384]{2,1,0:T(8,128)(2,1)S(1)} collective-permute-done((bf16[2,256,384]{2,1,0:T(8,128)(2,1)S(1)}, bf16[2,256,384]{2,1,0:T(8,128)(2,1)S(1)}, u32[]{:S(2)}, u32[]{:S(2)}) %collective-permute-start.11) | collective-permute-done | bytes 393248 | tf_op jit(solution)/shard_map/ppermute | solution.py:24
  35.5 1.6 %shard_map.98 = (bf16[256,384]{1,0:T(8,128)(2,1)S(1)}, bf16[2,128,384]{2,1,0:T(8,128)(2,1)S(1)}, bf16[2,128,384]{2,1,0:T(8,128)(2,1)S(1)}, bf16[128,384]{1,0:T(8,128)(2,1)S(1)}, bf16[128,384]{1,0:T(8,128)(2,1)S(1)}) custom-call(bf16[128,3072]{1,0:T(8,128)(2,1)S(1)} %bitcast.19, bf16[3,128,384]{2,1,0:T(8,128)(2,1)S(1)} %collective-permute-done.core_ref.refs_0_, ...), custom_call_target="tpu_custom_call" | custom-call | flops 402653184 | bytes 6291456 | tf_op jit(solution)/shard_map/pallas_call | solution.py:411
  37.1 1.6 %collective-permute-start.16 = (bf16[128,384]{1,0:T(8,128)(2,1)S(1)}, bf16[128,384]{1,0:T(8,128)(2,1)S(1)}, u32[]{:S(2)}, u32[]{:S(2)}) collective-permute-start(bf16[128,384]{1,0:T(8,128)(2,1)S(1)} %get-tuple-element.50), channel_id=1, source_target_pairs={{0,4},{1,3},{2,6},{3,1},{4,0},{5,7},{6,2},{7,5},{8,12},{9,11},{10,... | collective-permute-start | bytes 294920 | tf_op jit(solution)/shard_map/ppermute | solution.py:30
  38.7 0.8 %collective-permute-start.12 = (bf16[256,384]{1,0:T(8,128)(2,1)S(1)}, bf16[256,384]{1,0:T(8,128)(2,1)S(1)}, u32[]{:S(2)}, u32[]{:S(2)}) collective-permute-start(bf16[256,384]{1,0:T(8,128)(2,1)S(1)} %get-tuple-element.42), channel_id=1, source_target_pairs={{0,1},{1,0},{2,3},{3,2},{4,5},{5,4},{6,7},{7,6},{8,9},{9,8},{10,11... | collective-permute-start | bytes 589832 | tf_op jit(solution)/shard_map/ppermute | solution.py:24
  39.6 2.3 %collective-permute-start.14 = (bf16[128,384]{1,0:T(8,128)(2,1)S(1)}, bf16[128,384]{1,0:T(8,128)(2,1)S(1)}, u32[]{:S(2)}, u32[]{:S(2)}) collective-permute-start(bf16[128,384]{1,0:T(8,128)(2,1)S(1)} %get-tuple-element.51), channel_id=1, source_target_pairs={{0,2},{1,5},{2,0},{3,7},{4,6},{5,1},{6,4},{7,3},{8,10},{9,13},{10,... | collective-permute-start | bytes 294920 | tf_op jit(solution)/shard_map/ppermute | solution.py:30
  42.0 1.3 %collective-permute-start.13 = (bf16[32,1536]{1,0:T(8,128)(2,1)S(1)}, bf16[32,1536]{1,0:T(8,128)(2,1)S(1)}, u32[]{:S(2)}, u32[]{:S(2)}) collective-permute-start(bf16[32,1536]{1,0:T(8,128)(2,1)S(1)} %shard_map.99), channel_id=1, source_target_pairs={{8,0},{16,8},{24,16},{9,1},{17,9},{25,17},{10,2},{18,10},{26,18},{... | collective-permute-start | bytes 294920 | tf_op jit(solution)/shard_map/ppermute | solution.py:20
  43.3 0.5 collective-permute-done.17.refs_7_.refs_1_
  43.9 1.3 %collective-permute-start.19 = (bf16[32,768]{1,0:T(8,128)(2,1)S(1)}, bf16[32,768]{1,0:T(8,128)(2,1)S(1)}, u32[]{:S(2)}, u32[]{:S(2)}) collective-permute-start(bf16[32,768]{1,0:T(8,128)(2,1)S(1)} %shard_map.102), channel_id=1, source_target_pairs={{8,0},{16,8},{24,16},{9,1},{17,9},{25,17},{10,2},{18,10},{26,18},{... | collective-permute-start | bytes 147464 | tf_op jit(solution)/shard_map/ppermute | solution.py:20
  45.2 0.7 %collective-permute-done.15.refs_5_.refs_1_ = bf16[128,384]{1,0:T(8,128)(2,1)S(1)} collective-permute-done((bf16[128,384]{1,0:T(8,128)(2,1)S(1)}, bf16[128,384]{1,0:T(8,128)(2,1)S(1)}, u32[]{:S(2)}, u32[]{:S(2)}) %collective-permute-start.15) | collective-permute-done | bytes 98336 | tf_op jit(solution)/shard_map/ppermute | solution.py:30
  46.0 1.3 %collective-permute-start.18 = (bf16[32,768]{1,0:T(8,128)(2,1)S(1)}, bf16[32,768]{1,0:T(8,128)(2,1)S(1)}, u32[]{:S(2)}, u32[]{:S(2)}) collective-permute-start(bf16[32,768]{1,0:T(8,128)(2,1)S(1)} %shard_map.101), channel_id=1, source_target_pairs={{8,0},{16,8},{24,16},{9,1},{17,9},{25,17},{10,2},{18,10},{26,18},{... | collective-permute-start | bytes 147464 | tf_op jit(solution)/shard_map/ppermute | solution.py:20
  48.0 1.5 %collective-permute-done.13.lead_ref = bf16[32,1536]{1,0:T(8,128)(2,1)S(1)} collective-permute-done((bf16[32,1536]{1,0:T(8,128)(2,1)S(1)}, bf16[32,1536]{1,0:T(8,128)(2,1)S(1)}, u32[]{:S(2)}, u32[]{:S(2)}) %collective-permute-start.13) | collective-permute-done | bytes 98336 | tf_op jit(solution)/shard_map/ppermute | solution.py:20
  49.4 1.4 %shard_map.100 = (bf16[8,16,3072]{2,1,0:T(8,128)(2,1)}, bf16[8,16,3072]{2,1,0:T(8,128)(2,1)}) custom-call(s32[1]{0:T(128)S(6)} %copy.11.offset_ref, f32[1,128]{1,0:T(1,128)S(1)} %shard_map.86.delta_ref, bf16[128,3072]{1,0:T(8,128)(2,1)S(1)} %bitcast.31, bf16[32,1536]{1,0:T(8,128)(2,1)S(1)} %collective-permute-done.13.lead_ref, ...), custom_call_target="tpu_custom_call" | custom-call | flops 786432 | bytes 3145728 | tf_op jit(solution)/shard_map/pallas_call | solution.py:515
  50.9 1.6 %collective-permute-done.18.refs_0_ = bf16[32,768]{1,0:T(8,128)(2,1)S(1)} collective-permute-done((bf16[32,768]{1,0:T(8,128)(2,1)S(1)}, bf16[32,768]{1,0:T(8,128)(2,1)S(1)}, u32[]{:S(2)}, u32[]{:S(2)}) %collective-permute-start.18) | collective-permute-done | bytes 49184 | tf_op jit(solution)/shard_map/ppermute | solution.py:20
  52.5 0.7 %shard_map.103 = bf16[8,16,3072]{2,1,0:T(8,128)(2,1)} custom-call(s32[1]{0:T(128)S(6)} %copy.11.offset_ref, bf16[2,16,3072]{2,1,0:T(8,128)(2,1)S(1)} %copy-done.4, bf16[32,768]{1,0:T(8,128)(2,1)S(1)} %collective-permute-done.18.refs_0_, bf16[32,768]{1,0:T(8,128)(2,1)S(1)} %collective-permute-done.19.refs_1_, ...), custom_call_target="tpu_custom_call", output_to_operand_aliasing={{}: (4, {})} | custom-call | bytes 589824 | tf_op jit(solution)/shard_map/pallas_call | solution.py:554
  (42 shorter events, 1.1 us)
Async XLA Ops:
  2.1 16.6 %collective-permute-start.1 = (bf16[3,128,768]{2,1,0:T(8,128)(2,1)S(1)}, bf16[3,128,768]{2,1,0:T(8,128)(2,1)S(1)}, u32[]{:S(2)}, u32[]{:S(2)}) collective-permute-start(bf16[3,128,768]{2,1,0:T(8,128)(2,1)S(1)} %get-tuple-element.26), channel_id=1, source_target_pairs={{0,2},{1,5},{2,0},{3,7},{4,6},{5,1},{6,4},{7,3},{8,10},{9,13},{10,... | collective-permute-start | bytes 1769480 | tf_op jit(solution)/shard_map/ppermute | solution.py:30
  5.1 16.3 %collective-permute-start.2 = (bf16[3,128,768]{2,1,0:T(8,128)(2,1)S(1)}, bf16[3,128,768]{2,1,0:T(8,128)(2,1)S(1)}, u32[]{:S(2)}, u32[]{:S(2)}) collective-permute-start(bf16[3,128,768]{2,1,0:T(8,128)(2,1)S(1)} %get-tuple-element.27), channel_id=1, source_target_pairs={{0,4},{1,3},{2,6},{3,1},{4,0},{5,7},{6,2},{7,5},{8,12},{9,11},{10,... | collective-permute-start | bytes 1769480 | tf_op jit(solution)/shard_map/ppermute | solution.py:30
  8.1 19.1 %collective-permute-start.9 = (bf16[2,128,768]{2,1,0:T(8,128)(2,1)S(1)}, bf16[2,128,768]{2,1,0:T(8,128)(2,1)S(1)}, u32[]{:S(2)}, u32[]{:S(2)}) collective-permute-start(bf16[2,128,768]{2,1,0:T(8,128)(2,1)S(1)} %get-tuple-element.34), channel_id=1, source_target_pairs={{0,4},{1,5},{2,6},{3,7},{4,0},{5,1},{6,2},{7,3},{8,12},{9,13},{10,... | collective-permute-start | bytes 1179656 | tf_op jit(solution)/shard_map/ppermute | solution.py:24
  8.7 18.6 %collective-permute-start.7 = (bf16[2,128,768]{2,1,0:T(8,128)(2,1)S(1)}, bf16[2,128,768]{2,1,0:T(8,128)(2,1)S(1)}, u32[]{:S(2)}, u32[]{:S(2)}) collective-permute-start(bf16[2,128,768]{2,1,0:T(8,128)(2,1)S(1)} %get-tuple-element.31), channel_id=1, source_target_pairs={{0,2},{1,3},{2,0},{3,1},{4,6},{5,7},{6,4},{7,5},{8,10},{9,11},{10,... | collective-permute-start | bytes 1179656 | tf_op jit(solution)/shard_map/ppermute | solution.py:24
  21.5 1.6 %collective-permute-start.6 = (bf16[3,128,384]{2,1,0:T(8,128)(2,1)S(1)}, bf16[3,128,384]{2,1,0:T(8,128)(2,1)S(1)}, u32[]{:S(2)}, u32[]{:S(2)}) collective-permute-start(bf16[3,128,384]{2,1,0:T(8,128)(2,1)S(1)} %shard_map.92), channel_id=1, source_target_pairs={{0,1},{1,0},{2,3},{3,2},{4,5},{5,4},{6,7},{7,6},{8,9},{9,8},{10,11... | collective-permute-start | bytes 884744 | tf_op jit(solution)/shard_map/ppermute | solution.py:24
  21.6 1.9 %collective-permute-start.3 = (bf16[3,128,384]{2,1,0:T(8,128)(2,1)S(1)}, bf16[3,128,384]{2,1,0:T(8,128)(2,1)S(1)}, u32[]{:S(2)}, u32[]{:S(2)}) collective-permute-start(bf16[3,128,384]{2,1,0:T(8,128)(2,1)S(1)} %shard_map.90), channel_id=1, source_target_pairs={{0,1},{1,0},{2,3},{3,2},{4,5},{5,4},{6,7},{7,6},{8,9},{9,8},{10,11... | collective-permute-start | bytes 884744 | tf_op jit(solution)/shard_map/ppermute | solution.py:24
  22.1 6.2 %collective-permute-start = (bf16[3,128,384]{2,1,0:T(8,128)(2,1)S(1)}, bf16[3,128,384]{2,1,0:T(8,128)(2,1)S(1)}, u32[]{:S(2)}, u32[]{:S(2)}) collective-permute-start(bf16[3,128,384]{2,1,0:T(8,128)(2,1)S(1)} %get-tuple-element.25), channel_id=1, source_target_pairs={{0,1},{1,0},{2,3},{3,2},{4,5},{5,4},{6,7},{7,6},{8,9},{9,8},{10,11... | collective-permute-start | bytes 884744 | tf_op jit(solution)/shard_map/ppermute | solution.py:24
  23.1 5.9 %copy-start.3 = (bf16[1,8,16,3072]{3,2,1,0:T(8,128)(2,1)S(1)}, bf16[1,8,16,3072]{3,2,1,0:T(8,128)(2,1)}, u32[]{:S(2)}) copy-start(bf16[1,8,16,3072]{3,2,1,0:T(8,128)(2,1)} %param.7) | copy-start | bytes 2359300
  23.2 12.4 %collective-permute-start.11 = (bf16[2,256,384]{2,1,0:T(8,128)(2,1)S(1)}, bf16[2,256,384]{2,1,0:T(8,128)(2,1)S(1)}, u32[]{:S(2)}, u32[]{:S(2)}) collective-permute-start(bf16[2,256,384]{2,1,0:T(8,128)(2,1)S(1)} %shard_map.97), channel_id=1, source_target_pairs={{0,2},{1,3},{2,0},{3,1},{4,6},{5,7},{6,4},{7,5},{8,10},{9,11},{10,... | collective-permute-start | bytes 1179656 | tf_op jit(solution)/shard_map/ppermute | solution.py:24
  23.5 4.9 %copy-start.5 = (s32[4]{0:T(128)S(1)}, s32[4]{0:T(128)}, u32[]{:S(2)}) copy-start(s32[4]{0:T(128)} %timesteps_ref.1) | copy-start | bytes 52
  23.5 5.9 %copy-start.2 = (bf16[1,8,16,3072]{3,2,1,0:T(8,128)(2,1)S(1)}, bf16[1,8,16,3072]{3,2,1,0:T(8,128)(2,1)}, u32[]{:S(2)}) copy-start(bf16[1,8,16,3072]{3,2,1,0:T(8,128)(2,1)} %param.10) | copy-start | bytes 2359300
  23.6 11.9 %collective-permute-start.4 = (bf16[2,256,384]{2,1,0:T(8,128)(2,1)S(1)}, bf16[2,256,384]{2,1,0:T(8,128)(2,1)S(1)}, u32[]{:S(2)}, u32[]{:S(2)}) collective-permute-start(bf16[2,256,384]{2,1,0:T(8,128)(2,1)S(1)} %shard_map.91), channel_id=1, source_target_pairs={{0,4},{1,5},{2,6},{3,7},{4,0},{5,1},{6,2},{7,3},{8,12},{9,13},{10,... | collective-permute-start | bytes 1179656 | tf_op jit(solution)/shard_map/ppermute | solution.py:24
  27.2 2.2 %copy-start = (bf16[1,8,16,3072]{3,2,1,0:T(8,128)(2,1)S(1)}, bf16[1,8,16,3072]{3,2,1,0:T(8,128)(2,1)}, u32[]{:S(2)}) copy-start(bf16[1,8,16,3072]{3,2,1,0:T(8,128)(2,1)} %param.8) | copy-start | bytes 2359300
  27.2 2.2 %copy-start.1 = (bf16[1,8,16,3072]{3,2,1,0:T(8,128)(2,1)S(1)}, bf16[1,8,16,3072]{3,2,1,0:T(8,128)(2,1)}, u32[]{:S(2)}) copy-start(bf16[1,8,16,3072]{3,2,1,0:T(8,128)(2,1)} %param.9) | copy-start | bytes 2359300
  27.2 4.0 %collective-permute-start.5 = (bf16[3,128,384]{2,1,0:T(8,128)(2,1)S(1)}, bf16[3,128,384]{2,1,0:T(8,128)(2,1)S(1)}, u32[]{:S(2)}, u32[]{:S(2)}) collective-permute-start(bf16[3,128,384]{2,1,0:T(8,128)(2,1)S(1)} %get-tuple-element.29), channel_id=1, source_target_pairs={{0,1},{1,0},{2,3},{3,2},{4,5},{5,4},{6,7},{7,6},{8,9},{9,8},{10,11... | collective-permute-start | bytes 884744 | tf_op jit(solution)/shard_map/ppermute | solution.py:24
  27.2 2.2 %collective-permute-start.10 = (bf16[2,128,384]{2,1,0:T(8,128)(2,1)S(1)}, bf16[2,128,384]{2,1,0:T(8,128)(2,1)S(1)}, u32[]{:S(2)}, u32[]{:S(2)}) collective-permute-start(bf16[2,128,384]{2,1,0:T(8,128)(2,1)S(1)} %shard_map.95), channel_id=1, source_target_pairs={{0,1},{1,0},{2,3},{3,2},{4,5},{5,4},{6,7},{7,6},{8,9},{9,8},{10,11... | collective-permute-start | bytes 589832 | tf_op jit(solution)/shard_map/ppermute | solution.py:24
  28.4 2.8 %collective-permute-start.8 = (bf16[2,128,384]{2,1,0:T(8,128)(2,1)S(1)}, bf16[2,128,384]{2,1,0:T(8,128)(2,1)S(1)}, u32[]{:S(2)}, u32[]{:S(2)}) collective-permute-start(bf16[2,128,384]{2,1,0:T(8,128)(2,1)S(1)} %shard_map.93), channel_id=1, source_target_pairs={{0,1},{1,0},{2,3},{3,2},{4,5},{5,4},{6,7},{7,6},{8,9},{9,8},{10,11... | collective-permute-start | bytes 589832 | tf_op jit(solution)/shard_map/ppermute | solution.py:24
  37.1 6.2 %collective-permute-start.16 = (bf16[128,384]{1,0:T(8,128)(2,1)S(1)}, bf16[128,384]{1,0:T(8,128)(2,1)S(1)}, u32[]{:S(2)}, u32[]{:S(2)}) collective-permute-start(bf16[128,384]{1,0:T(8,128)(2,1)S(1)} %get-tuple-element.50), channel_id=1, source_target_pairs={{0,4},{1,3},{2,6},{3,1},{4,0},{5,7},{6,2},{7,5},{8,12},{9,11},{10,... | collective-permute-start | bytes 294920 | tf_op jit(solution)/shard_map/ppermute | solution.py:30
  38.7 3.1 %collective-permute-start.12 = (bf16[256,384]{1,0:T(8,128)(2,1)S(1)}, bf16[256,384]{1,0:T(8,128)(2,1)S(1)}, u32[]{:S(2)}, u32[]{:S(2)}) collective-permute-start(bf16[256,384]{1,0:T(8,128)(2,1)S(1)} %get-tuple-element.42), channel_id=1, source_target_pairs={{0,1},{1,0},{2,3},{3,2},{4,5},{5,4},{6,7},{7,6},{8,9},{9,8},{10,11... | collective-permute-start | bytes 589832 | tf_op jit(solution)/shard_map/ppermute | solution.py:24
  39.5 4.3 %collective-permute-start.17 = (bf16[128,384]{1,0:T(8,128)(2,1)S(1)}, bf16[128,384]{1,0:T(8,128)(2,1)S(1)}, u32[]{:S(2)}, u32[]{:S(2)}) collective-permute-start(bf16[128,384]{1,0:T(8,128)(2,1)S(1)} %get-tuple-element.48), channel_id=1, source_target_pairs={{0,5},{1,2},{2,7},{3,0},{4,1},{5,6},{6,3},{7,4},{8,13},{9,10},{10,... | collective-permute-start | bytes 294920 | tf_op jit(solution)/shard_map/ppermute | solution.py:30
  39.6 5.6 %collective-permute-start.14 = (bf16[128,384]{1,0:T(8,128)(2,1)S(1)}, bf16[128,384]{1,0:T(8,128)(2,1)S(1)}, u32[]{:S(2)}, u32[]{:S(2)}) collective-permute-start(bf16[128,384]{1,0:T(8,128)(2,1)S(1)} %get-tuple-element.51), channel_id=1, source_target_pairs={{0,2},{1,5},{2,0},{3,7},{4,6},{5,1},{6,4},{7,3},{8,10},{9,13},{10,... | collective-permute-start | bytes 294920 | tf_op jit(solution)/shard_map/ppermute | solution.py:30
  41.9 4.0 %collective-permute-start.15 = (bf16[128,384]{1,0:T(8,128)(2,1)S(1)}, bf16[128,384]{1,0:T(8,128)(2,1)S(1)}, u32[]{:S(2)}, u32[]{:S(2)}) collective-permute-start(bf16[128,384]{1,0:T(8,128)(2,1)S(1)} %get-tuple-element.49), channel_id=1, source_target_pairs={{0,3},{1,4},{2,1},{3,6},{4,7},{5,0},{6,5},{7,2},{8,11},{9,12},{10,... | collective-permute-start | bytes 294920 | tf_op jit(solution)/shard_map/ppermute | solution.py:30
  42.0 7.4 %collective-permute-start.13 = (bf16[32,1536]{1,0:T(8,128)(2,1)S(1)}, bf16[32,1536]{1,0:T(8,128)(2,1)S(1)}, u32[]{:S(2)}, u32[]{:S(2)}) collective-permute-start(bf16[32,1536]{1,0:T(8,128)(2,1)S(1)} %shard_map.99), channel_id=1, source_target_pairs={{8,0},{16,8},{24,16},{9,1},{17,9},{25,17},{10,2},{18,10},{26,18},{... | collective-permute-start | bytes 294920 | tf_op jit(solution)/shard_map/ppermute | solution.py:20
  43.9 7.0 %collective-permute-start.19 = (bf16[32,768]{1,0:T(8,128)(2,1)S(1)}, bf16[32,768]{1,0:T(8,128)(2,1)S(1)}, u32[]{:S(2)}, u32[]{:S(2)}) collective-permute-start(bf16[32,768]{1,0:T(8,128)(2,1)S(1)} %shard_map.102), channel_id=1, source_target_pairs={{8,0},{16,8},{24,16},{9,1},{17,9},{25,17},{10,2},{18,10},{26,18},{... | collective-permute-start | bytes 147464 | tf_op jit(solution)/shard_map/ppermute | solution.py:20
  46.0 6.5 %collective-permute-start.18 = (bf16[32,768]{1,0:T(8,128)(2,1)S(1)}, bf16[32,768]{1,0:T(8,128)(2,1)S(1)}, u32[]{:S(2)}, u32[]{:S(2)}) collective-permute-start(bf16[32,768]{1,0:T(8,128)(2,1)S(1)} %shard_map.101), channel_id=1, source_target_pairs={{8,0},{16,8},{24,16},{9,1},{17,9},{25,17},{10,2},{18,10},{26,18},{... | collective-permute-start | bytes 147464 | tf_op jit(solution)/shard_map/ppermute | solution.py:20
  49.4 3.0 %copy-start.4 = (bf16[2,16,3072]{2,1,0:T(8,128)(2,1)S(1)}, bf16[2,16,3072]{2,1,0:T(8,128)(2,1)}, u32[]{:S(2)}) copy-start(bf16[2,16,3072]{2,1,0:T(8,128)(2,1)} %fresh_ref.1) | copy-start | bytes 589828
